TPU v7x, 128 devices: a whole 4x4x4 slice. The times are simulated.
128 devices in a mesh: seq: 16 (over y, x_lo, core), tp: 8 (over z, x_hi).
Axes of the slice: x: 4 (x_hi: 2, x_lo: 2; x = x_hi * 2 + x_lo), y: 4, z: 4, core: 2. Of those that a mesh axis runs over, the one named last changes fastest.
Arguments:
- tokens: bfloat16 [16384, 4096], P('seq', 'tp'), may hold values from -8 to 8
- norm_gain: float32 [4096], replicated, may hold values from 0.1 to 1.9
- w_query: bfloat16 [4096, 4096], P(None, 'tp'), may hold values from -1 to 1
- w_key: bfloat16 [4096, 4096], P(None, 'tp'), may hold values from -1 to 1
- w_value: bfloat16 [4096, 4096], P(None, 'tp'), may hold values from -0.09375 to 0.09375
- w_out: bfloat16 [4096, 4096], P('tp'), may hold values from -0.09375 to 0.09375
- offsets: int32 [5, 32], P(None, 'tp'), may hold values from 0 to 15, as said below
Outputs:
- mixed: bfloat16 [16384, 4096], P('seq', 'tp')
Inputs may be any that keep to these rules, and one draw needn't show every extreme that they name: offsets[b, h] lies in 0 to 2**b - 1, and in each branch b every value of that range is taken by some head.
All inputs are finite; a program needn't handle non-finite values.
Results may differ from a plain program's by a relative error of at most 0.0095.
Values may be sent and summed in bfloat16 or wider, within the bound.
No kernel may reach another device: no remote copies, remote signals or barrier semaphores. Data moves between devices by JAX's collectives and lax.ppermute only.
A program may use at most 192 MiB of HBM per device.

v0:
```python
import jax
import jax.numpy as jnp
from jax import lax
from jax.sharding import PartitionSpec as P


def partner_2(value, axis, apart):
    mask = 2**apart
    pairs = [(source, source ^ mask) for source in range(lax.axis_size(axis))]
    return lax.ppermute(value, axis, pairs)


def collect(block, group_span, device_index):
    for bit_pos in range(group_span.bit_length() - 1):
        partner = partner_2(block, "seq", bit_pos)
        lowered = device_index // 2**bit_pos % 2 == 0
        block = jnp.where(
            lowered, jnp.concatenate([block, partner], 0), jnp.concatenate([partner, block], 0)
        )
    return block


def on_device(tokens, norm_gain, w_query, w_key, w_value, w_out, offsets):
    gathered = lax.all_gather(tokens, "tp", axis=1, tiled=True)
    tokens_f = gathered.astype(jnp.float32)
    scaled = lax.rsqrt(jnp.mean(tokens_f * tokens_f, -1, keepdims=True) + 1e-05)
    normed = (tokens_f * scaled * norm_gain).astype(jnp.bfloat16)
    tok_rows = tokens.shape[0]
    head_count = offsets.shape[1]
    head_size = w_query.shape[1] // head_count
    levels = offsets.shape[0]
    scale = head_size ** (-0.5)

    def project(weight):
        result = jnp.dot(normed, weight, preferred_element_type=jnp.float32).astype(jnp.bfloat16)
        return result.reshape(tok_rows, head_count, head_size)

    queries = project(w_query)
    key_values = jnp.stack([project(w_key), project(w_value)], 1)
    device_index = lax.axis_index("seq")
    groups = lax.axis_size("seq")
    segment = tok_rows * groups // 16
    picked_q = []
    picked_kv = []
    onehots = []
    spans = []
    for level_id in range(levels):
        dilation = 2**level_id
        picked = tok_rows // dilation
        onehot = jnp.arange(dilation)[:, None] == offsets[level_id][None, :]
        shaped_q = queries.reshape(picked, dilation, head_count, head_size)
        picked_q.append(
            jnp.sum(jnp.where(onehot[None, :, :, None], shaped_q, jnp.zeros((), jnp.bfloat16)), 1)
        )
        shaped_kv = key_values.reshape(picked, dilation, 2, head_count, head_size)
        picked_kv.append(
            jnp.sum(
                jnp.where(onehot[None, :, None, :, None], shaped_kv, jnp.zeros((), jnp.bfloat16)), 1
            )
        )
        onehots.append(onehot)
        spans.append(max(1, segment * dilation // tok_rows))
    visible = [
        collect(picked_kv[level_id], spans[level_id], device_index) for level_id in range(levels)
    ]
    maxima = []
    totals = []
    sums = []
    for level_id in range(levels):
        dilation = 2**level_id
        picked = tok_rows // dilation
        group_span = spans[level_id]
        key_block = visible[level_id]
        query_start = device_index * picked
        key_start = device_index // group_span * group_span * picked
        query_pos = query_start + jnp.arange(picked)
        key_pos = key_start + jnp.arange(key_block.shape[0])
        allowed = (query_pos[:, None] // segment == key_pos[None, :] // segment) & (
            key_pos[None, :] <= query_pos[:, None]
        )
        scores = (
            jnp.einsum(
                "qhd,khd->hqk",
                picked_q[level_id],
                key_block[:, 0],
                preferred_element_type=jnp.float32,
            )
            * scale
        )
        scores = jnp.where(allowed[None], scores, -jnp.inf)
        row_max = jnp.max(scores, -1)
        probs = jnp.exp(scores - row_max[..., None])
        total = jnp.sum(probs, -1)
        weighted = jnp.einsum(
            "hqk,khd->qhd",
            probs.astype(jnp.bfloat16),
            key_block[:, 1],
            preferred_element_type=jnp.float32,
        )
        onehot = onehots[level_id]
        maxima.append(
            jnp.where(onehot[None], row_max.T[:, None, :], -jnp.inf).reshape(tok_rows, head_count)
        )
        totals.append(
            jnp.where(onehot[None], total.T[:, None, :], 0.0).reshape(tok_rows, head_count)
        )
        sums.append(
            jnp.where(onehot[None, :, :, None], weighted[:, None], 0.0).reshape(
                tok_rows, head_count, head_size
            )
        )
    largest = maxima[0]
    for level_id in range(1, levels):
        largest = jnp.maximum(largest, maxima[level_id])
    denominator = jnp.zeros((tok_rows, head_count), jnp.float32)
    numerator = jnp.zeros((tok_rows, head_count, head_size), jnp.float32)
    for level_id in range(levels):
        factor = jnp.exp(maxima[level_id] - largest)
        denominator = denominator + factor * totals[level_id]
        numerator = numerator + factor[..., None] * sums[level_id]
    attended = (
        (numerator / denominator[..., None])
        .astype(jnp.bfloat16)
        .reshape(tok_rows, head_count * head_size)
    )
    term = jnp.dot(attended, w_out, preferred_element_type=jnp.float32)
    summed = lax.psum_scatter(
        term.astype(jnp.bfloat16), "tp", scatter_dimension=1, tiled=True
    ).astype(jnp.float32)
    return (tokens.astype(jnp.float32) + summed).astype(jnp.bfloat16)


def solution(mesh):
    placed = (
        P("seq", "tp"),
        P(),
        P(None, "tp"),
        P(None, "tp"),
        P(None, "tp"),
        P("tp", None),
        P(None, "tp"),
    )
    return jax.shard_map(
        on_device, mesh=mesh, in_specs=placed, out_specs=P("seq", "tp"), check_vma=False
    )
```

profile of v0, /device:TPU:0, one launch (start us, length us, event | category | flops | bytes accessed | tf_op | source)
XLA Modules:
  0.0 463.3 jit_solution(11825922179415450968)
XLA Ops:
  17.7 1.9 compare_and_fusion
  19.6 105.8 %all-gather.2.cloned.1.call-done = bf16[1024,4096]{1,0:T(8,128)(2,1)} async-done(((bf16[1024,512]{1,0:T(8,128)(2,1)}), bf16[1024,4096]{1,0:T(8,128)(2,1)}) %all-gather.2.cloned.1.call-update) | async-done | bytes 8388624 | tf_op jit(solution)/shard_map/all_gather | solution.py:24
  125.5 5.2 %fusion = f32[1024]{0:T(1024)S(1)} fusion(bf16[1024,4096]{1,0:T(8,128)(2,1)} %all-gather.2.cloned.1.call-done), kind=kLoop, calls=%fused_computation.2 | loop fusion | flops 12581888 | bytes 8392704 | tf_op jit(solution)/shard_map/reduce_sum | solution.py:26
  131.3 6.8 %convolution_convert_fusion.1 = bf16[1024,512]{0,1:T(8,128)(2,1)S(1)} fusion(bf16[4096,512]{1,0:T(8,128)(2,1)} %param.11, bf16[1024,4096]{1,0:T(8,128)(2,1)S(1)} %copy-done.1, f32[4096]{0:T(1024)S(1)} %copy-done.55, f32[1024]{0:T(1024)S(1)} %add_rsqrt_fusion), kind=kOutput, calls=%fused_computation.66 | convolution fusion | flops 4312268800 | bytes 13651968 | tf_op jit(solution)/shard_map/dot_general | solution.py:35
  142.2 9.2 %convolution_convert_fusion.3 = bf16[1024,512]{0,1:T(8,128)(2,1)S(1)} fusion(bf16[4096,512]{1,0:T(8,128)(2,1)} %param.9, bf16[1024,4096]{1,0:T(8,128)(2,1)} %all-gather.2.cloned.1.call-done, f32[4096]{0:T(1024)S(1)} %copy-done.56, f32[1024]{0:T(1024)S(1)} %add_rsqrt_fusion), kind=kOutput, calls=%fused_computation.68 | convolution fusion | flops 4312268800 | bytes 13651968 | tf_op jit(solution)/shard_map/dot_general | solution.py:35
  154.2 10.2 %convolution_convert_fusion.2 = bf16[1024,512]{0,1:T(8,128)(2,1)} fusion(bf16[4096,512]{1,0:T(8,128)(2,1)} %param.10, bf16[1024,4096]{1,0:T(8,128)(2,1)} %all-gather.2.cloned.1.call-done, f32[4096]{0:T(1024)} %param.8, f32[1024]{0:T(1024)S(1)} %add_rsqrt_fusion), kind=kOutput, calls=%fused_computation.67 | convolution fusion | flops 4312268800 | bytes 13651968 | tf_op jit(solution)/shard_map/dot_general | solution.py:35
  169.6 1.7 fusion.30
  172.0 1.7 copy.59
  173.7 2.3 copy.57
  176.0 3.1 fusion.31
  180.3 2.2 fusion.29
  183.5 2.7 fusion.28
  187.3 1.6 copy.58
  190.4 2.9 fusion.3
  193.4 5.5 %fusion.4 = f32[4,1024]{1,0:T(4,128)} fusion(f32[4,1024,1024]{1,2,0:T(8,128)S(1)} %get-tuple-element.24, f32[4,1024]{1,0:T(4,128)S(1)} %get-tuple-element.23, pred[1024,1024]{0,1:T(8,128)(4,1)S(1)} %copy-done.4), kind=kLoop, calls=%fused_computation.8 | loop fusion | flops 16773120 | bytes 17858560 | tf_op jit(solution)/shard_map/reduce_sum | solution.py:93
  202.8 1.7 select_reduce_fusion.2
  204.5 2.1 maximum_select_fusion.12
  208.1 3.2 collective-permute-done.7
  217.0 1.8 maximum_select_fusion.9
  219.3 3.3 collective-permute-done.4
  222.6 1.8 maximum_select_fusion.10
  226.0 1.9 maximum_select_fusion.11
  228.0 2.8 collective-permute-start.9
  230.8 2.9 maximum_select_fusion.2
  233.7 1.8 fusion.9
  235.5 3.2 copy-done.2
  238.7 3.6 fusion.41
  242.3 2.6 copy.98
  245.7 4.9 %fusion.10 = f32[4,512]{1,0:T(4,128)S(1)} fusion(f32[4,512,1024]{2,1,0:T(8,128)} %copy-done.2, f32[4,512]{1,0:T(4,128)S(1)} %get-tuple-element.21, pred[512,1024]{1,0:T(8,128)(4,1)} %compare_and_fusion.1), kind=kLoop, calls=%fused_computation.16 | loop fusion | flops 8386560 | bytes 8929280 | tf_op jit(solution)/shard_map/reduce_sum | solution.py:93
  251.5 1.9 broadcast_in_dim.590
  254.6 1.9 broadcast_in_dim.537
  256.5 1.8 copy.69
  258.4 2.1 maximum_select_fusion.4
  261.5 1.9 copy-done.8
  266.8 3.4 fusion.16
  270.7 2.1 maximum_select_fusion.6
  276.8 2.2 fusion.37
  279.3 2.2 maximum_select_fusion.8
  284.3 12.4 %bitcast_multiply_fusion.1 = f32[1024,4,128]{0,2,1:T(8,128)} fusion(f32[4,1024,1024]{1,2,0:T(8,128)} %copy-done, f32[4,1024]{1,0:T(4,128)S(1)} %copy-done.36, pred[1024,1024]{0,1:T(8,128)(4,1)S(1)} %copy-done.5, bf16[1024,2,4,128]{3,0,2,1:T(8,128)(2,1)} %copy-done.19, f32[1024,4]{0,1:T(4,128)S(1)} %get-tuple-element.14, pred[4]{0:T(512)(128)(4,1)S(1)} %copy-done.49), kind=kOutput, calls=%fused_computation.54 | convolution fusion | flops 1091567616 | bytes 21004292 | tf_op jit(solution)/shard_map/hqk,khd->qhd/dot_general | solution.py:94
  296.6 2.9 copy.99
  301.6 4.0 broadcast_in_dim.572
  305.6 4.0 broadcast_in_dim.585
  309.6 4.0 broadcast_in_dim.581
  313.6 4.0 broadcast_in_dim.577
  326.0 2.2 div.199
  328.2 14.2 %convolution_convert_fusion = bf16[1024,4096]{1,0:T(8,128)(2,1)} fusion(bf16[512,4096]{1,0:T(8,128)(2,1)} %param.12, f32[128,8,4,128]{3,2,1,0:T(4,128)} %bitcast.206, f32[128,8,4,128]{3,2,1,0:T(4,128)} %bitcast.208, f32[128,8,4,128]{3,2,1,0:T(4,128)S(1)} %bitcast.202, f32[128,8,4,128]{3,2,1,0:T(4,128)S(1)} %bitcast.203, ...), kind=kOutput, calls=%fused_computation.14 | convolution fusion | flops 4306501632 | bytes 33816576 | tf_op jit(solution)/shard_map/dot_general | solution.py:126
  342.5 111.2 %reduce-scatter.2.cloned.1.call-done = bf16[1024,512]{1,0:T(8,128)(2,1)} async-done(((bf16[1024,4096]{1,0:T(8,128)(2,1)}), bf16[1024,512]{1,0:T(8,128)(2,1)}) %reduce-scatter.2.cloned.1.call-update) | async-done | bytes 1048592 | tf_op jit(solution)/shard_map/reduce_scatter | solution.py:127
  453.7 2.5 add_convert_fusion
  (228 shorter events, 66.8 us)
Async XLA Ops:
  6.5 7.8 %copy-start.38 = (s32[5,4]{0,1:T(4,128)S(1)}, s32[5,4]{0,1:T(4,128)}, u32[]{:S(2)}) copy-start(s32[5,4]{0,1:T(4,128)} %param.13) | copy-start | bytes 244
  6.5 119.0 %all-gather.2.cloned.1.call-start = ((), (), s32[]{:S(2)}) async-start(), calls=%async_computation.1 | async-start | bytes 9437184 | tf_op jit(solution)/shard_map/all_gather | solution.py:24
  7.3 446.5 %reduce-scatter.2.cloned.1.call-start = ((), (), s32[]{:S(2)}) async-start(), calls=%async_computation.2 | async-start | bytes 9437184 | tf_op jit(solution)/shard_map/reduce_scatter | solution.py:127
  13.3 117.4 %copy-start.39 = (pred[1024,4]{0,1:T(4,128)(4,1)}, pred[1024,4]{0,1:T(4,128)(4,1)S(1)}, u32[]{:S(2)}) copy-start(pred[1024,4]{0,1:T(4,128)(4,1)S(1)} %broadcast_in_dim.530) | copy-start | bytes 12292
  14.4 175.3 %copy-start.48 = (pred[4]{0:T(512)(128)(4,1)}, pred[4]{0:T(512)(128)(4,1)S(1)}, u32[]{:S(2)}) copy-start(pred[4]{0:T(512)(128)(4,1)S(1)} %fusion.98) | copy-start | bytes 16
  17.7 113.0 %copy-start.55 = (f32[4096]{0:T(1024)S(1)}, f32[4096]{0:T(1024)}, u32[]{:S(2)}) copy-start(f32[4096]{0:T(1024)} %param.8) | copy-start | bytes 49156
  125.5 5.8 %copy-start.1 = (bf16[1024,4096]{1,0:T(8,128)(2,1)S(1)}, bf16[1024,4096]{1,0:T(8,128)(2,1)}, u32[]{:S(2)}) copy-start(bf16[1024,4096]{1,0:T(8,128)(2,1)} %all-gather.2.cloned.1.call-done) | copy-start | bytes 25165828
  172.0 32.5 %collective-permute-start.3 = (bf16[128,2,4,128]{3,0,2,1:T(8,128)(2,1)}, bf16[128,2,4,128]{3,0,2,1:T(8,128)(2,1)}, u32[]{:S(2)}, u32[]{:S(2)}) collective-permute-start(bf16[128,2,4,128]{3,0,2,1:T(8,128)(2,1)} %copy.82), channel_id=1, source_target_pairs={{0,8},{8,0},{16,24},{24,16},{32,40},{40,32},{48,56},{56,48},{64,72... | collective-permute-start | bytes 786440 | tf_op jit(solution)/shard_map/ppermute | solution.py:10
  172.0 4.0 copy-start.7
  176.0 4.3 copy-start.12
  176.0 4.3 copy-start.15
  176.0 4.3 copy-start.53
  179.1 4.3 copy-start.11
  179.1 4.3 copy-start.13
  179.1 4.3 copy-start.51
  179.8 21.1 %collective-permute-start.6 = (bf16[64,2,4,128]{3,0,2,1:T(8,128)(2,1)}, bf16[64,2,4,128]{3,0,2,1:T(8,128)(2,1)}, u32[]{:S(2)}, u32[]{:S(2)}) collective-permute-start(bf16[64,2,4,128]{3,0,2,1:T(8,128)(2,1)} %copy.90), channel_id=1, source_target_pairs={{0,8},{8,0},{16,24},{24,16},{32,40},{40,32},{48,56},{56,48},{64,72... | collective-permute-start | bytes 393224 | tf_op jit(solution)/shard_map/ppermute | solution.py:10
  187.2 29.8 %collective-permute-start.1 = (bf16[256,2,4,128]{3,0,2,1:T(8,128)(2,1)}, bf16[256,2,4,128]{3,0,2,1:T(8,128)(2,1)}, u32[]{:S(2)}, u32[]{:S(2)}) collective-permute-start(bf16[256,2,4,128]{3,0,2,1:T(8,128)(2,1)} %copy.75), channel_id=1, source_target_pairs={{0,8},{8,0},{16,24},{24,16},{32,40},{40,32},{48,56},{56,48},{64,72... | collective-permute-start | bytes 1572872 | tf_op jit(solution)/shard_map/ppermute | solution.py:10
  188.9 41.8 %collective-permute-start = (bf16[512,2,4,128]{3,0,2,1:T(8,128)(2,1)}, bf16[512,2,4,128]{3,0,2,1:T(8,128)(2,1)}, u32[]{:S(2)}, u32[]{:S(2)}) collective-permute-start(bf16[512,2,4,128]{3,0,2,1:T(8,128)(2,1)} %copy.65), channel_id=1, source_target_pairs={{0,8},{8,0},{16,24},{24,16},{32,40},{40,32},{48,56},{56,48},{64,72... | collective-permute-start | bytes 3145736 | tf_op jit(solution)/shard_map/ppermute | solution.py:10
  190.4 3.0 copy-start.19
  193.4 5.9 %copy-start = (f32[4,1024,1024]{1,2,0:T(8,128)}, f32[4,1024,1024]{1,2,0:T(8,128)S(1)}, u32[]{:S(2)}) copy-start(f32[4,1024,1024]{1,2,0:T(8,128)S(1)} %get-tuple-element.24) | copy-start | bytes 50331652
  193.4 5.9 %copy-start.35 = (f32[4,1024]{1,0:T(4,128)}, f32[4,1024]{1,0:T(4,128)S(1)}, u32[]{:S(2)}) copy-start(f32[4,1024]{1,0:T(4,128)S(1)} %get-tuple-element.23) | copy-start | bytes 49156
  193.4 5.9 %copy-start.10 = (bf16[256,4,4,128]{3,2,1,0:T(4,128)(2,1)S(1)}, bf16[256,4,4,128]{3,2,1,0:T(4,128)(2,1)}, u32[]{:S(2)}) copy-start(bf16[256,4,4,128]{3,2,1,0:T(4,128)(2,1)} %reshape_reshape.17) | copy-start | bytes 3145732
  193.4 5.9 %copy-start.54 = (pred[4,4]{1,0:T(4,128)(4,1)S(1)}, pred[4,4]{1,0:T(4,128)(4,1)}, u32[]{:S(2)}) copy-start(pred[4,4]{1,0:T(4,128)(4,1)} %copy-done.52) | copy-start | bytes 52
  199.3 3.4 copy-start.9
  202.1 9.2 %collective-permute-start.7 = (bf16[128,2,4,128]{3,0,2,1:T(8,128)(2,1)S(1)}, bf16[128,2,4,128]{3,0,2,1:T(8,128)(2,1)S(1)}, u32[]{:S(2)}, u32[]{:S(2)}) collective-permute-start(bf16[128,2,4,128]{3,0,2,1:T(8,128)(2,1)S(1)} %maximum_select_fusion.14), channel_id=1, source_target_pairs={{0,16},{8,24},{16,0},{24,8},{32,48},{40,56},{48,32},{56,40},{64,80... | collective-permute-start | bytes 786440 | tf_op jit(solution)/shard_map/ppermute | solution.py:10
  206.7 16.0 %collective-permute-start.4 = (bf16[256,2,4,128]{3,0,2,1:T(8,128)(2,1)}, bf16[256,2,4,128]{3,0,2,1:T(8,128)(2,1)}, u32[]{:S(2)}, u32[]{:S(2)}) collective-permute-start(bf16[256,2,4,128]{3,0,2,1:T(8,128)(2,1)} %maximum_select_fusion.12), channel_id=1, source_target_pairs={{0,16},{8,24},{16,0},{24,8},{32,48},{40,56},{48,32},{56,40},{64,80... | collective-permute-start | bytes 1572872 | tf_op jit(solution)/shard_map/ppermute | solution.py:10
  212.2 13.8 %collective-permute-start.8 = (bf16[256,2,4,128]{3,0,2,1:T(8,128)(2,1)}, bf16[256,2,4,128]{3,0,2,1:T(8,128)(2,1)}, u32[]{:S(2)}, u32[]{:S(2)}) collective-permute-start(bf16[256,2,4,128]{3,0,2,1:T(8,128)(2,1)} %maximum_select_fusion.13), channel_id=1, source_target_pairs={{0,32},{8,40},{16,48},{24,56},{32,0},{40,8},{48,16},{56,24},{64,96... | collective-permute-start | bytes 1572872 | tf_op jit(solution)/shard_map/ppermute | solution.py:10
  218.8 39.6 %collective-permute-start.2 = (bf16[512,2,4,128]{3,0,2,1:T(8,128)(2,1)S(1)}, bf16[512,2,4,128]{3,0,2,1:T(8,128)(2,1)}, u32[]{:S(2)}, u32[]{:S(2)}) collective-permute-start(bf16[512,2,4,128]{3,0,2,1:T(8,128)(2,1)S(1)} %maximum_select_fusion.9), channel_id=1, source_target_pairs={{0,16},{8,24},{16,0},{24,8},{32,48},{40,56},{48,32},{56,40},{64,80... | collective-permute-start | bytes 3145736 | tf_op jit(solution)/shard_map/ppermute | solution.py:10
  224.5 46.2 %collective-permute-start.5 = (bf16[512,2,4,128]{3,0,2,1:T(8,128)(2,1)S(1)}, bf16[512,2,4,128]{3,0,2,1:T(8,128)(2,1)}, u32[]{:S(2)}, u32[]{:S(2)}) collective-permute-start(bf16[512,2,4,128]{3,0,2,1:T(8,128)(2,1)S(1)} %maximum_select_fusion.10), channel_id=1, source_target_pairs={{0,32},{8,40},{16,48},{24,56},{32,0},{40,8},{48,16},{56,24},{64,96... | collective-permute-start | bytes 3145736 | tf_op jit(solution)/shard_map/ppermute | solution.py:10
  227.9 5.7 %copy-start.17 = (pred[512,1024]{1,0:T(8,128)(4,1)S(1)}, pred[512,1024]{1,0:T(8,128)(4,1)}, u32[]{:S(2)}) copy-start(pred[512,1024]{1,0:T(8,128)(4,1)} %compare_and_fusion.1) | copy-start | bytes 1572868
  227.9 5.7 %copy-start.27 = (bf16[512,4,128]{2,1,0:T(4,128)(2,1)S(1)}, bf16[512,4,128]{2,1,0:T(4,128)(2,1)}, u32[]{:S(2)}) copy-start(bf16[512,4,128]{2,1,0:T(4,128)(2,1)} %select_reduce_fusion.2) | copy-start | bytes 1572868
  228.0 51.3 %collective-permute-start.9 = (bf16[512,2,4,128]{3,0,2,1:T(8,128)(2,1)S(1)}, bf16[512,2,4,128]{3,0,2,1:T(8,128)(2,1)}, u32[]{:S(2)}, u32[]{:S(2)}) collective-permute-start(bf16[512,2,4,128]{3,0,2,1:T(8,128)(2,1)S(1)} %maximum_select_fusion.11), channel_id=1, source_target_pairs={{0,64},{8,72},{16,80},{24,88},{32,96},{40,104},{48,112},{56,120},{... | collective-permute-start | bytes 3145736 | tf_op jit(solution)/shard_map/ppermute | solution.py:10
  235.5 3.2 copy-start.2
  258.4 2.2 copy-start.28
  270.7 2.2 copy-start.25
  270.7 2.2 copy-start.32
  279.3 2.2 copy-start.29
  279.3 2.2 copy-start.30
  282.1 2.0 copy-start.33
  282.1 2.0 copy-start.34
  282.1 2.0 copy-start.36
  282.2 2.1 copy-start.5
  299.6 6.0 %copy-start.23 = (pred[1024,4]{1,0:T(8,128)(4,1)S(1)}, pred[1024,4]{1,0:T(8,128)(4,1)}, u32[]{:S(2)}) copy-start(pred[1024,4]{1,0:T(8,128)(4,1)} %copy.109) | copy-start | bytes 12292
  299.6 10.0 %copy-start.22 = (pred[1024,4]{1,0:T(8,128)(4,1)S(1)}, pred[1024,4]{1,0:T(8,128)(4,1)}, u32[]{:S(2)}) copy-start(pred[1024,4]{1,0:T(8,128)(4,1)} %copy.105) | copy-start | bytes 12292
  300.8 16.7 %copy-start.26 = (f32[64,4,128]{2,1,0:T(4,128)S(1)}, f32[64,4,128]{2,1,0:T(4,128)}, u32[]{:S(2)}) copy-start(f32[64,4,128]{2,1,0:T(4,128)} %copy.110) | copy-start | bytes 393220
  322.3 2.5 copy-start.18
  324.8 3.5 copy-start.31
  342.5 111.3 %copy-start.3 = (bf16[1024,512]{1,0:T(8,128)(2,1)S(1)}, bf16[1024,512]{1,0:T(8,128)(2,1)}, u32[]{:S(2)}) copy-start(bf16[1024,512]{1,0:T(8,128)(2,1)} %param.7) | copy-start | bytes 3145732
  (21 other events, 34.1 us)
Sparse Core Ops, SparseCore 0:
  9.5 115.9 all-gather.1
  342.6 111.0 reduce-scatter.1
where the time goes:
time: 472 us; the launch traced here: 463 us
  waiting for transfers between devices  224 us (47%)
  local copies, waits for them, and re-layouts  83.7 us (18%)
  matrix products  65.9 us (14%)
  other arithmetic  65 us (14%)
  between operations  14.8 us (3%)
  starting transfers between devices  9.62 us (2%)
    reduce_scatter x1, waiting for transfers between devices, on_device(): lax.psum_scatter(term.astype(jnp.bfloat16), 'tp', scatter_dimension=1, ti...  111 us
    all_gather x1, waiting for transfers between devices, on_device(): gathered = lax.all_gather(tokens, 'tp', axis=1, tiled=True)  106 us
    dot_general x3, matrix products, project(): jnp.dot(normed, weight, preferred_element_type=jnp.float32)  26.3 us
    select_n x10, other arithmetic, collect(): jnp.where(lowered, jnp.concatenate([block, partner], 0), jnp.concatenate(...  19.1 us
    dot_general x5, matrix products, on_device(): jnp.einsum('hqk,khd->qhd', probs.astype(jnp.bfloat16), key_block[:, 1], p...  18.5 us
    reduce_sum x5, other arithmetic, on_device(): total = jnp.sum(probs, -1)  16.3 us
    broadcast_in_dim x4, local copies, waits for them, and re-layouts, on_device(): jnp.where(onehot[None, :, :, None], shaped_q, jnp.zeros((), jnp.bfloat16))  16 us
    dot_general x1, matrix products, on_device(): term = jnp.dot(attended, w_out, preferred_element_type=jnp.float32)  14.2 us
  transfers between devices with their start and end apart: 12, of which 4 were waited for; matrix products, arithmetic and copies ran while one was open for 20% of the time, Pallas kernels for 0%

commit v1 on v0

v1 whole, which is shorter than its diff:
```python
import functools
import math

import jax
import jax.numpy as jnp
from jax import lax
from jax.experimental import pallas as pl
from jax.experimental.pallas import tpu as pltpu
from jax.sharding import PartitionSpec as P

BF16 = jnp.bfloat16
F32 = jnp.float32
LOG2E = math.log2(math.e)
LOW = -1e30
FAR = 1 << 20
VMEM_LIMIT = 56 * 1024 * 1024
SMALL = pl.CostEstimate(flops=1024, bytes_accessed=1024, transcendentals=0)


def z_shift(value, step):
    pairs = [(t, ((t // 2 + step) % 4) * 2 + t % 2) for t in range(8)]
    return lax.ppermute(value, "tp", pairs)


def x_swap(value):
    return lax.ppermute(value, "tp", [(t, t ^ 1) for t in range(8)])


def seq_swap(value, mask):
    return lax.ppermute(value, "seq", [(s, s ^ mask) for s in range(16)])


def gather_x_first(block, *others):
    pair = jnp.stack([block, after(x_swap(block), *others)])
    below = z_shift(pair, 1)
    above = z_shift(pair, -1)
    far_own = z_shift(below[0], 1)
    far_other = z_shift(above[1], -1)
    return [
        (pair, 0, 0, 0),
        (pair, 1, 0, 1),
        (below, 0, -1, 0),
        (below, 1, -1, 1),
        (above, 0, 1, 0),
        (above, 1, 1, 1),
        (far_own, None, 2, 0),
        (far_other, None, 2, 1),
    ]


def gather_z_first(block):
    below = z_shift(block, 1)
    above = z_shift(block, -1)
    other = x_swap(block)
    far = z_shift(below, 1)
    others = x_swap(jnp.stack([below, above, far]))
    return [
        (block, None, 0, 0),
        (below, None, -1, 0),
        (above, None, 1, 0),
        (far, None, 2, 0),
        (other, None, 0, 1),
        (others, 0, -1, 1),
        (others, 1, 1, 1),
        (others, 2, 2, 1),
    ]


def piece_owners(pieces):
    tp = lax.axis_index("tp")
    z, x = tp // 2, tp % 2
    owners = [((z + dz + 4) % 4) * 2 + (x ^ dx) for _, _, dz, dx in pieces]
    return jnp.stack(owners).astype(jnp.int32)


def split_pieces(pieces):
    arrays, where = [], []
    for array, index, _, _ in pieces:
        for number, seen in enumerate(arrays):
            if seen is array:
                break
        else:
            number = len(arrays)
            arrays.append(array)
        where.append((number, index))
    return arrays, where


def whole_spec(array):
    zeros = (0,) * array.ndim
    return pl.BlockSpec(array.shape, lambda *_: zeros)


def copy_pieces(groups, owner_ref, arrays, x_s, sems):
    copies = []
    number = 0
    for row, lane, where, first in groups:
        for array, index in where:
            source = arrays[array] if index is None else arrays[array].at[index]
            rows, depth = source.shape
            low = owner_ref[first + len(copies) - number] * (x_s.shape[1] // 8) + lane
            low = pl.multiple_of(low, depth)
            copies.append(
                pltpu.make_async_copy(
                    source, x_s.at[row : row + rows, pl.ds(low, depth)], sems.at[len(copies)]
                )
            )
            copies[-1].start()
        number = len(copies)
    return copies


def piece_groups(gathers):
    operands, groups, owners = [], [], []
    for row, lane, pieces in gathers:
        arrays, where = split_pieces(pieces)
        where = [(len(operands) + array, index) for array, index in where]
        groups.append((row, lane, where, 8 * len(owners)))
        operands += arrays
        owners.append(piece_owners(pieces))
    return operands, groups, jnp.concatenate(owners)


def pick_places(levels, tokens, first, rows):
    unit = tokens // 16
    places = []
    base = 0
    for level in range(1, levels):
        count = rows >> level
        at = base + (first >> level)
        lows = [
            at,
            at - 8 * unit if level == 2 else None,
            at - 12 * unit if level >= 3 else None,
            at - 14 * unit if level == 4 else None,
        ]
        places.append((count, lows))
        base += tokens >> level
    return places


def keys_kernel(groups, n_arrays, n_old, first, heads, levels, *refs):
    owner_ref, offset_ref = refs[:2]
    arrays = refs[2 : 2 + n_arrays]
    gain_ref, wk_ref, wv_ref = refs[2 + n_arrays : 5 + n_arrays]
    refs = refs[5 + n_arrays + n_old :]
    x_out, k_out, v_out = refs[:3]
    picks = refs[3:7]
    x_s, w_s, kv_s, split_s, pick_s, piece_sems, w_sems, x_sem, kv_sems, pick_sems = refs[7:]
    rows, depth = x_s.shape
    tokens = k_out.shape[0]

    copies = copy_pieces(groups, owner_ref, arrays, x_s, piece_sems)
    w_copies = []
    for i, w_ref in enumerate((wk_ref, wv_ref)):
        for k in range(4):
            part = slice(k * depth // 4, (k + 1) * depth // 4)
            w_copies.append(pltpu.make_async_copy(w_ref.at[part], w_s.at[i, part], w_sems.at[i, k]))
            w_copies[-1].start()
    for copy in copies:
        copy.wait()

    def normalise(i, carry):
        at = pl.ds(pl.multiple_of(i * 32, 32), 32)
        value = x_s[at, :].astype(F32)
        scaled = lax.rsqrt(jnp.mean(value * value, -1, keepdims=True) + 1e-05)
        x_s[at, :] = (value * scaled * gain_ref[...]).astype(BF16)
        return carry

    lax.fori_loop(0, rows // 32, normalise, 0, unroll=2)
    here = slice(first, first + rows)
    waits = [pltpu.make_async_copy(x_s, x_out.at[here], x_sem)]
    waits[0].start()

    for i, out in enumerate((k_out, v_out)):
        for copy in w_copies[4 * i : 4 * i + 4]:
            copy.wait()
        full = jnp.dot(x_s[...], w_s[i], preferred_element_type=F32)
        kv_s[i] = full.astype(BF16)
        waits.append(pltpu.make_async_copy(kv_s.at[i], out.at[here], kv_sems.at[i]))
        waits[-1].start()
        for head in range(heads):
            split_s[i * heads + head] = full[:, head * 128 : head * 128 + 128]

    local = 0
    for level, (count, lows) in enumerate(pick_places(levels, tokens, first, rows), 1):
        for head in range(heads):
            start = offset_ref[level, head]
            for side in range(2):
                lane = (side * heads + head) * 128
                pick_s[local : local + count, lane : lane + 128] = split_s[
                    side * heads + head, pl.ds(start, count, stride=2**level), :
                ].astype(BF16)
        for which, low in enumerate(lows):
            if low is not None:
                waits.append(
                    pltpu.make_async_copy(
                        pick_s.at[local : local + count],
                        picks[which].at[low : low + count],
                        pick_sems.at[level - 1, which],
                    )
                )
                waits[-1].start()
        local += count
    for copy in waits:
        copy.wait()


def keys(gathers, first, rows, tokens, old, norm_gain, w_key, w_value, offsets):
    operands, groups, owners = piece_groups(gathers)
    depth, width = w_key.shape
    levels, heads = offsets.shape
    unit = tokens // 16
    outs = [jax.ShapeDtypeStruct((tokens, depth), BF16)]
    outs += [jax.ShapeDtypeStruct((tokens, width), BF16)] * 2
    outs += [jax.ShapeDtypeStruct((n * unit, 2 * width), BF16) for n in (15, 4, 3, 1)]
    anywhere = pl.BlockSpec(memory_space=pl.ANY)
    scalars = pl.BlockSpec(memory_space=pltpu.SMEM)
    vector = pl.BlockSpec(memory_space=pltpu.VMEM)
    before = 5 + len(operands)
    return pl.pallas_call(
        functools.partial(keys_kernel, groups, len(operands), len(old), first, heads, levels),
        in_specs=[scalars, scalars]
        + [anywhere] * len(operands)
        + [vector]
        + [anywhere] * (2 + len(old)),
        out_specs=[anywhere for _ in outs],
        scratch_shapes=[
            pltpu.VMEM((rows, depth), BF16),
            pltpu.VMEM((2, depth, width), BF16),
            pltpu.VMEM((2, rows, width), BF16),
            pltpu.VMEM((2 * heads, rows, 128), F32),
            pltpu.VMEM((rows * 15 // 16, 2 * width), BF16),
            pltpu.SemaphoreType.DMA((8 * len(groups),)),
            pltpu.SemaphoreType.DMA((2, 4)),
            pltpu.SemaphoreType.DMA,
            pltpu.SemaphoreType.DMA((2,)),
            pltpu.SemaphoreType.DMA((levels - 1, 4)),
        ],
        out_shape=outs,
        input_output_aliases={before + i: i for i in range(len(old))},
        compiler_params=pltpu.CompilerParams(vmem_limit_bytes=VMEM_LIMIT),
        cost_estimate=SMALL,
        name="keys",
    )(owners, offsets, *operands, norm_gain[None], w_key, w_value, *old)


def queries_kernel(q_scale, x_ref, w_ref, out_ref):
    full = jnp.dot(x_ref[...], w_ref[...], preferred_element_type=F32)
    out_ref[...] = (full * q_scale).astype(BF16)


def queries(normed, w_query, heads):
    tokens, depth = normed.shape
    width = w_query.shape[1]
    tile = 256
    return pl.pallas_call(
        functools.partial(queries_kernel, LOG2E * (width // heads) ** (-0.5)),
        grid=(tokens // tile,),
        in_specs=[
            pl.BlockSpec((tile, depth), lambda i: (i, 0)),
            pl.BlockSpec((depth, width), lambda i: (0, 0)),
        ],
        out_specs=pl.BlockSpec((tile, width), lambda i: (i, 0)),
        out_shape=jax.ShapeDtypeStruct((tokens, width), BF16),
        compiler_params=pltpu.CompilerParams(vmem_limit_bytes=VMEM_LIMIT),
        cost_estimate=SMALL,
        name="queries",
    )(normed, w_query)


def exchange(own, second, p34, fourth, ready_1, ready_2):
    unit = fourth.shape[0]
    by_x = seq_swap(p34, 2)
    by_y = seq_swap(p34, 4)
    by_x2 = seq_swap(second, 2)
    by_y2 = seq_swap(fourth, 8)
    by_y3 = seq_swap(fourth, 12)
    core_own = seq_swap(own, 1)
    by_x = after(by_x, ready_1)
    by_yx = seq_swap(by_x, 4)
    x_fourth = by_x[2 * unit :]
    by_y2x = seq_swap(x_fourth, 8)
    by_y3x = seq_swap(x_fourth, 12)
    others = jnp.concatenate(
        [by_x, by_y, by_yx, by_x2, by_y2, by_y3, by_y2x, by_y3x]
    )
    others = after(others, ready_2)
    core_others = seq_swap(others, 1)
    return own, core_own, others, core_others


def level_blocks(level, unit):
    count = unit * (16 >> level)
    base = unit * (0, 0, 8, 12, 14)[level]
    blocks = [(0, base, count, 0), (1, base, count, 1)]
    other = []
    if level == 2:
        other.append((9, 2))
    if level >= 3:
        other += [((0, 2)[level - 3] + 3 * i, m) for i, m in enumerate((2, 4, 6))]
    if level == 4:
        other += [(13 + i, m) for i, m in enumerate((8, 12, 10, 14))]
    for low, mask in other:
        blocks += [(2, low * unit, count, mask), (3, low * unit, count, mask + 1)]
    return blocks


def key_table(unit, levels):
    position = lax.axis_index("seq")
    rows = []
    for level in range(1, levels):
        columns = []
        for _, _, count, mask in level_blocks(level, unit):
            if mask == 0:
                columns.append(jnp.arange(count, dtype=jnp.int32))
            else:
                top = 1 << (mask.bit_length() - 1)
                columns.append(jnp.full((count,), jnp.where((position & top) != 0, -1, FAR), jnp.int32))
        rows.append(jnp.concatenate(columns))
    return jnp.stack(rows)


TILE = 256
NT = (((1,), (1,)), ((), ()))


def local_kernel(q_ref, k_ref, v_ref, m_ref, l_ref, a_ref, v_s):
    tokens = q_ref.shape[0]
    v_s[:, :128] = v_ref[...]
    v_s[:, 128:] = jnp.ones((tokens, 128), BF16)
    lower = lax.broadcasted_iota(jnp.int32, (TILE, TILE), 0) >= lax.broadcasted_iota(
        jnp.int32, (TILE, TILE), 1
    )
    for number in range(tokens // TILE):
        low, high = number * TILE, number * TILE + TILE
        query = q_ref[low:high, :]
        own = lax.dot_general(query, k_ref[low:high, :], NT, preferred_element_type=F32)
        scores = jnp.where(lower, own, LOW)
        if number:
            before = lax.dot_general(query, k_ref[:low, :], NT, preferred_element_type=F32)
            scores = jnp.concatenate([before, scores], 1)
        top = jnp.max(scores, 1, keepdims=True)
        probs = jnp.exp2(scores - top).astype(BF16)
        both = jnp.dot(probs, v_s[:high, :], preferred_element_type=F32)
        m_ref[low:high, :] = jnp.broadcast_to(top, (TILE, 128))
        a_ref[low:high, :] = both[:, :128]
        l_ref[low:high, :] = both[:, 128:]


def attend_local(q, k, v):
    tokens, width = q.shape
    block = pl.BlockSpec((tokens, 128), lambda h: (0, h))
    return pl.pallas_call(
        local_kernel,
        grid=(width // 128,),
        in_specs=[block] * 3,
        out_specs=[block] * 3,
        scratch_shapes=[pltpu.VMEM((tokens, 256), BF16)],
        out_shape=[jax.ShapeDtypeStruct((tokens, width), F32)] * 3,
        compiler_params=pltpu.CompilerParams(vmem_limit_bytes=VMEM_LIMIT),
        cost_estimate=SMALL,
        name="attend_local",
    )(q, k, v)


def attend_kernel(levels, head_base, *refs):
    offset_ref, q_ref, m_ref, l_ref, a_ref = refs[:5]
    k_group, v_group = refs[5:9], refs[9:13]
    table_ref, out_ref, q_f, k_s, v_s, m_s, l_s, a_s = refs[13:]
    head = head_base + pl.program_id(0)
    tokens = q_f.shape[0]
    unit = k_group[0].shape[0] // 15
    q_f[...] = q_ref[...].astype(F32)
    m_s[...] = m_ref[...]
    l_s[...] = l_ref[...]
    a_s[...] = a_ref[...]
    v_s[:, 128:] = jnp.ones((tokens, 128), BF16)

    for level in range(1, levels):
        dilation = 2**level
        picked = tokens // dilation
        start = offset_ref[level, head]
        row = 0
        for source, low, count, _ in level_blocks(level, unit):
            k_s[row : row + count, :] = k_group[source][low : low + count, :]
            v_s[row : row + count, :128] = v_group[source][low : low + count, :]
            row += count
        order = table_ref[level - 1 : level, :]
        size = min(TILE, picked)
        for number in range(picked // size):
            rows = pl.ds(start + number * size * dilation, size, stride=dilation)
            query = q_f[rows, :].astype(BF16)
            scores = lax.dot_general(query, k_s[...], NT, preferred_element_type=F32)
            at = lax.broadcasted_iota(jnp.int32, (size, tokens), 0) + number * size
            scores = jnp.where(order <= at, scores, LOW)
            m_old = m_s[rows, :]
            top = jnp.maximum(m_old[:, :1], jnp.max(scores, 1, keepdims=True))
            probs = jnp.exp2(scores - top).astype(BF16)
            both = jnp.dot(probs, v_s[...], preferred_element_type=F32)
            factor = jnp.exp2(m_old - top)
            m_s[rows, :] = jnp.broadcast_to(top, (size, 128))
            a_s[rows, :] = factor * a_s[rows, :] + both[:, :128]
            l_s[rows, :] = factor * l_s[rows, :] + both[:, 128:]

    out_ref[...] = (a_s[...] / l_s[...]).astype(BF16)


def attend(q, state, exchanged, table, offsets, head_base):
    levels, heads = offsets.shape
    tokens = q.shape[0]
    half = heads // 2
    mine = pl.BlockSpec((tokens, 128), lambda h, offset: (0, h + head_base))

    def group_spec(array, shift):
        return pl.BlockSpec((array.shape[0], 128), lambda h, offset: (0, h + shift))

    return pl.pallas_call(
        functools.partial(attend_kernel, levels, head_base),
        grid_spec=pltpu.PrefetchScalarGridSpec(
            num_scalar_prefetch=1,
            grid=(half,),
            in_specs=[mine] * 4
            + [group_spec(a, head_base) for a in exchanged]
            + [group_spec(a, heads + head_base) for a in exchanged]
            + [whole_spec(table)],
            out_specs=pl.BlockSpec((tokens, 128), lambda h, offset: (0, h)),
            scratch_shapes=[
                pltpu.VMEM((tokens, 128), F32),
                pltpu.VMEM((tokens, 128), BF16),
                pltpu.VMEM((tokens, 256), BF16),
                pltpu.VMEM((tokens, 128), F32),
                pltpu.VMEM((tokens, 128), F32),
                pltpu.VMEM((tokens, 128), F32),
            ],
        ),
        out_shape=jax.ShapeDtypeStruct((tokens, 128 * half), BF16),
        compiler_params=pltpu.CompilerParams(vmem_limit_bytes=VMEM_LIMIT),
        cost_estimate=SMALL,
        name="attend",
    )(offsets, q, *state, *exchanged, *exchanged, table)


def output_kernel(group, n_arrays, share, *refs):
    owner_ref, refs = refs[0], refs[1:]
    arrays, refs = refs[:n_arrays], refs[n_arrays:]
    base_ref, w_ref, out_ref, x_s, w_s, piece_sems, w_sems = refs
    copies = copy_pieces([group], owner_ref, arrays, x_s, piece_sems)
    for i in range(w_s.shape[1]):
        copies.append(pltpu.make_async_copy(w_ref.at[share + i], w_s.at[:, i], w_sems.at[i]))
        copies[-1].start()
    for copy in copies:
        copy.wait()
    tile = 512
    rows, depth = x_s.shape

    @pl.loop(0, rows // tile)
    def _(n):
        at = pl.ds(pl.multiple_of(n * tile, tile), tile)
        weight = w_s[...].reshape(depth, out_ref.shape[1])
        total = jnp.dot(x_s[at, :], weight, preferred_element_type=F32)
        out_ref[at, :] = (base_ref[at, :].astype(F32) + total).astype(out_ref.dtype)


def output(pieces, base, w_columns, share, dtype):
    operands, groups, owners = piece_groups([(0, 0, pieces)])
    rows, width = base.shape
    shares = w_columns.shape[0] // 2
    depth = w_columns.size // width // 2
    anywhere = pl.BlockSpec(memory_space=pl.ANY)
    vector = pl.BlockSpec(memory_space=pltpu.VMEM)
    return pl.pallas_call(
        functools.partial(output_kernel, groups[0], len(operands), share),
        in_specs=[pl.BlockSpec(memory_space=pltpu.SMEM)]
        + [anywhere] * len(operands)
        + [vector, anywhere],
        out_specs=vector,
        scratch_shapes=[
            pltpu.VMEM((rows, depth), BF16),
            pltpu.VMEM((w_columns.shape[1], shares) + w_columns.shape[2:], BF16),
            pltpu.SemaphoreType.DMA((8,)),
            pltpu.SemaphoreType.DMA((shares,)),
        ],
        out_shape=jax.ShapeDtypeStruct((rows, width), dtype),
        compiler_params=pltpu.CompilerParams(vmem_limit_bytes=VMEM_LIMIT),
        cost_estimate=SMALL,
        name="output",
    )(owners, *operands, base, w_columns)


def column_shares(w_out):
    seq = lax.axis_index("seq")
    share = seq // 4 * 2 + seq % 2
    rows = w_out.shape[0] // 8
    part = lax.dynamic_slice_in_dim(w_out, share * rows, rows, 0)
    width = w_out.shape[1] // 8
    cut = part.reshape(rows, 8, width).transpose(1, 0, 2)
    return lax.all_to_all(cut, "tp", 0, 0, tiled=True)


def gather_shares(mine):
    groups = [[y * 4 + x_lo * 2 + core for y in range(4) for core in range(2)] for x_lo in range(2)]
    return lax.all_gather(mine, "seq", axis=0, axis_index_groups=groups)


def after(value, *others):
    return lax.optimization_barrier((value, *others))[0]


def on_device(tokens, norm_gain, w_query, w_key, w_value, w_out, offsets):
    rows = tokens.shape[0]
    levels, heads = offsets.shape
    quarter = rows // 4
    spans = ((0, quarter), (quarter, 2 * quarter), (3 * quarter, quarter))

    def keys_of(number, pieces, old):
        low, count = spans[number]
        return keys([(0, 0, pieces)], low, count, rows, old, norm_gain, w_key, w_value, offsets)

    first = gather_z_first(tokens[:quarter])
    second = gather_x_first(tokens[quarter : 3 * quarter], first[1][0], first[2][0])
    mine = column_shares(after(w_out, first[3][0]))
    old = keys_of(0, first, [])
    third = gather_x_first(tokens[3 * quarter :], old[0])
    w_columns = gather_shares(after(mine, old[1]))
    old = keys_of(1, second, old)
    old = keys_of(2, third, old)
    normed, k, v = old[:3]
    q = queries(normed, w_query, heads)
    state = attend_local(q, k, v)
    exchanged = exchange(*old[3:], q, state[0])
    table = key_table(rows // 16, levels)
    gathered = []
    for number, gather in enumerate((gather_z_first, gather_x_first)):
        attended = attend(q, state, exchanged, table, offsets, number * heads // 2)
        gathered.append(gather(attended))
    total = output(gathered[1], tokens, w_columns, 4, F32)
    return output(gathered[0], total, w_columns, 0, BF16)


def solution(mesh):
    placed = (
        P("seq", "tp"),
        P(),
        P(None, "tp"),
        P(None, "tp"),
        P(None, "tp"),
        P("tp", None),
        P(None, "tp"),
    )
    return jax.shard_map(
        on_device, mesh=mesh, in_specs=placed, out_specs=P("seq", "tp"), check_vma=False
    )
```

time: 472 us -> 275 us (0.58); the launches traced: 463 us -> 275 us
  waiting for transfers between devices: 224 us -> 95.1 us
  Pallas kernels: 0 us -> 86.8 us
  matrix products: 65.9 us -> 0 us
  local copies, waits for them, and re-layouts: 83.7 us -> 19.8 us
  other arithmetic: 65 us -> 6 us
  starting transfers between devices: 9.62 us -> 53 us
    reduce_scatter x1 -> x0, waiting for transfers between devices: 111 us -> none  [on_device(): lax.psum_scatter(term.astype(jnp.bfloat16), 'tp', scatter_dimension=1, ti...]
    all_gather x1, waiting for transfers between devices: 106 us -> 0.01 us  [gather_shares(): return lax.all_gather(mine, 'seq', axis=0, axis_index_groups=groups)]
    ppermute x10 -> x35, waiting for transfers between devices: 6.5 us -> 95 us  [the longest x18 56 us: z_shift(): return lax.ppermute(value, 'tp', pairs)]
    pallas_call x0 -> x9, Pallas kernels: none -> 86.8 us  [the longest x3 34.2 us: keys(): pl.pallas_call(functools.partial(keys_kernel, groups, len(operands), len(...]
    dot_general x14 -> x0, matrix products: 65.9 us -> none  [the longest x3 26.3 us: project(): jnp.dot(normed, weight, preferred_element_type=jnp.float32)]
    ppermute x10 -> x35, starting transfers between devices: 9.58 us -> 47.3 us  [the longest x18 26.5 us: z_shift(): return lax.ppermute(value, 'tp', pairs)]
    reduce_sum x14 -> x0, other arithmetic: 37.6 us -> none  [the longest x5 16.3 us: on_device(): total = jnp.sum(probs, -1)]
    broadcast_in_dim x35 -> x6, local copies, waits for them, and re-layouts: 34.1 us -> 0.01 us  [key_table(): jnp.full((count,), jnp.where(position & top != 0, -1, FAR), jnp.int32)]
  transfers between devices with their start and end apart: 12 -> 37, of which waited for: 4 -> 14; matrix products, arithmetic and copies ran while one was open for 20% -> 8% of each run, Pallas kernels for 0% -> 29%
where the time goes in v1:
time: 275 us
  waiting for transfers between devices  95.1 us (35%)
  Pallas kernels  86.8 us (32%)
  starting transfers between devices  53 us (19%)
  local copies, waits for them, and re-layouts  19.8 us (7%)
  between operations  13.9 us (5%)
  other arithmetic  6 us (2%)
    ppermute x18, waiting for transfers between devices, z_shift(): return lax.ppermute(value, 'tp', pairs)  56 us
    pallas_call x3, Pallas kernels, keys(): pl.pallas_call(functools.partial(keys_kernel, groups, len(operands), len(...  34.2 us
    ppermute x7, waiting for transfers between devices, x_swap(): return lax.ppermute(value, 'tp', [(t, t ^ 1) for t in range(8)])  31 us
    ppermute x18, starting transfers between devices, z_shift(): return lax.ppermute(value, 'tp', pairs)  26.5 us
    pallas_call x2, Pallas kernels, attend(): pl.pallas_call(functools.partial(attend_kernel, levels, head_base), grid_...  18.3 us
    pallas_call x2, Pallas kernels, output(): pl.pallas_call(functools.partial(output_kernel, groups[0], len(operands),...  15.9 us
    ppermute x10, starting transfers between devices, seq_swap(): return lax.ppermute(value, 'seq', [(s, s ^ mask) for s in range(16)])  11.1 us
    ppermute x7, starting transfers between devices, x_swap(): return lax.ppermute(value, 'tp', [(t, t ^ 1) for t in range(8)])  9.68 us
  transfers between devices with their start and end apart: 37, of which 14 were waited for; matrix products, arithmetic and copies ran while one was open for 8% of the time, Pallas kernels for 29%

profile of v1, /device:TPU:0, one launch (start us, length us, event | category | flops | bytes accessed | tf_op | source)
XLA Modules:
  0.0 274.5 jit_solution(6158264881490102809)
XLA Ops:
  6.5 1.1 slice_bitcast_fusion.7
  7.6 3.2 %collective-permute-start.10 = (bf16[512,512]{1,0:T(8,128)(2,1)S(1)}, bf16[512,512]{1,0:T(8,128)(2,1)S(1)}, u32[]{:S(2)}, u32[]{:S(2)}) collective-permute-start(bf16[512,512]{1,0:T(8,128)(2,1)S(1)} %get-tuple-element.66), channel_id=1, source_target_pairs={{0,1},{1,0},{2,3},{3,2},{4,5},{5,4},{6,7},{7,6},{8,9},{9,8},{10,11... | collective-permute-start | bytes 1572872 | tf_op jit(solution)/shard_map/ppermute | solution.py:26
  10.8 1.9 slice_bitcast_fusion.6
  12.7 1.9 collective-permute-start.1
  14.7 2.1 collective-permute-start.2
  16.8 6.0 %collective-permute-done.1.refs_3_ = bf16[256,512]{1,0:T(8,128)(2,1)S(1)} collective-permute-done((bf16[256,512]{1,0:T(8,128)(2,1)S(1)}, bf16[256,512]{1,0:T(8,128)(2,1)S(1)}, u32[]{:S(2)}, u32[]{:S(2)}) %collective-permute-start.1) | collective-permute-done | bytes 262176 | tf_op jit(solution)/shard_map/ppermute | solution.py:22
  23.0 2.1 collective-permute-start.11
  25.1 8.2 %collective-permute-done.3.refs_5_ = bf16[256,512]{1,0:T(8,128)(2,1)S(1)} collective-permute-done((bf16[256,512]{1,0:T(8,128)(2,1)S(1)}, bf16[256,512]{1,0:T(8,128)(2,1)S(1)}, u32[]{:S(2)}, u32[]{:S(2)}) %collective-permute-start.3) | collective-permute-done | bytes 262176 | tf_op jit(solution)/shard_map/ppermute | solution.py:22
  33.3 1.0 pad_maximum_fusion.3
  34.9 1.1 constant_dynamic-slice_fusion
  37.1 5.7 %all-to-all-start = ((bf16[8,64,512]{2,1,0:T(8,128)(2,1)}), bf16[8,64,512]{2,1,0:T(8,128)(2,1)}, u32[]{:S(2)}, u32[]{:S(2)}) async-start(bf16[8,64,512]{2,1,0:T(8,128)(2,1)} %copy.44), calls=%async_computation | async-start | bytes 1048576 | tf_op jit(solution)/shard_map/all_to_all | solution.py:498
  42.9 3.6 %collective-permute-start.4 = (bf16[256,512]{1,0:T(8,128)(2,1)S(1)}, bf16[256,512]{1,0:T(8,128)(2,1)}, u32[]{:S(2)}, u32[]{:S(2)}) collective-permute-start(bf16[256,512]{1,0:T(8,128)(2,1)S(1)} %get-tuple-element.68.refs_2_), channel_id=1, source_target_pairs={{0,1},{1,0},{2,3},{3,2},{4,5},{5,4},{6,7},{7,6},{8,9},{9,8},{10,11... | collective-permute-start | bytes 786440 | tf_op jit(solution)/shard_map/ppermute | solution.py:26
  47.8 17.7 %collective-permute-done.4.refs_6_ = bf16[256,512]{1,0:T(8,128)(2,1)} collective-permute-done((bf16[256,512]{1,0:T(8,128)(2,1)S(1)}, bf16[256,512]{1,0:T(8,128)(2,1)}, u32[]{:S(2)}, u32[]{:S(2)}) %collective-permute-start.4) | collective-permute-done | bytes 262176 | tf_op jit(solution)/shard_map/ppermute | solution.py:26
  65.6 9.7 %keys.3 = (bf16[1024,4096]{1,0:T(8,128)(2,1)}, bf16[1024,512]{1,0:T(8,128)(2,1)}, bf16[1024,512]{1,0:T(8,128)(2,1)}, bf16[960,1024]{1,0:T(8,128)(2,1)}, bf16[256...) custom-call(s32[8]{0:T(128)} %stack.139.refs_0_, s32[5,4]{1,0:T(8,128)} %copy.42.refs_1_.refs_0_, ...), custom_call_target="tpu_custom_call" | custom-call | flops 1024 | bytes 1024 | tf_op jit(solution)/shard_map/keys/pallas_call | solution.py:221
  75.3 1.8 pad_maximum_fusion.4.refs_2_
  77.1 3.2 %collective-permute-start.7 = (bf16[2,256,512]{2,1,0:T(8,128)(2,1)}, bf16[2,256,512]{2,1,0:T(8,128)(2,1)}, u32[]{:S(2)}, u32[]{:S(2)}) collective-permute-start(bf16[2,256,512]{2,1,0:T(8,128)(2,1)} %pad_maximum_fusion.4.refs_2_), channel_id=1, source_target_pairs={{0,6},{1,7},{2,0},{3,1},{4,2},{5,3},{6,4},{7,5},{8,14},{9,15},{10,... | collective-permute-start | bytes 1572872 | tf_op jit(solution)/shard_map/ppermute | solution.py:22
  81.4 3.3 %collective-permute-start.14 = (bf16[512,512]{1,0:T(8,128)(2,1)S(1)}, bf16[512,512]{1,0:T(8,128)(2,1)S(1)}, u32[]{:S(2)}, u32[]{:S(2)}) collective-permute-start(bf16[512,512]{1,0:T(8,128)(2,1)S(1)} %slice_bitcast_fusion.2), channel_id=1, source_target_pairs={{0,6},{1,7},{2,0},{3,1},{4,2},{5,3},{6,4},{7,5},{8,14},{9,15},{10,... | collective-permute-start | bytes 1572872 | tf_op jit(solution)/shard_map/ppermute | solution.py:22
  84.7 8.5 %collective-permute-done.6.refs_3_ = bf16[2,256,512]{2,1,0:T(8,128)(2,1)} collective-permute-done((bf16[2,256,512]{2,1,0:T(8,128)(2,1)}, bf16[2,256,512]{2,1,0:T(8,128)(2,1)}, u32[]{:S(2)}, u32[]{:S(2)}) %collective-permute-start.6) | collective-permute-done | bytes 524320 | tf_op jit(solution)/shard_map/ppermute | solution.py:22
  93.1 1.7 slice_bitcast_fusion.5
  94.8 1.7 slice_bitcast_fusion.4
  96.5 3.2 %collective-permute-start.9 = (bf16[256,512]{1,0:T(8,128)(2,1)}, bf16[256,512]{1,0:T(8,128)(2,1)}, u32[]{:S(2)}, u32[]{:S(2)}) collective-permute-start(bf16[256,512]{1,0:T(8,128)(2,1)} %slice_bitcast_fusion.4), channel_id=1, source_target_pairs={{0,6},{1,7},{2,0},{3,1},{4,2},{5,3},{6,4},{7,5},{8,14},{9,15},{10,... | collective-permute-start | bytes 786440 | tf_op jit(solution)/shard_map/ppermute | solution.py:22
  101.2 14.6 %keys.4 = (bf16[1024,4096]{1,0:T(8,128)(2,1)}, bf16[1024,512]{1,0:T(8,128)(2,1)}, bf16[1024,512]{1,0:T(8,128)(2,1)}, bf16[960,1024]{1,0:T(8,128)(2,1)}, bf16[256...) custom-call(s32[8]{0:T(128)} %stack.140.refs_0_, ...), custom_call_target="tpu_custom_call", output_to_operand_aliasing={{0}: (10, {}), {1}: (11, {}), {2}: (12, {}), {3}: (13, {}),... | custom-call | flops 1024 | bytes 1024 | tf_op jit(solution)/shard_map/keys/pallas_call | solution.py:221
  116.5 9.9 %keys.5 = (bf16[1024,4096]{1,0:T(8,128)(2,1)}, bf16[1024,512]{1,0:T(8,128)(2,1)}, bf16[1024,512]{1,0:T(8,128)(2,1)}, bf16[960,1024]{1,0:T(8,128)(2,1)}, bf16[256...) custom-call(s32[8]{0:T(128)} %stack.140.refs_0_, ...), custom_call_target="tpu_custom_call", output_to_operand_aliasing={{0}: (10, {}), {1}: (11, {}), {2}: (12, {}), {3}: (13, {}),... | custom-call | flops 1024 | bytes 1024 | tf_op jit(solution)/shard_map/keys/pallas_call | solution.py:221
  127.1 1.5 collective-permute-start.17
  128.7 1.4 collective-permute-start.19
  130.1 9.1 %queries.1.q_ref.refs_1_ = bf16[1024,512]{1,0:T(8,128)(2,1)} custom-call(bf16[1024,4096]{1,0:T(8,128)(2,1)} %get-tuple-element.51.x_ref, bf16[4096,512]{1,0:T(8,128)(2,1)} %w_ref.1), custom_call_target="tpu_custom_call" | custom-call | flops 1024 | bytes 1024 | tf_op jit(solution)/shard_map/queries/pallas_call | solution.py:257
  139.7 3.2 %collective-permute-start.20 = (bf16[64,1024]{1,0:T(8,128)(2,1)S(1)}, bf16[64,1024]{1,0:T(8,128)(2,1)S(1)}, u32[]{:S(2)}, u32[]{:S(2)}) collective-permute-start(bf16[64,1024]{1,0:T(8,128)(2,1)S(1)} %copy-done.15), channel_id=1, source_target_pairs={{0,64},{8,72},{16,80},{24,88},{32,96},{40,104},{48,112},{56,120},{... | collective-permute-start | bytes 393224 | tf_op jit(solution)/shard_map/ppermute | solution.py:30
  142.8 1.1 collective-permute-start.21
  143.9 9.2 %attend_local.1 = (f32[1024,512]{1,0:T(8,128)}, f32[1024,512]{1,0:T(8,128)}, f32[1024,512]{1,0:T(8,128)}) custom-call(bf16[1024,512]{1,0:T(8,128)(2,1)} %queries.1.q_ref.refs_1_, bf16[1024,512]{1,0:T(8,128)(2,1)} %get-tuple-element.52.k_ref, bf16[1024,512]{1,0:T(8,128)(2,1)} %get-tuple-element.53.v_ref), custom_call_target="tpu_custom_call" | custom-call | flops 1024 | bytes 1024 | tf_op jit(solution)/shard_map/attend_local/pallas_call | solution.py:354
  153.9 1.7 collective-permute-start.22
  161.0 1.5 collective-permute-done.23
  164.6 5.6 %collective-permute-done.15.refs_6_.refs_10_ = bf16[960,1024]{1,0:T(8,128)(2,1)} collective-permute-done((bf16[960,1024]{1,0:T(8,128)(2,1)S(1)}, bf16[960,1024]{1,0:T(8,128)(2,1)}, u32[]{:S(2)}, u32[]{:S(2)}) %collective-permute-start.15) | collective-permute-done | bytes 1966112 | tf_op jit(solution)/shard_map/ppermute | solution.py:30
  170.7 9.4 %attend.2.refs_1_ = bf16[1024,256]{1,0:T(8,128)(2,1)} custom-call(s32[5,4]{1,0:T(8,128)} %copy.42.refs_1_.refs_0_, bf16[1024,512]{1,0:T(8,128)(2,1)} %queries.1.q_ref.refs_1_, f32[1024,512]{1,0:T(8,128)} %get-tuple-element.54.refs_2_, f32[1024,512]{1,0:T(8,128)} %get-tuple-element.55.refs_3_, f32[1024,512]{1,0:T(8,128)} %get-tuple-element.56.refs_4_, ...), custom_call_target="tpu_custom_call" | custom-call | flops 1024 | bytes 1024 | tf_op jit(solution)/shard_map/attend/pallas_call | solution.py:418
  180.2 8.9 %attend.3 = bf16[1024,256]{1,0:T(8,128)(2,1)} custom-call(s32[5,4]{1,0:T(8,128)} %copy.42.refs_1_.refs_0_, bf16[1024,512]{1,0:T(8,128)(2,1)} %queries.1.q_ref.refs_1_, f32[1024,512]{1,0:T(8,128)} %get-tuple-element.54.refs_2_, f32[1024,512]{1,0:T(8,128)} %get-tuple-element.55.refs_3_, f32[1024,512]{1,0:T(8,128)} %get-tuple-element.56.refs_4_, ...), custom_call_target="tpu_custom_call" | custom-call | flops 1024 | bytes 1024 | tf_op jit(solution)/shard_map/attend/pallas_call | solution.py:418
  189.1 1.0 collective-permute-start.30
  190.1 3.2 %collective-permute-start.26 = (bf16[1024,256]{1,0:T(8,128)(2,1)}, bf16[1024,256]{1,0:T(8,128)(2,1)S(1)}, u32[]{:S(2)}, u32[]{:S(2)}) collective-permute-start(bf16[1024,256]{1,0:T(8,128)(2,1)} %attend.2.refs_1_), channel_id=1, source_target_pairs={{0,6},{1,7},{2,0},{3,1},{4,2},{5,3},{6,4},{7,5},{8,14},{9,15},{10,... | collective-permute-start | bytes 1572872 | tf_op jit(solution)/shard_map/ppermute | solution.py:22
  193.3 2.3 collective-permute-done.25.refs_2_
  195.6 9.2 %collective-permute-done.30 = bf16[1024,256]{1,0:T(8,128)(2,1)S(1)} collective-permute-done((bf16[1024,256]{1,0:T(8,128)(2,1)}, bf16[1024,256]{1,0:T(8,128)(2,1)S(1)}, u32[]{:S(2)}, u32[]{:S(2)}) %collective-permute-start.30) | collective-permute-done | bytes 524320 | tf_op jit(solution)/shard_map/ppermute | solution.py:26
  204.8 1.1 pad_maximum_fusion.2.refs_1_
  206.1 3.2 %collective-permute-start.32 = (bf16[2,1024,256]{2,1,0:T(8,128)(2,1)S(1)}, bf16[2,1024,256]{2,1,0:T(8,128)(2,1)S(1)}, u32[]{:S(2)}, u32[]{:S(2)}) collective-permute-start(bf16[2,1024,256]{2,1,0:T(8,128)(2,1)S(1)} %pad_maximum_fusion.2.refs_1_), channel_id=1, source_target_pairs={{0,6},{1,7},{2,0},{3,1},{4,2},{5,3},{6,4},{7,5},{8,14},{9,15},{10,... | collective-permute-start | bytes 3145736 | tf_op jit(solution)/shard_map/ppermute | solution.py:22
  209.3 1.3 collective-permute-done.27.refs_4_
  210.6 1.3 pad_maximum_fusion
  212.9 19.5 %collective-permute-done.31.refs_2_ = bf16[2,1024,256]{2,1,0:T(8,128)(2,1)S(1)} collective-permute-done((bf16[2,1024,256]{2,1,0:T(8,128)(2,1)S(1)}, bf16[2,1024,256]{2,1,0:T(8,128)(2,1)S(1)}, u32[]{:S(2)}, u32[]{:S(2)}) %collective-permute-start.31) | collective-permute-done | bytes 1048608 | tf_op jit(solution)/shard_map/ppermute | solution.py:22
  232.6 3.3 %collective-permute-start.34 = (bf16[1024,256]{1,0:T(8,128)(2,1)S(1)}, bf16[1024,256]{1,0:T(8,128)(2,1)}, u32[]{:S(2)}, u32[]{:S(2)}) collective-permute-start(bf16[1024,256]{1,0:T(8,128)(2,1)S(1)} %slice_bitcast_fusion), channel_id=1, source_target_pairs={{0,6},{1,7},{2,0},{3,1},{4,2},{5,3},{6,4},{7,5},{8,14},{9,15},{10,... | collective-permute-start | bytes 1572872 | tf_op jit(solution)/shard_map/ppermute | solution.py:22
  236.8 10.1 %collective-permute-done.33.refs_4_ = bf16[1024,256]{1,0:T(8,128)(2,1)} collective-permute-done((bf16[1024,256]{1,0:T(8,128)(2,1)S(1)}, bf16[1024,256]{1,0:T(8,128)(2,1)}, u32[]{:S(2)}, u32[]{:S(2)}) %collective-permute-start.33) | collective-permute-done | bytes 524320 | tf_op jit(solution)/shard_map/ppermute | solution.py:22
  246.9 8.0 %output.2.refs_7_ = f32[1024,512]{1,0:T(8,128)} custom-call(s32[8]{0:T(128)} %stack.140.refs_0_, bf16[2,1024,256]{2,1,0:T(8,128)(2,1)} %copy-done.2, bf16[2,1024,256]{2,1,0:T(8,128)(2,1)} %copy-done.5, bf16[2,1024,256]{2,1,0:T(8,128)(2,1)} %copy-done.6, bf16[1024,256]{1,0:T(8,128)(2,1)} %collective-permute-done.33.refs_4_, ...), custom_call_target="tpu_custom_call" | custom-call | flops 1024 | bytes 1024 | tf_op jit(solution)/shard_map/output/pallas_call | solution.py:472
  254.9 4.0 %collective-permute-done.28.refs_5_ = bf16[1024,256]{1,0:T(8,128)(2,1)S(1)} collective-permute-done((bf16[1024,256]{1,0:T(8,128)(2,1)}, bf16[1024,256]{1,0:T(8,128)(2,1)S(1)}, u32[]{:S(2)}, u32[]{:S(2)}) %collective-permute-start.28) | collective-permute-done | bytes 524320 | tf_op jit(solution)/shard_map/ppermute | solution.py:26
  259.7 7.9 %output.3 = bf16[1024,512]{1,0:T(8,128)(2,1)} custom-call(s32[8]{0:T(128)} %stack.139.refs_0_, bf16[1024,256]{1,0:T(8,128)(2,1)} %attend.2.refs_1_, bf16[1024,256]{1,0:T(8,128)(2,1)} %copy-done.7, bf16[1024,256]{1,0:T(8,128)(2,1)} %copy-done.8, bf16[1024,256]{1,0:T(8,128)(2,1)} %copy-done.9, bf16[1024,256]{1,0:T(8,128)(2,1)} %copy-done.17, ...), custom_call_target="tpu_custom_call" | custom-call | flops 1024 | bytes 1024 | tf_op jit(solution)/shard_map/output/pallas_call | solution.py:472
  (126 shorter events, 19.3 us)
Async XLA Ops:
  7.6 15.2 %collective-permute-start.10 = (bf16[512,512]{1,0:T(8,128)(2,1)S(1)}, bf16[512,512]{1,0:T(8,128)(2,1)S(1)}, u32[]{:S(2)}, u32[]{:S(2)}) collective-permute-start(bf16[512,512]{1,0:T(8,128)(2,1)S(1)} %get-tuple-element.66), channel_id=1, source_target_pairs={{0,1},{1,0},{2,3},{3,2},{4,5},{5,4},{6,7},{7,6},{8,9},{9,8},{10,11... | collective-permute-start | bytes 1572872 | tf_op jit(solution)/shard_map/ppermute | solution.py:26
  12.7 30.1 %copy-start.10 = (bf16[256,512]{1,0:T(8,128)(2,1)}, bf16[256,512]{1,0:T(8,128)(2,1)S(1)}, u32[]{:S(2)}) copy-start(bf16[256,512]{1,0:T(8,128)(2,1)S(1)} %get-tuple-element.68.refs_2_) | copy-start | bytes 786436
  12.7 10.1 %collective-permute-start.1 = (bf16[256,512]{1,0:T(8,128)(2,1)S(1)}, bf16[256,512]{1,0:T(8,128)(2,1)S(1)}, u32[]{:S(2)}, u32[]{:S(2)}) collective-permute-start(bf16[256,512]{1,0:T(8,128)(2,1)S(1)} %get-tuple-element.68.refs_2_), channel_id=1, source_target_pairs={{0,2},{1,3},{2,4},{3,5},{4,6},{5,7},{6,0},{7,1},{8,10},{9,11},{10,... | collective-permute-start | bytes 786440 | tf_op jit(solution)/shard_map/ppermute | solution.py:22
  14.7 8.2 %collective-permute-start.2 = (bf16[256,512]{1,0:T(8,128)(2,1)S(1)}, bf16[256,512]{1,0:T(8,128)(2,1)S(1)}, u32[]{:S(2)}, u32[]{:S(2)}) collective-permute-start(bf16[256,512]{1,0:T(8,128)(2,1)S(1)} %get-tuple-element.68.refs_2_), channel_id=1, source_target_pairs={{0,6},{1,7},{2,0},{3,1},{4,2},{5,3},{6,4},{7,5},{8,14},{9,15},{10,... | collective-permute-start | bytes 786440 | tf_op jit(solution)/shard_map/ppermute | solution.py:22
  22.8 10.5 %collective-permute-start.3 = (bf16[256,512]{1,0:T(8,128)(2,1)S(1)}, bf16[256,512]{1,0:T(8,128)(2,1)S(1)}, u32[]{:S(2)}, u32[]{:S(2)}) collective-permute-start(bf16[256,512]{1,0:T(8,128)(2,1)S(1)} %collective-permute-done.1.refs_3_), channel_id=1, source_target_pairs={{0,2},{1,3},{2,4},{3,5},{4,6},{5,7},{6,0},{7,1},{8,10},{9,11},{10,... | collective-permute-start | bytes 786440 | tf_op jit(solution)/shard_map/ppermute | solution.py:22
  22.9 14.2 %copy-start.1 = (bf16[2,512,512]{2,1,0:T(8,128)(2,1)}, bf16[2,512,512]{2,1,0:T(8,128)(2,1)S(1)}, u32[]{:S(2)}) copy-start(bf16[2,512,512]{2,1,0:T(8,128)(2,1)S(1)} %pad_maximum_fusion.1.refs_2_) | copy-start | bytes 3145732
  23.0 57.4 %collective-permute-start.11 = (bf16[2,512,512]{2,1,0:T(8,128)(2,1)S(1)}, bf16[2,512,512]{2,1,0:T(8,128)(2,1)S(1)}, u32[]{:S(2)}, u32[]{:S(2)}) collective-permute-start(bf16[2,512,512]{2,1,0:T(8,128)(2,1)S(1)} %pad_maximum_fusion.1.refs_2_), channel_id=1, source_target_pairs={{0,2},{1,3},{2,4},{3,5},{4,6},{5,7},{6,0},{7,1},{8,10},{9,11},{10,... | collective-permute-start | bytes 3145736 | tf_op jit(solution)/shard_map/ppermute | solution.py:22
  34.3 12.3 %copy-start.19 = (s32[5,4]{0,1:T(4,128)S(1)}, s32[5,4]{0,1:T(4,128)}, u32[]{:S(2)}) copy-start(s32[5,4]{0,1:T(4,128)} %param.13) | copy-start | bytes 244
  34.3 31.3 %collective-permute-start.5 = (bf16[3,256,512]{2,1,0:T(8,128)(2,1)}, bf16[3,256,512]{2,1,0:T(8,128)(2,1)}, u32[]{:S(2)}, u32[]{:S(2)}) collective-permute-start(bf16[3,256,512]{2,1,0:T(8,128)(2,1)} %pad_maximum_fusion.3), channel_id=1, source_target_pairs={{0,1},{1,0},{2,3},{3,2},{4,5},{5,4},{6,7},{7,6},{8,9},{9,8},{10,11... | collective-permute-start | bytes 2359304 | tf_op jit(solution)/shard_map/ppermute | solution.py:26
  34.3 47.0 %collective-permute-start.12 = (bf16[2,512,512]{2,1,0:T(8,128)(2,1)S(1)}, bf16[2,512,512]{2,1,0:T(8,128)(2,1)S(1)}, u32[]{:S(2)}, u32[]{:S(2)}) collective-permute-start(bf16[2,512,512]{2,1,0:T(8,128)(2,1)S(1)} %pad_maximum_fusion.1.refs_2_), channel_id=1, source_target_pairs={{0,6},{1,7},{2,0},{3,1},{4,2},{5,3},{6,4},{7,5},{8,14},{9,15},{10,... | collective-permute-start | bytes 3145736 | tf_op jit(solution)/shard_map/ppermute | solution.py:22
  37.1 43.2 %all-to-all-start = ((bf16[8,64,512]{2,1,0:T(8,128)(2,1)}), bf16[8,64,512]{2,1,0:T(8,128)(2,1)}, u32[]{:S(2)}, u32[]{:S(2)}) async-start(bf16[8,64,512]{2,1,0:T(8,128)(2,1)} %copy.44), calls=%async_computation | async-start | bytes 1048576 | tf_op jit(solution)/shard_map/all_to_all | solution.py:498
  42.8 204.1 %all-gather.3.cloned.1.call-start = ((), (), s32[]{:S(2)}) async-start(), calls=%async_computation.1 | async-start | bytes 4718592 | tf_op jit(solution)/shard_map/all_gather | solution.py:503
  42.9 22.7 %collective-permute-start.4 = (bf16[256,512]{1,0:T(8,128)(2,1)S(1)}, bf16[256,512]{1,0:T(8,128)(2,1)}, u32[]{:S(2)}, u32[]{:S(2)}) collective-permute-start(bf16[256,512]{1,0:T(8,128)(2,1)S(1)} %get-tuple-element.68.refs_2_), channel_id=1, source_target_pairs={{0,1},{1,0},{2,3},{3,2},{4,5},{5,4},{6,7},{7,6},{8,9},{9,8},{10,11... | collective-permute-start | bytes 786440 | tf_op jit(solution)/shard_map/ppermute | solution.py:26
  46.4 28.9 %collective-permute-start = (bf16[256,512]{1,0:T(8,128)(2,1)}, bf16[256,512]{1,0:T(8,128)(2,1)}, u32[]{:S(2)}, u32[]{:S(2)}) collective-permute-start(bf16[256,512]{1,0:T(8,128)(2,1)} %get-tuple-element.69), channel_id=1, source_target_pairs={{0,1},{1,0},{2,3},{3,2},{4,5},{5,4},{6,7},{7,6},{8,9},{9,8},{10,11... | collective-permute-start | bytes 786440 | tf_op jit(solution)/shard_map/ppermute | solution.py:26
  77.1 16.0 %collective-permute-start.6 = (bf16[2,256,512]{2,1,0:T(8,128)(2,1)}, bf16[2,256,512]{2,1,0:T(8,128)(2,1)}, u32[]{:S(2)}, u32[]{:S(2)}) collective-permute-start(bf16[2,256,512]{2,1,0:T(8,128)(2,1)} %pad_maximum_fusion.4.refs_2_), channel_id=1, source_target_pairs={{0,2},{1,3},{2,4},{3,5},{4,6},{5,7},{6,0},{7,1},{8,10},{9,11},{10,... | collective-permute-start | bytes 1572872 | tf_op jit(solution)/shard_map/ppermute | solution.py:22
  77.1 17.7 %collective-permute-start.7 = (bf16[2,256,512]{2,1,0:T(8,128)(2,1)}, bf16[2,256,512]{2,1,0:T(8,128)(2,1)}, u32[]{:S(2)}, u32[]{:S(2)}) collective-permute-start(bf16[2,256,512]{2,1,0:T(8,128)(2,1)} %pad_maximum_fusion.4.refs_2_), channel_id=1, source_target_pairs={{0,6},{1,7},{2,0},{3,1},{4,2},{5,3},{6,4},{7,5},{8,14},{9,15},{10,... | collective-permute-start | bytes 1572872 | tf_op jit(solution)/shard_map/ppermute | solution.py:22
  80.4 20.0 %copy-start.3 = (bf16[2,512,512]{2,1,0:T(8,128)(2,1)}, bf16[2,512,512]{2,1,0:T(8,128)(2,1)S(1)}, u32[]{:S(2)}) copy-start(bf16[2,512,512]{2,1,0:T(8,128)(2,1)S(1)} %collective-permute-done.11.refs_3_) | copy-start | bytes 3145732
  81.3 19.0 %collective-permute-start.13 = (bf16[512,512]{1,0:T(8,128)(2,1)}, bf16[512,512]{1,0:T(8,128)(2,1)}, u32[]{:S(2)}, u32[]{:S(2)}) collective-permute-start(bf16[512,512]{1,0:T(8,128)(2,1)} %slice_bitcast_fusion.3), channel_id=1, source_target_pairs={{0,2},{1,3},{2,4},{3,5},{4,6},{5,7},{6,0},{7,1},{8,10},{9,11},{10,... | collective-permute-start | bytes 1572872 | tf_op jit(solution)/shard_map/ppermute | solution.py:22
  81.3 19.1 %copy-start.4 = (bf16[2,512,512]{2,1,0:T(8,128)(2,1)}, bf16[2,512,512]{2,1,0:T(8,128)(2,1)S(1)}, u32[]{:S(2)}) copy-start(bf16[2,512,512]{2,1,0:T(8,128)(2,1)S(1)} %collective-permute-done.12.refs_4_) | copy-start | bytes 3145732
  81.4 19.0 %collective-permute-start.14 = (bf16[512,512]{1,0:T(8,128)(2,1)S(1)}, bf16[512,512]{1,0:T(8,128)(2,1)S(1)}, u32[]{:S(2)}, u32[]{:S(2)}) collective-permute-start(bf16[512,512]{1,0:T(8,128)(2,1)S(1)} %slice_bitcast_fusion.2), channel_id=1, source_target_pairs={{0,6},{1,7},{2,0},{3,1},{4,2},{5,3},{6,4},{7,5},{8,14},{9,15},{10,... | collective-permute-start | bytes 1572872 | tf_op jit(solution)/shard_map/ppermute | solution.py:22
  94.8 21.0 %collective-permute-start.8 = (bf16[256,512]{1,0:T(8,128)(2,1)}, bf16[256,512]{1,0:T(8,128)(2,1)S(1)}, u32[]{:S(2)}, u32[]{:S(2)}) collective-permute-start(bf16[256,512]{1,0:T(8,128)(2,1)} %slice_bitcast_fusion.5), channel_id=1, source_target_pairs={{0,2},{1,3},{2,4},{3,5},{4,6},{5,7},{6,0},{7,1},{8,10},{9,11},{10,... | collective-permute-start | bytes 786440 | tf_op jit(solution)/shard_map/ppermute | solution.py:22
  96.5 19.3 %collective-permute-start.9 = (bf16[256,512]{1,0:T(8,128)(2,1)}, bf16[256,512]{1,0:T(8,128)(2,1)}, u32[]{:S(2)}, u32[]{:S(2)}) collective-permute-start(bf16[256,512]{1,0:T(8,128)(2,1)} %slice_bitcast_fusion.4), channel_id=1, source_target_pairs={{0,6},{1,7},{2,0},{3,1},{4,2},{5,3},{6,4},{7,5},{8,14},{9,15},{10,... | collective-permute-start | bytes 786440 | tf_op jit(solution)/shard_map/ppermute | solution.py:22
  126.4 12.8 %collective-permute-start.16 = (bf16[192,1024]{1,0:T(8,128)(2,1)}, bf16[192,1024]{1,0:T(8,128)(2,1)S(1)}, u32[]{:S(2)}, u32[]{:S(2)}) collective-permute-start(bf16[192,1024]{1,0:T(8,128)(2,1)} %get-tuple-element.58), channel_id=1, source_target_pairs={{0,16},{8,24},{16,0},{24,8},{32,48},{40,56},{48,32},{56,40},{64,80... | collective-permute-start | bytes 1179656 | tf_op jit(solution)/shard_map/ppermute | solution.py:30
  127.1 26.8 %collective-permute-start.17 = (bf16[192,1024]{1,0:T(8,128)(2,1)}, bf16[192,1024]{1,0:T(8,128)(2,1)S(1)}, u32[]{:S(2)}, u32[]{:S(2)}) collective-permute-start(bf16[192,1024]{1,0:T(8,128)(2,1)} %get-tuple-element.58), channel_id=1, source_target_pairs={{0,32},{8,40},{16,48},{24,56},{32,0},{40,8},{48,16},{56,24},{64,96... | collective-permute-start | bytes 1179656 | tf_op jit(solution)/shard_map/ppermute | solution.py:30
  128.7 29.1 %collective-permute-start.19 = (bf16[256,1024]{1,0:T(8,128)(2,1)}, bf16[256,1024]{1,0:T(8,128)(2,1)S(1)}, u32[]{:S(2)}, u32[]{:S(2)}) collective-permute-start(bf16[256,1024]{1,0:T(8,128)(2,1)} %get-tuple-element.60), channel_id=1, source_target_pairs={{0,16},{8,24},{16,0},{24,8},{32,48},{40,56},{48,32},{56,40},{64,80... | collective-permute-start | bytes 1572872 | tf_op jit(solution)/shard_map/ppermute | solution.py:30
  139.2 17.2 %collective-permute-start.18 = (bf16[192,1024]{1,0:T(8,128)(2,1)S(1)}, bf16[192,1024]{1,0:T(8,128)(2,1)S(1)}, u32[]{:S(2)}, u32[]{:S(2)}) collective-permute-start(bf16[192,1024]{1,0:T(8,128)(2,1)S(1)} %collective-permute-done.16), channel_id=1, source_target_pairs={{0,32},{8,40},{16,48},{24,56},{32,0},{40,8},{48,16},{56,24},{64,96... | collective-permute-start | bytes 1179656 | tf_op jit(solution)/shard_map/ppermute | solution.py:30
  139.7 18.9 %collective-permute-start.20 = (bf16[64,1024]{1,0:T(8,128)(2,1)S(1)}, bf16[64,1024]{1,0:T(8,128)(2,1)S(1)}, u32[]{:S(2)}, u32[]{:S(2)}) collective-permute-start(bf16[64,1024]{1,0:T(8,128)(2,1)S(1)} %copy-done.15), channel_id=1, source_target_pairs={{0,64},{8,72},{16,80},{24,88},{32,96},{40,104},{48,112},{56,120},{... | collective-permute-start | bytes 393224 | tf_op jit(solution)/shard_map/ppermute | solution.py:30
  142.8 16.4 %collective-permute-start.21 = (bf16[64,1024]{1,0:T(8,128)(2,1)S(1)}, bf16[64,1024]{1,0:T(8,128)(2,1)S(1)}, u32[]{:S(2)}, u32[]{:S(2)}) collective-permute-start(bf16[64,1024]{1,0:T(8,128)(2,1)S(1)} %copy-done.15), channel_id=1, source_target_pairs={{0,96},{8,104},{16,112},{24,120},{32,64},{40,72},{48,80},{56,88},{... | collective-permute-start | bytes 393224 | tf_op jit(solution)/shard_map/ppermute | solution.py:30
  153.9 6.5 %collective-permute-start.22 = (bf16[64,1024]{1,0:T(8,128)(2,1)S(1)}, bf16[64,1024]{1,0:T(8,128)(2,1)S(1)}, u32[]{:S(2)}, u32[]{:S(2)}) collective-permute-start(bf16[64,1024]{1,0:T(8,128)(2,1)S(1)} %slice.37), channel_id=1, source_target_pairs={{0,64},{8,72},{16,80},{24,88},{32,96},{40,104},{48,112},{56,120},{... | collective-permute-start | bytes 393224 | tf_op jit(solution)/shard_map/ppermute | solution.py:30
  156.3 6.2 %collective-permute-start.23 = (bf16[64,1024]{1,0:T(8,128)(2,1)S(1)}, bf16[64,1024]{1,0:T(8,128)(2,1)S(1)}, u32[]{:S(2)}, u32[]{:S(2)}) collective-permute-start(bf16[64,1024]{1,0:T(8,128)(2,1)S(1)} %slice.37), channel_id=1, source_target_pairs={{0,96},{8,104},{16,112},{24,120},{32,64},{40,72},{48,80},{56,88},{... | collective-permute-start | bytes 393224 | tf_op jit(solution)/shard_map/ppermute | solution.py:30
  163.2 7.5 %collective-permute-start.24 = (bf16[1088,1024]{1,0:T(8,128)(2,1)}, bf16[1088,1024]{1,0:T(8,128)(2,1)}, u32[]{:S(2)}, u32[]{:S(2)}) collective-permute-start(bf16[1088,1024]{1,0:T(8,128)(2,1)} %constant_dynamic-update-slice_fusion.refs_7_.refs_11_), channel_id=1, source_target_pairs={{0,8},{8,0},{16,24},{24,16},{32,40},{40,32},{48,56},{56,48},{64,72... | collective-permute-start | bytes 6684680 | tf_op jit(solution)/shard_map/ppermute | solution.py:30
  163.2 7.0 %collective-permute-start.15 = (bf16[960,1024]{1,0:T(8,128)(2,1)S(1)}, bf16[960,1024]{1,0:T(8,128)(2,1)}, u32[]{:S(2)}, u32[]{:S(2)}) collective-permute-start(bf16[960,1024]{1,0:T(8,128)(2,1)S(1)} %copy-done), channel_id=1, source_target_pairs={{0,8},{8,0},{16,24},{24,16},{32,40},{40,32},{48,56},{56,48},{64,72... | collective-permute-start | bytes 5898248 | tf_op jit(solution)/shard_map/ppermute | solution.py:30
  180.1 15.5 %collective-permute-start.25 = (bf16[1024,256]{1,0:T(8,128)(2,1)}, bf16[1024,256]{1,0:T(8,128)(2,1)S(1)}, u32[]{:S(2)}, u32[]{:S(2)}) collective-permute-start(bf16[1024,256]{1,0:T(8,128)(2,1)} %attend.2.refs_1_), channel_id=1, source_target_pairs={{0,2},{1,3},{2,4},{3,5},{4,6},{5,7},{6,0},{7,1},{8,10},{9,11},{10,... | collective-permute-start | bytes 1572872 | tf_op jit(solution)/shard_map/ppermute | solution.py:22
  189.1 15.8 %collective-permute-start.30 = (bf16[1024,256]{1,0:T(8,128)(2,1)}, bf16[1024,256]{1,0:T(8,128)(2,1)S(1)}, u32[]{:S(2)}, u32[]{:S(2)}) collective-permute-start(bf16[1024,256]{1,0:T(8,128)(2,1)} %attend.3), channel_id=1, source_target_pairs={{0,1},{1,0},{2,3},{3,2},{4,5},{5,4},{6,7},{7,6},{8,9},{9,8},{10,11... | collective-permute-start | bytes 1572872 | tf_op jit(solution)/shard_map/ppermute | solution.py:26
  190.1 19.2 %collective-permute-start.26 = (bf16[1024,256]{1,0:T(8,128)(2,1)}, bf16[1024,256]{1,0:T(8,128)(2,1)S(1)}, u32[]{:S(2)}, u32[]{:S(2)}) collective-permute-start(bf16[1024,256]{1,0:T(8,128)(2,1)} %attend.2.refs_1_), channel_id=1, source_target_pairs={{0,6},{1,7},{2,0},{3,1},{4,2},{5,3},{6,4},{7,5},{8,14},{9,15},{10,... | collective-permute-start | bytes 1572872 | tf_op jit(solution)/shard_map/ppermute | solution.py:22
  195.6 16.4 %copy-start.7 = (bf16[1024,256]{1,0:T(8,128)(2,1)}, bf16[1024,256]{1,0:T(8,128)(2,1)S(1)}, u32[]{:S(2)}) copy-start(bf16[1024,256]{1,0:T(8,128)(2,1)S(1)} %collective-permute-done.25.refs_2_) | copy-start | bytes 1572868
  195.6 15.0 %collective-permute-start.27 = (bf16[1024,256]{1,0:T(8,128)(2,1)S(1)}, bf16[1024,256]{1,0:T(8,128)(2,1)S(1)}, u32[]{:S(2)}, u32[]{:S(2)}) collective-permute-start(bf16[1024,256]{1,0:T(8,128)(2,1)S(1)} %collective-permute-done.25.refs_2_), channel_id=1, source_target_pairs={{0,2},{1,3},{2,4},{3,5},{4,6},{5,7},{6,0},{7,1},{8,10},{9,11},{10,... | collective-permute-start | bytes 1572872 | tf_op jit(solution)/shard_map/ppermute | solution.py:22
  206.0 26.6 %copy-start.2 = (bf16[2,1024,256]{2,1,0:T(8,128)(2,1)}, bf16[2,1024,256]{2,1,0:T(8,128)(2,1)S(1)}, u32[]{:S(2)}) copy-start(bf16[2,1024,256]{2,1,0:T(8,128)(2,1)S(1)} %pad_maximum_fusion.2.refs_1_) | copy-start | bytes 3145732
  206.0 26.4 %collective-permute-start.31 = (bf16[2,1024,256]{2,1,0:T(8,128)(2,1)S(1)}, bf16[2,1024,256]{2,1,0:T(8,128)(2,1)S(1)}, u32[]{:S(2)}, u32[]{:S(2)}) collective-permute-start(bf16[2,1024,256]{2,1,0:T(8,128)(2,1)S(1)} %pad_maximum_fusion.2.refs_1_), channel_id=1, source_target_pairs={{0,2},{1,3},{2,4},{3,5},{4,6},{5,7},{6,0},{7,1},{8,10},{9,11},{10,... | collective-permute-start | bytes 3145736 | tf_op jit(solution)/shard_map/ppermute | solution.py:22
  206.1 26.5 %collective-permute-start.32 = (bf16[2,1024,256]{2,1,0:T(8,128)(2,1)S(1)}, bf16[2,1024,256]{2,1,0:T(8,128)(2,1)S(1)}, u32[]{:S(2)}, u32[]{:S(2)}) collective-permute-start(bf16[2,1024,256]{2,1,0:T(8,128)(2,1)S(1)} %pad_maximum_fusion.2.refs_1_), channel_id=1, source_target_pairs={{0,6},{1,7},{2,0},{3,1},{4,2},{5,3},{6,4},{7,5},{8,14},{9,15},{10,... | collective-permute-start | bytes 3145736 | tf_op jit(solution)/shard_map/ppermute | solution.py:22
  209.3 23.3 %copy-start.8 = (bf16[1024,256]{1,0:T(8,128)(2,1)}, bf16[1024,256]{1,0:T(8,128)(2,1)S(1)}, u32[]{:S(2)}) copy-start(bf16[1024,256]{1,0:T(8,128)(2,1)S(1)} %collective-permute-done.26.refs_3_) | copy-start | bytes 1572868
  210.6 22.0 %copy-start.9 = (bf16[1024,256]{1,0:T(8,128)(2,1)}, bf16[1024,256]{1,0:T(8,128)(2,1)S(1)}, u32[]{:S(2)}) copy-start(bf16[1024,256]{1,0:T(8,128)(2,1)S(1)} %collective-permute-done.27.refs_4_) | copy-start | bytes 1572868
  212.0 46.9 %collective-permute-start.29 = (bf16[3,1024,256]{2,1,0:T(8,128)(2,1)}, bf16[3,1024,256]{2,1,0:T(8,128)(2,1)}, u32[]{:S(2)}, u32[]{:S(2)}) collective-permute-start(bf16[3,1024,256]{2,1,0:T(8,128)(2,1)} %pad_maximum_fusion), channel_id=1, source_target_pairs={{0,1},{1,0},{2,3},{3,2},{4,5},{5,4},{6,7},{7,6},{8,9},{9,8},{10,11... | collective-permute-start | bytes 4718600 | tf_op jit(solution)/shard_map/ppermute | solution.py:26
  232.4 14.5 %copy-start.5 = (bf16[2,1024,256]{2,1,0:T(8,128)(2,1)}, bf16[2,1024,256]{2,1,0:T(8,128)(2,1)S(1)}, u32[]{:S(2)}) copy-start(bf16[2,1024,256]{2,1,0:T(8,128)(2,1)S(1)} %collective-permute-done.31.refs_2_) | copy-start | bytes 3145732
  232.4 14.5 %collective-permute-start.33 = (bf16[1024,256]{1,0:T(8,128)(2,1)S(1)}, bf16[1024,256]{1,0:T(8,128)(2,1)}, u32[]{:S(2)}, u32[]{:S(2)}) collective-permute-start(bf16[1024,256]{1,0:T(8,128)(2,1)S(1)} %slice_bitcast_fusion.1), channel_id=1, source_target_pairs={{0,2},{1,3},{2,4},{3,5},{4,6},{5,7},{6,0},{7,1},{8,10},{9,11},{10,... | collective-permute-start | bytes 1572872 | tf_op jit(solution)/shard_map/ppermute | solution.py:22
  232.5 14.4 %copy-start.6 = (bf16[2,1024,256]{2,1,0:T(8,128)(2,1)}, bf16[2,1024,256]{2,1,0:T(8,128)(2,1)S(1)}, u32[]{:S(2)}) copy-start(bf16[2,1024,256]{2,1,0:T(8,128)(2,1)S(1)} %collective-permute-done.32.refs_3_) | copy-start | bytes 3145732
  232.6 14.3 %collective-permute-start.34 = (bf16[1024,256]{1,0:T(8,128)(2,1)S(1)}, bf16[1024,256]{1,0:T(8,128)(2,1)}, u32[]{:S(2)}, u32[]{:S(2)}) collective-permute-start(bf16[1024,256]{1,0:T(8,128)(2,1)S(1)} %slice_bitcast_fusion), channel_id=1, source_target_pairs={{0,6},{1,7},{2,0},{3,1},{4,2},{5,3},{6,4},{7,5},{8,14},{9,15},{10,... | collective-permute-start | bytes 1572872 | tf_op jit(solution)/shard_map/ppermute | solution.py:22
  235.9 23.0 %collective-permute-start.28 = (bf16[1024,256]{1,0:T(8,128)(2,1)}, bf16[1024,256]{1,0:T(8,128)(2,1)S(1)}, u32[]{:S(2)}, u32[]{:S(2)}) collective-permute-start(bf16[1024,256]{1,0:T(8,128)(2,1)} %attend.2.refs_1_), channel_id=1, source_target_pairs={{0,1},{1,0},{2,3},{3,2},{4,5},{5,4},{6,7},{7,6},{8,9},{9,8},{10,11... | collective-permute-start | bytes 1572872 | tf_op jit(solution)/shard_map/ppermute | solution.py:26
  (9 other events, 55.7 us)
Sparse Core Ops, SparseCore 0:
  80.5 29.1 all-gather.2

commit v2 on v1

v2 whole, which is shorter than its diff:
```python
import functools
import math

import jax
import jax.numpy as jnp
from jax import lax
from jax.experimental import pallas as pl
from jax.experimental.pallas import tpu as pltpu
from jax.sharding import PartitionSpec as P

BF16 = jnp.bfloat16
F32 = jnp.float32
LOG2E = math.log2(math.e)
LOW = -1e30
FAR = 1 << 20
VMEM_LIMIT = 56 * 1024 * 1024
FLOPS_PER_US = 1000000000
F1 = 0
F3 = 1
F4 = 1
F7 = 1
F8 = 0
F9 = 0
CO = 30
CA = 9
C0 = 12
C1 = 20
C2 = 8
F5 = 1
F6 = 0


def cost(us):
    return pl.CostEstimate(flops=int(us * FLOPS_PER_US), bytes_accessed=1024, transcendentals=0)


def z_shift(value, step):
    pairs = [(t, ((t // 2 + step) % 4) * 2 + t % 2) for t in range(8)]
    return lax.ppermute(value, "tp", pairs)


def x_swap(value):
    return lax.ppermute(value, "tp", [(t, t ^ 1) for t in range(8)])


def seq_swap(value, mask):
    return lax.ppermute(value, "seq", [(s, s ^ mask) for s in range(16)])


def x_first_pieces(pair, below, above, far_own, far_other):
    return [
        (pair, 0, 0, 0),
        (pair, 1, 0, 1),
        (below, 0, -1, 0),
        (below, 1, -1, 1),
        (above, 0, 1, 0),
        (above, 1, 1, 1),
        (far_own, None, 2, 0),
        (far_other, None, 2, 1),
    ]


def z_first_pieces(block, below, above, far, other, others, other_far=None):
    return [
        (block, None, 0, 0),
        (below, None, -1, 0),
        (above, None, 1, 0),
        (far, None, 2, 0),
        (other, None, 0, 1),
        (others, 0, -1, 1),
        (others, 1, 1, 1),
        (others, 2, 2, 1) if other_far is None else (other_far, None, 2, 1),
    ]


def piece_owners(pieces):
    tp = lax.axis_index("tp")
    z, x = tp // 2, tp % 2
    owners = [((z + dz + 4) % 4) * 2 + (x ^ dx) for _, _, dz, dx in pieces]
    return jnp.stack(owners).astype(jnp.int32)


def split_pieces(pieces):
    arrays, where = [], []
    for array, index, _, _ in pieces:
        for number, seen in enumerate(arrays):
            if seen is array:
                break
        else:
            number = len(arrays)
            arrays.append(array)
        where.append((number, index))
    return arrays, where


def whole_spec(array):
    zeros = (0,) * array.ndim
    return pl.BlockSpec(array.shape, lambda *_: zeros)


def copy_pieces(where, owner_ref, arrays, x_s, sems, owned):
    copies = []
    for number, (array, index) in enumerate(where):
        source = arrays[array] if index is None else arrays[array].at[index]
        depth = source.shape[1]
        place = owner_ref[number] if owned else number
        low = pl.multiple_of(place * depth, depth) if owned else number * depth
        copies.append(
            pltpu.make_async_copy(source, x_s.at[:, pl.ds(low, depth)], sems.at[number])
        )
        copies[-1].start()
    return copies


def pick_places(levels, tokens, first, rows):
    unit = tokens // 16
    places = []
    base = 0
    for level in range(1, levels):
        count = rows >> level
        at = base + (first >> level)
        lows = [
            at,
            at - 8 * unit if level == 2 else None,
            at - 12 * unit if level >= 3 else None,
            at - 14 * unit if level == 4 else None,
        ]
        places.append((count, lows))
        base += tokens >> level
    return places


def project_kernel(where, n_arrays, first, heads, levels, q_scale, has_before, final, n_old, *refs):
    owner_ref, offset_ref = refs[:2]
    arrays = refs[2 : 2 + n_arrays]
    gain_ref, *w_refs = refs[2 + n_arrays : 6 + n_arrays]
    refs = refs[6 + n_arrays :]
    if has_before:
        acc_in, square_in = refs[:2]
        refs = refs[2:]
    refs = refs[n_old:]
    n_out = 7 if final else 2
    outs, refs = refs[:n_out], refs[n_out:]
    x_s, w_s, acc_s, square_s, piece_sems, w_sems, acc_sems, square_sem = refs[:8]
    rows = x_s.shape[0]
    depth = x_s.shape[1] // len(where)

    copies = copy_pieces(where, owner_ref, arrays, x_s, piece_sems, False)
    w_copies = []
    for i, w_ref in enumerate(w_refs):
        for number in range(len(where)):
            low = pl.multiple_of(owner_ref[number] * depth, depth)
            w_copies.append(
                pltpu.make_async_copy(
                    w_ref.at[pl.ds(low, depth)],
                    w_s.at[i, number * depth : (number + 1) * depth],
                    w_sems.at[i, number],
                )
            )
            w_copies[-1].start()
    before = []
    if has_before:
        square_copy = pltpu.make_async_copy(square_in, square_s, square_sem)
        square_copy.start()
        before = [pltpu.make_async_copy(acc_in.at[i], acc_s.at[i], acc_sems.at[i]) for i in range(3)]
        for copy in before:
            copy.start()
        square_copy.wait()
    else:
        square_s[...] = jnp.zeros_like(square_s)

    for number, copy in enumerate(copies):
        copy.wait()
        gain = gain_ref[pl.ds(owner_ref[number], 1), :]
        lanes = slice(number * depth, (number + 1) * depth)

        def gained(i, carry, gain=gain, lanes=lanes):
            at = pl.ds(pl.multiple_of(i * 64, 64), 64)
            value = x_s[at, lanes].astype(F32)
            square = value * value
            total = square_s[at, :]
            for low in range(0, depth, 128):
                total += square[:, low : low + 128]
            square_s[at, :] = total
            x_s[at, lanes] = (value * gain).astype(BF16)
            return carry

        lax.fori_loop(0, rows // 64, gained, 0, unroll=2)

    tile = 256
    waits = []
    if final:
        kvq_s, split_s, pick_s, out_sems, pick_sems = refs[8:]
        k_out, v_out, q_out = outs[:3]
        picks = outs[3:7]
    for i in range(3):
        for copy in w_copies[len(where) * i : len(where) * (i + 1)] + before[i : i + 1]:
            copy.wait()

        @pl.loop(0, rows // tile)
        def _(n, i=i):
            at = pl.ds(pl.multiple_of(n * tile, tile), tile)
            full = jnp.dot(x_s[at, :], w_s[i], preferred_element_type=F32)
            if has_before:
                full += acc_s[i, at, :]
            if not final:
                acc_s[i, at, :] = full
                return
            mean = jnp.sum(square_s[at, :], 1, keepdims=True) / (depth * 8)
            scaled = lax.rsqrt(mean + 1e-05)
            full = full * (scaled * q_scale if i == 2 else scaled)
            kvq_s[i, at, :] = full.astype(BF16)
            if i < 2:
                for head in range(heads):
                    split_s[i * heads + head, at, :] = full[:, head * 128 : head * 128 + 128]

        if final:
            out = (k_out, v_out, q_out)[i]
            here = slice(first, first + rows)
            waits.append(pltpu.make_async_copy(kvq_s.at[i], out.at[here], out_sems.at[i]))
        else:
            waits.append(pltpu.make_async_copy(acc_s.at[i], outs[0].at[i], acc_sems.at[i]))
        waits[-1].start()
        if i != 1 or not final:
            continue
        tokens = k_out.shape[0]
        local = 0
        for level, (count, lows) in enumerate(pick_places(levels, tokens, first, rows), 1):
            for head in range(heads):
                start = offset_ref[level, head]
                for side in range(2):
                    lane = (side * heads + head) * 128
                    pick_s[local : local + count, lane : lane + 128] = split_s[
                        side * heads + head, pl.ds(start, count, stride=2**level), :
                    ].astype(BF16)
            for which, low in enumerate(lows):
                if low is not None:
                    waits.append(
                        pltpu.make_async_copy(
                            pick_s.at[local : local + count],
                            picks[which].at[low : low + count],
                            pick_sems.at[level - 1, which],
                        )
                    )
                    waits[-1].start()
            local += count
    if not final:
        waits.append(pltpu.make_async_copy(square_s, outs[1], square_sem))
        waits[-1].start()
    for copy in waits:
        copy.wait()


def project(pieces, first, tokens, before, old, final, norm_gain, weights, offsets, us):
    operands, where = split_pieces(pieces)
    rows, depth = pieces[-1][0].shape[-2:]
    width = weights[0].shape[1]
    levels, heads = offsets.shape
    unit = tokens // 16
    if final:
        outs = [jax.ShapeDtypeStruct((tokens, width), BF16)] * 3
        outs += [jax.ShapeDtypeStruct((n * unit, 2 * width), BF16) for n in (15, 4, 3, 1)]
    else:
        outs = [
            jax.ShapeDtypeStruct((3, rows, width), F32),
            jax.ShapeDtypeStruct((rows, 128), F32),
        ]
    anywhere = pl.BlockSpec(memory_space=pl.ANY)
    scalars = pl.BlockSpec(memory_space=pltpu.SMEM)
    vector = pl.BlockSpec(memory_space=pltpu.VMEM)
    scratch = [
        pltpu.VMEM((rows, len(where) * depth), BF16),
        pltpu.VMEM((3, len(where) * depth, width), BF16),
        pltpu.VMEM((3, rows, width) if before or not final else (1, 8, 128), F32),
        pltpu.VMEM((rows, 128), F32),
        pltpu.SemaphoreType.DMA((len(where),)),
        pltpu.SemaphoreType.DMA((3, len(where))),
        pltpu.SemaphoreType.DMA((3,)),
        pltpu.SemaphoreType.DMA,
    ]
    if final:
        scratch += [
            pltpu.VMEM((3, rows, width), BF16),
            pltpu.VMEM((2 * heads, rows, 128), F32),
            pltpu.VMEM((rows * 15 // 16, 2 * width), BF16),
            pltpu.SemaphoreType.DMA((3,)),
            pltpu.SemaphoreType.DMA((levels - 1, 4)),
        ]
    lead = 6 + len(operands) + len(before)
    return pl.pallas_call(
        functools.partial(
            project_kernel,
            where,
            len(operands),
            first,
            heads,
            levels,
            LOG2E * (width // heads) ** (-0.5),
            bool(before),
            final,
            len(old),
        ),
        in_specs=[scalars, scalars]
        + [anywhere] * len(operands)
        + [vector]
        + [anywhere] * (3 + len(before) + len(old)),
        out_specs=[anywhere for _ in outs],
        scratch_shapes=scratch,
        out_shape=outs,
        input_output_aliases={lead + i: i for i in range(len(old))},
        compiler_params=pltpu.CompilerParams(vmem_limit_bytes=VMEM_LIMIT),
        cost_estimate=cost(us),
        name="project",
    )(
        piece_owners(pieces),
        offsets,
        *operands,
        norm_gain.reshape(-1, depth),
        *weights,
        *before,
        *old,
    )


def first_exchange(own, second, p34, fourth):
    by_x = seq_swap(p34, 2)
    by_y = seq_swap(p34, 4)
    by_x2 = seq_swap(second, 2)
    by_y2 = seq_swap(fourth, 8)
    by_y3 = seq_swap(fourth, 12)
    core_own = seq_swap(own, 1)
    return own, core_own, by_x, by_y, by_x2, by_y2, by_y3


def second_exchange(own, core_own, by_x, by_y, by_x2, by_y2, by_y3, ready):
    unit = by_y2.shape[0]
    by_x, by_y, by_x2 = after(by_x, ready, by_y), after(by_y, ready), after(by_x2, ready)
    by_y2, by_y3 = after(by_y2, ready), after(by_y3, ready)
    by_yx = seq_swap(by_x, 4)
    x_fourth = by_x[2 * unit :]
    by_y2x = seq_swap(x_fourth, 8)
    by_y3x = seq_swap(x_fourth, 12)
    others = [by_x, by_y, by_x2, by_y2, by_y3, by_yx, by_y2x, by_y3x]
    return own, core_own, *others, *[seq_swap(value, 1) for value in others]


def level_blocks(level, unit):
    count = unit * (16 >> level)
    base = unit * (0, 0, 8, 12, 14)[level]
    blocks = [(0, base, count, 0), (1, base, count, 1)]
    other = []
    if level == 2:
        other.append((4, 0, 2))
    if level >= 3:
        other += [(n, (0, 2)[level - 3], m) for n, m in ((2, 2), (3, 4), (7, 6))]
    if level == 4:
        other += [(5, 0, 8), (6, 0, 12), (8, 0, 10), (9, 0, 14)]
    for source, low, mask in other:
        blocks += [(source, low * unit, count, mask), (source + 8, low * unit, count, mask + 1)]
    return blocks


def key_table(unit, levels):
    position = lax.axis_index("seq")
    rows = []
    for level in range(1, levels):
        columns = []
        for _, _, count, mask in level_blocks(level, unit):
            if mask == 0:
                columns.append(jnp.arange(count, dtype=jnp.int32))
            else:
                top = 1 << (mask.bit_length() - 1)
                columns.append(jnp.full((count,), jnp.where((position & top) != 0, -1, FAR), jnp.int32))
        rows.append(jnp.concatenate(columns))
    return jnp.stack(rows)


TILE = 256
NT = (((1,), (1,)), ((), ()))


def local_kernel(q_ref, k_ref, v_ref, m_ref, l_ref, a_ref, v_s):
    tokens = q_ref.shape[0]
    v_s[:, :128] = v_ref[...]
    v_s[:, 128:] = jnp.ones((tokens, 128), BF16)
    lower = lax.broadcasted_iota(jnp.int32, (TILE, TILE), 0) >= lax.broadcasted_iota(
        jnp.int32, (TILE, TILE), 1
    )
    for number in range(tokens // TILE):
        low, high = number * TILE, number * TILE + TILE
        query = q_ref[low:high, :]
        own = lax.dot_general(query, k_ref[low:high, :], NT, preferred_element_type=F32)
        scores = jnp.where(lower, own, LOW)
        if number:
            before = lax.dot_general(query, k_ref[:low, :], NT, preferred_element_type=F32)
            scores = jnp.concatenate([before, scores], 1)
        top = jnp.max(scores, 1, keepdims=True)
        probs = jnp.exp2(scores - top).astype(BF16)
        both = jnp.dot(probs, v_s[:high, :], preferred_element_type=F32)
        m_ref[low:high, :] = jnp.broadcast_to(top, (TILE, 128))
        a_ref[low:high, :] = both[:, :128]
        l_ref[low:high, :] = both[:, 128:]


def attend_local(q, k, v):
    tokens, width = q.shape
    block = pl.BlockSpec((tokens, 128), lambda h: (0, h))
    return pl.pallas_call(
        local_kernel,
        grid=(width // 128,),
        in_specs=[block] * 3,
        out_specs=[block] * 3,
        scratch_shapes=[pltpu.VMEM((tokens, 256), BF16)],
        out_shape=[jax.ShapeDtypeStruct((tokens, width), F32)] * 3,
        compiler_params=pltpu.CompilerParams(vmem_limit_bytes=VMEM_LIMIT),
        cost_estimate=cost(9),
        name="attend_local",
    )(q, k, v)


def attend_kernel(levels, head_base, *refs):
    offset_ref, q_ref, m_ref, l_ref, a_ref = refs[:5]
    k_group, v_group = refs[5:23], refs[23:41]
    table_ref, out_ref, q_f, k_s, v_s, m_s, l_s, a_s = refs[41:]
    head = head_base + pl.program_id(0)
    tokens = q_f.shape[0]
    unit = k_group[0].shape[0] // 15
    q_f[...] = q_ref[...].astype(F32)
    m_s[...] = m_ref[...]
    l_s[...] = l_ref[...]
    a_s[...] = a_ref[...]
    v_s[:, 128:] = jnp.ones((tokens, 128), BF16)

    for level in range(1, levels):
        dilation = 2**level
        picked = tokens // dilation
        start = offset_ref[level, head]
        row = 0
        for source, low, count, _ in level_blocks(level, unit):
            k_s[row : row + count, :] = k_group[source][low : low + count, :]
            v_s[row : row + count, :128] = v_group[source][low : low + count, :]
            row += count
        order = table_ref[level - 1 : level, :]
        size = min(TILE, picked)
        for number in range(picked // size):
            rows = pl.ds(start + number * size * dilation, size, stride=dilation)
            query = q_f[rows, :].astype(BF16)
            scores = lax.dot_general(query, k_s[...], NT, preferred_element_type=F32)
            at = lax.broadcasted_iota(jnp.int32, (size, tokens), 0) + number * size
            scores = jnp.where(order <= at, scores, LOW)
            m_old = m_s[rows, :]
            top = jnp.maximum(m_old[:, :1], jnp.max(scores, 1, keepdims=True))
            probs = jnp.exp2(scores - top).astype(BF16)
            both = jnp.dot(probs, v_s[...], preferred_element_type=F32)
            factor = jnp.exp2(m_old - top)
            m_s[rows, :] = jnp.broadcast_to(top, (size, 128))
            a_s[rows, :] = factor * a_s[rows, :] + both[:, :128]
            l_s[rows, :] = factor * l_s[rows, :] + both[:, 128:]

    out_ref[...] = (a_s[...] / l_s[...]).astype(BF16)


def attend(q, state, exchanged, table, offsets, head_base):
    levels, heads = offsets.shape
    tokens = q.shape[0]
    half = heads // 2
    mine = pl.BlockSpec((tokens, 128), lambda h, offset: (0, h + head_base))

    def group_spec(array, shift):
        return pl.BlockSpec((array.shape[0], 128), lambda h, offset: (0, h + shift))

    return pl.pallas_call(
        functools.partial(attend_kernel, levels, head_base),
        grid_spec=pltpu.PrefetchScalarGridSpec(
            num_scalar_prefetch=1,
            grid=(half,),
            in_specs=[mine] * 4
            + [group_spec(a, head_base) for a in exchanged]
            + [group_spec(a, heads + head_base) for a in exchanged]
            + [whole_spec(table)],
            out_specs=pl.BlockSpec((tokens, 128), lambda h, offset: (0, h)),
            scratch_shapes=[
                pltpu.VMEM((tokens, 128), F32),
                pltpu.VMEM((tokens, 128), BF16),
                pltpu.VMEM((tokens, 256), BF16),
                pltpu.VMEM((tokens, 128), F32),
                pltpu.VMEM((tokens, 128), F32),
                pltpu.VMEM((tokens, 128), F32),
            ],
        ),
        out_shape=jax.ShapeDtypeStruct((tokens, 128 * half), BF16),
        compiler_params=pltpu.CompilerParams(vmem_limit_bytes=VMEM_LIMIT),
        cost_estimate=cost(CA),
        name="attend",
    )(offsets, q, *state, *exchanged, *exchanged, table)


def output_kernel(where, n_arrays, share, *refs):
    owner_ref, refs = refs[0], refs[1:]
    arrays, refs = refs[:n_arrays], refs[n_arrays:]
    base_ref, w_ref, out_ref, x_s, w_s, piece_sems, w_sems = refs
    copies = copy_pieces(where, owner_ref, arrays, x_s, piece_sems, True)
    for i in range(w_s.shape[1]):
        copies.append(pltpu.make_async_copy(w_ref.at[share + i], w_s.at[:, i], w_sems.at[i]))
        copies[-1].start()
    for copy in copies:
        copy.wait()
    tile = 512
    rows, depth = x_s.shape

    @pl.loop(0, rows // tile)
    def _(n):
        at = pl.ds(pl.multiple_of(n * tile, tile), tile)
        weight = w_s[...].reshape(depth, out_ref.shape[1])
        total = jnp.dot(x_s[at, :], weight, preferred_element_type=F32)
        out_ref[at, :] = (base_ref[at, :].astype(F32) + total).astype(out_ref.dtype)


def output(pieces, base, w_columns, share, dtype, us):
    operands, where = split_pieces(pieces)
    rows, width = base.shape
    shares = w_columns.shape[0] // 2
    depth = w_columns.size // width // 2
    anywhere = pl.BlockSpec(memory_space=pl.ANY)
    vector = pl.BlockSpec(memory_space=pltpu.VMEM)
    return pl.pallas_call(
        functools.partial(output_kernel, where, len(operands), share),
        in_specs=[pl.BlockSpec(memory_space=pltpu.SMEM)]
        + [anywhere] * len(operands)
        + [vector, anywhere],
        out_specs=vector,
        scratch_shapes=[
            pltpu.VMEM((rows, depth), BF16),
            pltpu.VMEM((w_columns.shape[1], shares) + w_columns.shape[2:], BF16),
            pltpu.SemaphoreType.DMA((8,)),
            pltpu.SemaphoreType.DMA((shares,)),
        ],
        out_shape=jax.ShapeDtypeStruct((rows, width), dtype),
        compiler_params=pltpu.CompilerParams(vmem_limit_bytes=VMEM_LIMIT),
        cost_estimate=cost(us),
        name="output",
    )(piece_owners(pieces), *operands, base, w_columns)


def column_shares(w_out):
    seq = lax.axis_index("seq")
    share = seq // 4 * 2 + seq % 2
    rows = w_out.shape[0] // 8
    part = lax.dynamic_slice_in_dim(w_out, share * rows, rows, 0)
    width = w_out.shape[1] // 8
    cut = part.reshape(rows, 8, width).transpose(1, 0, 2)
    return lax.all_to_all(cut, "tp", 0, 0, tiled=True)


def gather_shares(mine):
    groups = [[y * 4 + x_lo * 2 + core for y in range(4) for core in range(2)] for x_lo in range(2)]
    return lax.all_gather(mine, "seq", axis=0, axis_index_groups=groups)


def after(value, *others):
    return lax.optimization_barrier((value, *others))[0]


def on_device(tokens, norm_gain, w_query, w_key, w_value, w_out, offsets):
    rows = tokens.shape[0]
    levels, heads = offsets.shape
    low = rows // 4
    weights = (w_key, w_value, w_query)

    mine = column_shares(w_out)
    t0, t1 = tokens[:low], after(tokens[low:], mine)
    below0, above0 = z_shift(t0, 1), z_shift(t0, -1)
    other0, other1 = x_swap(t0), x_swap(t1)
    far0 = z_shift(below0, 1)
    pair1 = jnp.stack([t1, after(other1, below0, above0)])
    below1, above1 = z_shift(pair1, 1), z_shift(pair1, -1)
    others0 = x_swap(jnp.stack([below0, above0, far0]))
    first = z_first_pieces(t0, below0, above0, far0, other0, others0)
    old = project(first, 0, rows, [], [], True, norm_gain, weights, offsets, C0)
    w_columns = gather_shares(after(mine, far0))
    if F1:
        below1 = after(below1, old[1])
    far1 = z_shift(below1[0], 1), z_shift(above1[1], -1)
    second = x_first_pieces(pair1, below1, above1, *far1)
    sums = project(second[:6], low, rows, [], [], False, norm_gain, weights, offsets, C1)
    old = project(second[6:], low, rows, sums, old, True, norm_gain, weights, offsets, C2)
    k, v, q = old[:3]
    exchanged = first_exchange(*old[3:])
    state = attend_local(q, k, v)
    exchanged = second_exchange(*exchanged, state[0])
    table = key_table(rows // 16, levels)
    gathered = []
    att_a = attend(q, state, exchanged, table, offsets, 0)
    below_a, above_a, other_a = z_shift(att_a, 1), z_shift(att_a, -1), x_swap(att_a)
    if F5:
        q = after(q, att_a)
    if F6:
        q = after(q, below_a)
    att_b = attend(q, state, exchanged, table, offsets, heads // 2)
    far_a = z_shift(below_a, 1)
    other_b = x_swap(att_b)
    if F3:
        other_b = after(other_b, below_a, above_a)
    if F4:
        below_a = after(below_a, other_a)
    pair_b = jnp.stack([att_b, other_b])
    if F8:
        others_a = x_swap(jnp.stack([below_a, above_a]))
        if F9:
            far_a = after(far_a, others_a)
        other_far_a = x_swap(far_a)
    else:
        others_a, other_far_a = x_swap(jnp.stack([below_a, above_a, far_a])), None
    below_b, above_b = z_shift(pair_b, 1), z_shift(pair_b, -1)
    far_b = z_shift(below_b[0], 1), z_shift(above_b[1], -1)
    gathered = [
        z_first_pieces(att_a, below_a, above_a, far_a, other_a, others_a, other_far_a),
        x_first_pieces(pair_b, below_b, above_b, *far_b),
    ]
    if F7:
        total = output(gathered[0], tokens, w_columns, 0, F32, 8)
        return output(gathered[1], total, w_columns, 4, BF16, CO)
    total = output(gathered[1], tokens, w_columns, 4, F32, 8)
    return output(gathered[0], total, w_columns, 0, BF16, CO)


def solution(mesh):
    placed = (
        P("seq", "tp"),
        P(),
        P(None, "tp"),
        P(None, "tp"),
        P(None, "tp"),
        P("tp", None),
        P(None, "tp"),
    )
    return jax.shard_map(
        on_device, mesh=mesh, in_specs=placed, out_specs=P("seq", "tp"), check_vma=False
    )
```

time: 275 us -> 262 us (0.953)
  waiting for transfers between devices: 95.1 us -> 102 us
  local copies, waits for them, and re-layouts: 19.8 us -> 13.3 us
  Pallas kernels: 86.8 us -> 80.9 us
  starting transfers between devices: 53 us -> 48.3 us
  other arithmetic: 6 us -> 2.67 us
    ppermute x18 -> x14, waiting for transfers between devices: 56 us -> 32.2 us  [z_shift(): return lax.ppermute(value, 'tp', pairs)]
    ppermute x7 -> x6, waiting for transfers between devices: 31 us -> 43.1 us  [x_swap(): return lax.ppermute(value, 'tp', [(t, t ^ 1) for t in range(8)])]
    all_to_all x1, waiting for transfers between devices: 0.01 us -> 9.45 us  [column_shares(): return lax.all_to_all(cut, 'tp', 0, 0, tiled=True)]
    ppermute x10 -> x17, waiting for transfers between devices: 8.11 us -> 17.4 us  [seq_swap(): return lax.ppermute(value, 'seq', [(s, s ^ mask) for s in range(16)])]
    ppermute x18 -> x14, starting transfers between devices: 26.5 us -> 17.8 us  [z_shift(): return lax.ppermute(value, 'tp', pairs)]
    pallas_call x6 -> x5, Pallas kernels: 59.2 us -> 53.6 us  [the longest x3 37.7 us: project(): pl.pallas_call(functools.partial(project_kernel, where, len(operands), fi...]
    unnamed x56 -> x65, local copies, waits for them, and re-layouts: 8.33 us -> 4.3 us
    another operation x5, other arithmetic: 5.36 us -> 2.04 us  [the longest x1 0.97 us: on_device(): others0 = x_swap(jnp.stack([below0, above0, far0]))]
  transfers between devices with their start and end apart: 37 -> 39, of which waited for: 14 -> 17; matrix products, arithmetic and copies ran while one was open for 8% -> 4% of each run, Pallas kernels for 29% -> 28%
where the time goes in v2:
time: 262 us; the launch traced here: 261 us
  waiting for transfers between devices  102 us (39%)
  Pallas kernels  80.9 us (31%)
  starting transfers between devices  48.3 us (18%)
  between operations  14 us (5%)
  local copies, waits for them, and re-layouts  13.3 us (5%)
  other arithmetic  2.67 us (1%)
    ppermute x6, waiting for transfers between devices, x_swap(): return lax.ppermute(value, 'tp', [(t, t ^ 1) for t in range(8)])  43.1 us
    pallas_call x3, Pallas kernels, project(): pl.pallas_call(functools.partial(project_kernel, where, len(operands), fi...  37.7 us
    ppermute x14, waiting for transfers between devices, z_shift(): return lax.ppermute(value, 'tp', pairs)  32.2 us
    pallas_call x2, Pallas kernels, attend(): pl.pallas_call(functools.partial(attend_kernel, levels, head_base), grid_...  18 us
    ppermute x14, starting transfers between devices, z_shift(): return lax.ppermute(value, 'tp', pairs)  17.8 us
    ppermute x17, waiting for transfers between devices, seq_swap(): return lax.ppermute(value, 'seq', [(s, s ^ mask) for s in range(16)])  17.4 us
    pallas_call x2, Pallas kernels, output(): pl.pallas_call(functools.partial(output_kernel, where, len(operands), sha...  15.9 us
    ppermute x6, starting transfers between devices, x_swap(): return lax.ppermute(value, 'tp', [(t, t ^ 1) for t in range(8)])  12.1 us
  transfers between devices with their start and end apart: 39, of which 17 were waited for; matrix products, arithmetic and copies ran while one was open for 4% of the time, Pallas kernels for 28%

profile of v2, /device:TPU:0, one launch (start us, length us, event | category | flops | bytes accessed | tf_op | source)
XLA Modules:
  0.0 261.3 jit_solution(17199401393172820886)
XLA Ops:
  6.5 1.1 constant_dynamic-slice_fusion
  7.8 0.9 copy.32
  8.8 7.9 %all-to-all-start = ((bf16[8,64,512]{2,1,0:T(8,128)(2,1)}), bf16[8,64,512]{2,1,0:T(8,128)(2,1)S(1)}, u32[]{:S(2)}, u32[]{:S(2)}) async-start(bf16[8,64,512]{2,1,0:T(8,128)(2,1)} %copy.32), calls=%async_computation | async-start | bytes 1048576 | tf_op jit(solution)/shard_map/all_to_all | solution.py:552
  16.7 2.0 collective-permute-start.1
  18.8 9.5 %all-to-all-done = bf16[8,64,512]{2,1,0:T(8,128)(2,1)S(1)} async-done(((bf16[8,64,512]{2,1,0:T(8,128)(2,1)}), bf16[8,64,512]{2,1,0:T(8,128)(2,1)S(1)}, u32[]{:S(2)}, u32[]{:S(2)}) %all-to-all-start) | async-done | bytes 524320 | tf_op jit(solution)/shard_map/all_to_all | solution.py:552
  28.3 1.7 collective-permute-start
  30.2 1.2 collective-permute-done.1.refs_3_
  31.9 4.3 %collective-permute-done.2.refs_4_ = bf16[256,512]{1,0:T(8,128)(2,1)S(1)} collective-permute-done((bf16[256,512]{1,0:T(8,128)(2,1)S(1)}, bf16[256,512]{1,0:T(8,128)(2,1)S(1)}, u32[]{:S(2)}, u32[]{:S(2)}) %collective-permute-start.2) | collective-permute-done | bytes 262176 | tf_op jit(solution)/shard_map/ppermute | solution.py:39
  36.3 3.5 %collective-permute-done.7.refs_5_ = bf16[256,512]{1,0:T(8,128)(2,1)S(1)} collective-permute-done((bf16[256,512]{1,0:T(8,128)(2,1)S(1)}, bf16[256,512]{1,0:T(8,128)(2,1)S(1)}, u32[]{:S(2)}, u32[]{:S(2)}) %collective-permute-start.7) | collective-permute-done | bytes 262176 | tf_op jit(solution)/shard_map/ppermute | solution.py:39
  39.8 1.0 pad_maximum_fusion.3
  40.8 3.3 %collective-permute-start.9 = (bf16[3,256,512]{2,1,0:T(8,128)(2,1)}, bf16[3,256,512]{2,1,0:T(8,128)(2,1)}, u32[]{:S(2)}, u32[]{:S(2)}) collective-permute-start(bf16[3,256,512]{2,1,0:T(8,128)(2,1)} %pad_maximum_fusion.3), channel_id=1, source_target_pairs={{0,1},{1,0},{2,3},{3,2},{4,5},{5,4},{6,7},{7,6},{8,9},{9,8},{10,11... | collective-permute-start | bytes 2359304 | tf_op jit(solution)/shard_map/ppermute | solution.py:43
  44.0 6.2 %collective-permute-done = bf16[768,512]{1,0:T(8,128)(2,1)S(1)} collective-permute-done((bf16[768,512]{1,0:T(8,128)(2,1)S(1)}, bf16[768,512]{1,0:T(8,128)(2,1)S(1)}, u32[]{:S(2)}, u32[]{:S(2)}) %collective-permute-start) | collective-permute-done | bytes 786464 | tf_op jit(solution)/shard_map/ppermute | solution.py:43
  50.5 1.3 collective-permute-start.8
  51.9 1.9 collective-permute-start.5
  57.0 13.3 %collective-permute-done.8.refs_6_ = bf16[256,512]{1,0:T(8,128)(2,1)} collective-permute-done((bf16[256,512]{1,0:T(8,128)(2,1)S(1)}, bf16[256,512]{1,0:T(8,128)(2,1)}, u32[]{:S(2)}, u32[]{:S(2)}) %collective-permute-start.8) | collective-permute-done | bytes 262176 | tf_op jit(solution)/shard_map/ppermute | solution.py:43
  70.4 11.4 %project.4 = (bf16[1024,512]{1,0:T(8,128)(2,1)}, bf16[1024,512]{1,0:T(8,128)(2,1)}, bf16[1024,512]{1,0:T(8,128)(2,1)}, bf16[960,1024]{1,0:T(8,128)(2,1)}, bf16[2...) custom-call(s32[8]{0:T(128)} %stack.132.refs_0_, s32[5,4]{1,0:T(8,128)} %copy.37.refs_1_.refs_0_, ...), custom_call_target="tpu_custom_call" | custom-call | flops 12000000000 | bytes 1024 | tf_op jit(solution)/shard_map/project/pallas_call | solution.py:290
  81.8 1.6 collective-permute-done.3.refs_3_
  83.3 1.2 slice_bitcast_fusion.1
  84.7 3.3 %collective-permute-start.6 = (bf16[768,512]{1,0:T(8,128)(2,1)S(1)}, bf16[768,512]{1,0:T(8,128)(2,1)S(1)}, u32[]{:S(2)}, u32[]{:S(2)}) collective-permute-start(bf16[768,512]{1,0:T(8,128)(2,1)S(1)} %slice_bitcast_fusion), channel_id=1, source_target_pairs={{0,6},{1,7},{2,0},{3,1},{4,2},{5,3},{6,4},{7,5},{8,14},{9,15},{10,... | collective-permute-start | bytes 2359304 | tf_op jit(solution)/shard_map/ppermute | solution.py:39
  88.0 16.2 %project.3 = (f32[3,768,512]{2,1,0:T(8,128)}, f32[768,128]{1,0:T(8,128)}) custom-call(s32[6]{0:T(128)} %stack.131.refs_0_, s32[5,4]{1,0:T(8,128)} %copy.37.refs_1_.refs_0_, bf16[2,768,512]{2,1,0:T(8,128)(2,1)} %copy-done.1, bf16[2,768,512]{2,1,0:T(8,128)(2,1)} %collective-permute-done.3.refs_3_, bf16[2,768,512]{2,1,0:T(8,128)(2,1)} %copy-done.8, ...), custom_call_target="tpu_custom_call" | custom-call | flops 20000000000 | bytes 1024 | tf_op jit(solution)/shard_map/project/pallas_call | solution.py:290
  104.3 0.9 copy-done.17
  105.4 10.2 %project.5 = (bf16[1024,512]{1,0:T(8,128)(2,1)}, bf16[1024,512]{1,0:T(8,128)(2,1)}, bf16[1024,512]{1,0:T(8,128)(2,1)}, bf16[960,1024]{1,0:T(8,128)(2,1)}, bf16[2...) custom-call(s32[2]{0:T(128)} %pad_add_fusion.2.refs_0_, ...), custom_call_target="tpu_custom_call", output_to_operand_aliasing={{0}: (10, {}), {1}: (11, {}), {2}: (12, {}), {3}: (13, {}),... | custom-call | flops 8000000000 | bytes 1024 | tf_op jit(solution)/shard_map/project/pallas_call | solution.py:290
  115.5 0.8 collective-permute-start.11
  116.4 1.6 collective-permute-start.12
  117.9 1.4 collective-permute-start.13
  119.4 2.9 %collective-permute-start.14 = (bf16[64,1024]{1,0:T(8,128)(2,1)}, bf16[64,1024]{1,0:T(8,128)(2,1)S(1)}, u32[]{:S(2)}, u32[]{:S(2)}) collective-permute-start(bf16[64,1024]{1,0:T(8,128)(2,1)} %get-tuple-element.58), channel_id=1, source_target_pairs={{0,64},{8,72},{16,80},{24,88},{32,96},{40,104},{48,112},{56,120},{... | collective-permute-start | bytes 393224 | tf_op jit(solution)/shard_map/ppermute | solution.py:47
  122.3 9.3 %attend_local.1 = (f32[1024,512]{1,0:T(8,128)}, f32[1024,512]{1,0:T(8,128)}, f32[1024,512]{1,0:T(8,128)}) custom-call(bf16[1024,512]{1,0:T(8,128)(2,1)} %get-tuple-element.61.q_ref.refs_1_, bf16[1024,512]{1,0:T(8,128)(2,1)} %get-tuple-element.47.k_ref, bf16[1024,512]{1,0:T(8,128)(2,1)} %get-tuple-element.48.v_ref), custom_call_target="tpu_custom_call" | custom-call | flops 8999999488 | bytes 1024 | tf_op jit(solution)/shard_map/attend_local/pallas_call | solution.py:408
  132.4 6.1 %collective-permute-done.15.refs_11_.refs_29_ = bf16[64,1024]{1,0:T(8,128)(2,1)} collective-permute-done((bf16[64,1024]{1,0:T(8,128)(2,1)}, bf16[64,1024]{1,0:T(8,128)(2,1)}, u32[]{:S(2)}, u32[]{:S(2)}) %collective-permute-start.15) | collective-permute-done | bytes 131104 | tf_op jit(solution)/shard_map/ppermute | solution.py:47
  138.5 1.6 collective-permute-start.18
  140.3 8.6 %collective-permute-done.17.refs_13_.refs_31_ = bf16[64,1024]{1,0:T(8,128)(2,1)} collective-permute-done((bf16[64,1024]{1,0:T(8,128)(2,1)S(1)}, bf16[64,1024]{1,0:T(8,128)(2,1)}, u32[]{:S(2)}, u32[]{:S(2)}) %collective-permute-start.17) | collective-permute-done | bytes 131104 | tf_op jit(solution)/shard_map/ppermute | solution.py:47
  149.6 0.9 collective-permute-done.25.refs_21_.refs_39_
  152.3 1.1 collective-permute-done.20.refs_16_.refs_34_
  155.1 8.9 %attend.2.refs_1_ = bf16[1024,256]{1,0:T(8,128)(2,1)} custom-call(s32[5,4]{1,0:T(8,128)} %copy.37.refs_1_.refs_0_, bf16[1024,512]{1,0:T(8,128)(2,1)} %get-tuple-element.61.q_ref.refs_1_, f32[1024,512]{1,0:T(8,128)} %get-tuple-element.49.refs_2_, f32[1024,512]{1,0:T(8,128)} %get-tuple-element.50.refs_3_, f32[1024,512]{1,0:T(8,128)} %get-tuple-element.51.refs_4_, ...), custom_call_target="tpu_custom_call" | custom-call | flops 8999999488 | bytes 1024 | tf_op jit(solution)/shard_map/attend/pallas_call | solution.py:472
  164.0 9.1 %attend.3 = bf16[1024,256]{1,0:T(8,128)(2,1)} custom-call(s32[5,4]{1,0:T(8,128)} %copy.37.refs_1_.refs_0_, bf16[1024,512]{1,0:T(8,128)(2,1)} %get-tuple-element.61.q_ref.refs_1_, f32[1024,512]{1,0:T(8,128)} %get-tuple-element.49.refs_2_, f32[1024,512]{1,0:T(8,128)} %get-tuple-element.50.refs_3_, f32[1024,512]{1,0:T(8,128)} %get-tuple-element.51.refs_4_, ...), custom_call_target="tpu_custom_call" | custom-call | flops 8999999488 | bytes 1024 | tf_op jit(solution)/shard_map/attend/pallas_call | solution.py:472
  173.2 2.2 collective-permute-start.27
  175.3 3.0 %collective-permute-start.29 = (bf16[1024,256]{1,0:T(8,128)(2,1)S(1)}, bf16[1024,256]{1,0:T(8,128)(2,1)S(1)}, u32[]{:S(2)}, u32[]{:S(2)}) collective-permute-start(bf16[1024,256]{1,0:T(8,128)(2,1)S(1)} %copy-done.20), channel_id=1, source_target_pairs={{0,6},{1,7},{2,0},{3,1},{4,2},{5,3},{6,4},{7,5},{8,14},{9,15},{10,... | collective-permute-start | bytes 1572872 | tf_op jit(solution)/shard_map/ppermute | solution.py:39
  178.3 1.5 collective-permute-start.34
  179.8 9.9 %collective-permute-done.27 = bf16[1024,256]{1,0:T(8,128)(2,1)S(1)} collective-permute-done((bf16[1024,256]{1,0:T(8,128)(2,1)}, bf16[1024,256]{1,0:T(8,128)(2,1)S(1)}, u32[]{:S(2)}, u32[]{:S(2)}) %collective-permute-start.27) | collective-permute-done | bytes 524320 | tf_op jit(solution)/shard_map/ppermute | solution.py:43
  189.7 10.4 %collective-permute-done.34.refs_5_ = bf16[1024,256]{1,0:T(8,128)(2,1)S(1)} collective-permute-done((bf16[1024,256]{1,0:T(8,128)(2,1)S(1)}, bf16[1024,256]{1,0:T(8,128)(2,1)S(1)}, u32[]{:S(2)}, u32[]{:S(2)}) %collective-permute-start.34) | collective-permute-done | bytes 524320 | tf_op jit(solution)/shard_map/ppermute | solution.py:43
  201.2 2.2 collective-permute-start.36
  203.6 3.2 %collective-permute-start.31 = (bf16[2,1024,256]{2,1,0:T(8,128)(2,1)S(1)}, bf16[2,1024,256]{2,1,0:T(8,128)(2,1)}, u32[]{:S(2)}, u32[]{:S(2)}) collective-permute-start(bf16[2,1024,256]{2,1,0:T(8,128)(2,1)S(1)} %pad_maximum_fusion.2.refs_1_), channel_id=1, source_target_pairs={{0,6},{1,7},{2,0},{3,1},{4,2},{5,3},{6,4},{7,5},{8,14},{9,15},{10,... | collective-permute-start | bytes 3145736 | tf_op jit(solution)/shard_map/ppermute | solution.py:39
  207.4 21.6 %collective-permute-done.30.refs_2_ = bf16[2,1024,256]{2,1,0:T(8,128)(2,1)} collective-permute-done((bf16[2,1024,256]{2,1,0:T(8,128)(2,1)S(1)}, bf16[2,1024,256]{2,1,0:T(8,128)(2,1)}, u32[]{:S(2)}, u32[]{:S(2)}) %collective-permute-start.30) | collective-permute-done | bytes 1048608 | tf_op jit(solution)/shard_map/ppermute | solution.py:39
  229.0 1.1 slice_bitcast_fusion.3
  230.2 1.9 slice_bitcast_fusion.2
  232.0 3.2 %collective-permute-start.33 = (bf16[1024,256]{1,0:T(8,128)(2,1)}, bf16[1024,256]{1,0:T(8,128)(2,1)}, u32[]{:S(2)}, u32[]{:S(2)}) collective-permute-start(bf16[1024,256]{1,0:T(8,128)(2,1)} %slice_bitcast_fusion.2), channel_id=1, source_target_pairs={{0,6},{1,7},{2,0},{3,1},{4,2},{5,3},{6,4},{7,5},{8,14},{9,15},{10,... | collective-permute-start | bytes 1572872 | tf_op jit(solution)/shard_map/ppermute | solution.py:39
  235.2 3.3 %collective-permute-done.36.refs_6_ = bf16[3,1024,256]{2,1,0:T(8,128)(2,1)} collective-permute-done((bf16[3,1024,256]{2,1,0:T(8,128)(2,1)S(1)}, bf16[3,1024,256]{2,1,0:T(8,128)(2,1)}, u32[]{:S(2)}, u32[]{:S(2)}) %collective-permute-start.36) | collective-permute-done | bytes 1572896 | tf_op jit(solution)/shard_map/ppermute | solution.py:43
  238.5 7.9 %output.2.refs_6_ = f32[1024,512]{1,0:T(8,128)} custom-call(s32[8]{0:T(128)} %stack.132.refs_0_, bf16[1024,256]{1,0:T(8,128)(2,1)} %attend.2.refs_1_, bf16[1024,256]{1,0:T(8,128)(2,1)} %copy-done.4, bf16[1024,256]{1,0:T(8,128)(2,1)} %copy-done.5, bf16[1024,256]{1,0:T(8,128)(2,1)} %copy-done.6, bf16[1024,256]{1,0:T(8,128)(2,1)} %copy-done.22, ...), custom_call_target="tpu_custom_call" | custom-call | flops 8000000000 | bytes 1024 | tf_op jit(solution)/shard_map/output/pallas_call | solution.py:526
  246.5 8.0 %output.3 = bf16[1024,512]{1,0:T(8,128)(2,1)} custom-call(s32[8]{0:T(128)} %stack.126.refs_0_, bf16[2,1024,256]{2,1,0:T(8,128)(2,1)} %copy-done.3, bf16[2,1024,256]{2,1,0:T(8,128)(2,1)} %collective-permute-done.30.refs_2_, bf16[2,1024,256]{2,1,0:T(8,128)(2,1)} %collective-permute-done.31.refs_3_, bf16[1024,256]{1,0:T(8,128)(2,1)} %collective-permute-done.32.refs_4_, ...), custom_call_target="tpu_custom_call" | custom-call | flops 30000001024 | bytes 1024 | tf_op jit(solution)/shard_map/output/pallas_call | solution.py:526
  (137 shorter events, 11.9 us)
Async XLA Ops:
  8.8 19.5 %all-to-all-start = ((bf16[8,64,512]{2,1,0:T(8,128)(2,1)}), bf16[8,64,512]{2,1,0:T(8,128)(2,1)S(1)}, u32[]{:S(2)}, u32[]{:S(2)}) async-start(bf16[8,64,512]{2,1,0:T(8,128)(2,1)} %copy.32), calls=%async_computation | async-start | bytes 1048576 | tf_op jit(solution)/shard_map/all_to_all | solution.py:552
  16.6 218.6 %all-gather.3.cloned.1.call-start = ((), (), s32[]{:S(2)}) async-start(), calls=%async_computation.1 | async-start | bytes 4718592 | tf_op jit(solution)/shard_map/all_gather | solution.py:557
  16.7 33.8 %copy-start.9 = (bf16[256,512]{1,0:T(8,128)(2,1)}, bf16[256,512]{1,0:T(8,128)(2,1)S(1)}, u32[]{:S(2)}) copy-start(bf16[256,512]{1,0:T(8,128)(2,1)S(1)} %slice.22.refs_2_) | copy-start | bytes 786436
  16.7 14.7 %collective-permute-start.1 = (bf16[256,512]{1,0:T(8,128)(2,1)S(1)}, bf16[256,512]{1,0:T(8,128)(2,1)S(1)}, u32[]{:S(2)}, u32[]{:S(2)}) collective-permute-start(bf16[256,512]{1,0:T(8,128)(2,1)S(1)} %slice.22.refs_2_), channel_id=1, source_target_pairs={{0,2},{1,3},{2,4},{3,5},{4,6},{5,7},{6,0},{7,1},{8,10},{9,11},{10,... | collective-permute-start | bytes 786440 | tf_op jit(solution)/shard_map/ppermute | solution.py:39
  28.3 22.2 %copy-start = (bf16[8,64,512]{2,1,0:T(8,128)(2,1)}, bf16[8,64,512]{2,1,0:T(8,128)(2,1)S(1)}, u32[]{:S(2)}) copy-start(bf16[8,64,512]{2,1,0:T(8,128)(2,1)S(1)} %all-to-all-done) | copy-start | bytes 1572868
  28.3 22.0 %collective-permute-start = (bf16[768,512]{1,0:T(8,128)(2,1)S(1)}, bf16[768,512]{1,0:T(8,128)(2,1)S(1)}, u32[]{:S(2)}, u32[]{:S(2)}) collective-permute-start(bf16[768,512]{1,0:T(8,128)(2,1)S(1)} %slice.21), channel_id=1, source_target_pairs={{0,1},{1,0},{2,3},{3,2},{4,5},{5,4},{6,7},{7,6},{8,9},{9,8},{10,11... | collective-permute-start | bytes 2359304 | tf_op jit(solution)/shard_map/ppermute | solution.py:43
  29.9 6.4 %collective-permute-start.2 = (bf16[256,512]{1,0:T(8,128)(2,1)S(1)}, bf16[256,512]{1,0:T(8,128)(2,1)S(1)}, u32[]{:S(2)}, u32[]{:S(2)}) collective-permute-start(bf16[256,512]{1,0:T(8,128)(2,1)S(1)} %slice.22.refs_2_), channel_id=1, source_target_pairs={{0,6},{1,7},{2,0},{3,1},{4,2},{5,3},{6,4},{7,5},{8,14},{9,15},{10,... | collective-permute-start | bytes 786440 | tf_op jit(solution)/shard_map/ppermute | solution.py:39
  31.4 19.0 %copy-start.10 = (bf16[256,512]{1,0:T(8,128)(2,1)}, bf16[256,512]{1,0:T(8,128)(2,1)S(1)}, u32[]{:S(2)}) copy-start(bf16[256,512]{1,0:T(8,128)(2,1)S(1)} %collective-permute-done.1.refs_3_) | copy-start | bytes 786436
  31.4 8.4 %collective-permute-start.7 = (bf16[256,512]{1,0:T(8,128)(2,1)S(1)}, bf16[256,512]{1,0:T(8,128)(2,1)S(1)}, u32[]{:S(2)}, u32[]{:S(2)}) collective-permute-start(bf16[256,512]{1,0:T(8,128)(2,1)S(1)} %collective-permute-done.1.refs_3_), channel_id=1, source_target_pairs={{0,2},{1,3},{2,4},{3,5},{4,6},{5,7},{6,0},{7,1},{8,10},{9,11},{10,... | collective-permute-start | bytes 786440 | tf_op jit(solution)/shard_map/ppermute | solution.py:39
  40.8 29.6 %collective-permute-start.9 = (bf16[3,256,512]{2,1,0:T(8,128)(2,1)}, bf16[3,256,512]{2,1,0:T(8,128)(2,1)}, u32[]{:S(2)}, u32[]{:S(2)}) collective-permute-start(bf16[3,256,512]{2,1,0:T(8,128)(2,1)} %pad_maximum_fusion.3), channel_id=1, source_target_pairs={{0,1},{1,0},{2,3},{3,2},{4,5},{5,4},{6,7},{7,6},{8,9},{9,8},{10,11... | collective-permute-start | bytes 2359304 | tf_op jit(solution)/shard_map/ppermute | solution.py:43
  50.4 31.3 %copy-start.1 = (bf16[2,768,512]{2,1,0:T(8,128)(2,1)}, bf16[2,768,512]{2,1,0:T(8,128)(2,1)S(1)}, u32[]{:S(2)}) copy-start(bf16[2,768,512]{2,1,0:T(8,128)(2,1)S(1)} %pad_maximum_fusion.refs_2_) | copy-start | bytes 4718596
  50.4 32.9 %collective-permute-start.3 = (bf16[2,768,512]{2,1,0:T(8,128)(2,1)S(1)}, bf16[2,768,512]{2,1,0:T(8,128)(2,1)}, u32[]{:S(2)}, u32[]{:S(2)}) collective-permute-start(bf16[2,768,512]{2,1,0:T(8,128)(2,1)S(1)} %pad_maximum_fusion.refs_2_), channel_id=1, source_target_pairs={{0,2},{1,3},{2,4},{3,5},{4,6},{5,7},{6,0},{7,1},{8,10},{9,11},{10,... | collective-permute-start | bytes 4718600 | tf_op jit(solution)/shard_map/ppermute | solution.py:39
  50.5 19.8 %collective-permute-start.8 = (bf16[256,512]{1,0:T(8,128)(2,1)S(1)}, bf16[256,512]{1,0:T(8,128)(2,1)}, u32[]{:S(2)}, u32[]{:S(2)}) collective-permute-start(bf16[256,512]{1,0:T(8,128)(2,1)S(1)} %slice.22.refs_2_), channel_id=1, source_target_pairs={{0,1},{1,0},{2,3},{3,2},{4,5},{5,4},{6,7},{7,6},{8,9},{9,8},{10,11... | collective-permute-start | bytes 786440 | tf_op jit(solution)/shard_map/ppermute | solution.py:43
  51.9 32.8 %collective-permute-start.5 = (bf16[2,768,512]{2,1,0:T(8,128)(2,1)S(1)}, bf16[2,768,512]{2,1,0:T(8,128)(2,1)S(1)}, u32[]{:S(2)}, u32[]{:S(2)}) collective-permute-start(bf16[2,768,512]{2,1,0:T(8,128)(2,1)S(1)} %pad_maximum_fusion.refs_2_), channel_id=1, source_target_pairs={{0,6},{1,7},{2,0},{3,1},{4,2},{5,3},{6,4},{7,5},{8,14},{9,15},{10,... | collective-permute-start | bytes 4718600 | tf_op jit(solution)/shard_map/ppermute | solution.py:39
  84.6 19.6 %collective-permute-start.4 = (bf16[768,512]{1,0:T(8,128)(2,1)S(1)}, bf16[768,512]{1,0:T(8,128)(2,1)S(1)}, u32[]{:S(2)}, u32[]{:S(2)}) collective-permute-start(bf16[768,512]{1,0:T(8,128)(2,1)S(1)} %slice_bitcast_fusion.1), channel_id=1, source_target_pairs={{0,2},{1,3},{2,4},{3,5},{4,6},{5,7},{6,0},{7,1},{8,10},{9,11},{10,... | collective-permute-start | bytes 2359304 | tf_op jit(solution)/shard_map/ppermute | solution.py:39
  84.7 19.5 %collective-permute-start.6 = (bf16[768,512]{1,0:T(8,128)(2,1)S(1)}, bf16[768,512]{1,0:T(8,128)(2,1)S(1)}, u32[]{:S(2)}, u32[]{:S(2)}) collective-permute-start(bf16[768,512]{1,0:T(8,128)(2,1)S(1)} %slice_bitcast_fusion), channel_id=1, source_target_pairs={{0,6},{1,7},{2,0},{3,1},{4,2},{5,3},{6,4},{7,5},{8,14},{9,15},{10,... | collective-permute-start | bytes 2359304 | tf_op jit(solution)/shard_map/ppermute | solution.py:39
  115.5 16.3 %collective-permute-start.11 = (bf16[192,1024]{1,0:T(8,128)(2,1)}, bf16[192,1024]{1,0:T(8,128)(2,1)S(1)}, u32[]{:S(2)}, u32[]{:S(2)}) collective-permute-start(bf16[192,1024]{1,0:T(8,128)(2,1)} %get-tuple-element.53), channel_id=1, source_target_pairs={{0,16},{8,24},{16,0},{24,8},{32,48},{40,56},{48,32},{56,40},{64,80... | collective-permute-start | bytes 1179656 | tf_op jit(solution)/shard_map/ppermute | solution.py:47
  116.4 15.6 %collective-permute-start.12 = (bf16[192,1024]{1,0:T(8,128)(2,1)}, bf16[192,1024]{1,0:T(8,128)(2,1)S(1)}, u32[]{:S(2)}, u32[]{:S(2)}) collective-permute-start(bf16[192,1024]{1,0:T(8,128)(2,1)} %get-tuple-element.53), channel_id=1, source_target_pairs={{0,32},{8,40},{16,48},{24,56},{32,0},{40,8},{48,16},{56,24},{64,96... | collective-permute-start | bytes 1179656 | tf_op jit(solution)/shard_map/ppermute | solution.py:47
  117.9 35.7 %collective-permute-start.10 = (bf16[960,1024]{1,0:T(8,128)(2,1)}, bf16[960,1024]{1,0:T(8,128)(2,1)S(1)}, u32[]{:S(2)}, u32[]{:S(2)}) collective-permute-start(bf16[960,1024]{1,0:T(8,128)(2,1)} %get-tuple-element.52.refs_5_.refs_23_), channel_id=1, source_target_pairs={{0,8},{8,0},{16,24},{24,16},{32,40},{40,32},{48,56},{56,48},{64,72... | collective-permute-start | bytes 5898248 | tf_op jit(solution)/shard_map/ppermute | solution.py:47
  117.9 22.2 %collective-permute-start.13 = (bf16[256,1024]{1,0:T(8,128)(2,1)}, bf16[256,1024]{1,0:T(8,128)(2,1)S(1)}, u32[]{:S(2)}, u32[]{:S(2)}) collective-permute-start(bf16[256,1024]{1,0:T(8,128)(2,1)} %get-tuple-element.56), channel_id=1, source_target_pairs={{0,16},{8,24},{16,0},{24,8},{32,48},{40,56},{48,32},{56,40},{64,80... | collective-permute-start | bytes 1572872 | tf_op jit(solution)/shard_map/ppermute | solution.py:47
  119.4 12.2 %collective-permute-start.14 = (bf16[64,1024]{1,0:T(8,128)(2,1)}, bf16[64,1024]{1,0:T(8,128)(2,1)S(1)}, u32[]{:S(2)}, u32[]{:S(2)}) collective-permute-start(bf16[64,1024]{1,0:T(8,128)(2,1)} %get-tuple-element.58), channel_id=1, source_target_pairs={{0,64},{8,72},{16,80},{24,88},{32,96},{40,104},{48,112},{56,120},{... | collective-permute-start | bytes 393224 | tf_op jit(solution)/shard_map/ppermute | solution.py:47
  131.5 22.1 %copy-start.27 = (bf16[64,1024]{1,0:T(8,128)(2,1)}, bf16[64,1024]{1,0:T(8,128)(2,1)S(1)}, u32[]{:S(2)}) copy-start(bf16[64,1024]{1,0:T(8,128)(2,1)S(1)} %collective-permute-done.14.refs_10_.refs_28_) | copy-start | bytes 393220
  131.5 7.0 %collective-permute-start.15 = (bf16[64,1024]{1,0:T(8,128)(2,1)}, bf16[64,1024]{1,0:T(8,128)(2,1)}, u32[]{:S(2)}, u32[]{:S(2)}) collective-permute-start(bf16[64,1024]{1,0:T(8,128)(2,1)} %get-tuple-element.58), channel_id=1, source_target_pairs={{0,96},{8,104},{16,112},{24,120},{32,64},{40,72},{48,80},{56,88},{... | collective-permute-start | bytes 393224 | tf_op jit(solution)/shard_map/ppermute | solution.py:47
  131.9 21.7 %copy-start.13 = (bf16[192,1024]{1,0:T(8,128)(2,1)}, bf16[192,1024]{1,0:T(8,128)(2,1)S(1)}, u32[]{:S(2)}) copy-start(bf16[192,1024]{1,0:T(8,128)(2,1)S(1)} %collective-permute-done.11.refs_7_.refs_25_) | copy-start | bytes 1179652
  131.9 6.6 %collective-permute-start.22 = (bf16[64,1024]{1,0:T(8,128)(2,1)S(1)}, bf16[64,1024]{1,0:T(8,128)(2,1)}, u32[]{:S(2)}, u32[]{:S(2)}) collective-permute-start(bf16[64,1024]{1,0:T(8,128)(2,1)S(1)} %collective-permute-done.14.refs_10_.refs_28_), channel_id=1, source_target_pairs={{0,8},{8,0},{16,24},{24,16},{32,40},{40,32},{48,56},{56,48},{64,72... | collective-permute-start | bytes 393224 | tf_op jit(solution)/shard_map/ppermute | solution.py:47
  131.9 21.7 %copy-start.23 = (bf16[192,1024]{1,0:T(8,128)(2,1)}, bf16[192,1024]{1,0:T(8,128)(2,1)S(1)}, u32[]{:S(2)}) copy-start(bf16[192,1024]{1,0:T(8,128)(2,1)S(1)} %collective-permute-done.12.refs_8_.refs_26_) | copy-start | bytes 1179652
  132.0 19.1 %collective-permute-start.16 = (bf16[192,1024]{1,0:T(8,128)(2,1)S(1)}, bf16[192,1024]{1,0:T(8,128)(2,1)}, u32[]{:S(2)}, u32[]{:S(2)}) collective-permute-start(bf16[192,1024]{1,0:T(8,128)(2,1)S(1)} %collective-permute-done.11.refs_7_.refs_25_), channel_id=1, source_target_pairs={{0,32},{8,40},{16,48},{24,56},{32,0},{40,8},{48,16},{56,24},{64,96... | collective-permute-start | bytes 1179656 | tf_op jit(solution)/shard_map/ppermute | solution.py:47
  138.5 10.4 %collective-permute-start.17 = (bf16[64,1024]{1,0:T(8,128)(2,1)S(1)}, bf16[64,1024]{1,0:T(8,128)(2,1)}, u32[]{:S(2)}, u32[]{:S(2)}) collective-permute-start(bf16[64,1024]{1,0:T(8,128)(2,1)S(1)} %slice.25), channel_id=1, source_target_pairs={{0,64},{8,72},{16,80},{24,88},{32,96},{40,104},{48,112},{56,120},{... | collective-permute-start | bytes 393224 | tf_op jit(solution)/shard_map/ppermute | solution.py:47
  138.5 10.4 %collective-permute-start.18 = (bf16[64,1024]{1,0:T(8,128)(2,1)S(1)}, bf16[64,1024]{1,0:T(8,128)(2,1)}, u32[]{:S(2)}, u32[]{:S(2)}) collective-permute-start(bf16[64,1024]{1,0:T(8,128)(2,1)S(1)} %slice.25), channel_id=1, source_target_pairs={{0,96},{8,104},{16,112},{24,120},{32,64},{40,72},{48,80},{56,88},{... | collective-permute-start | bytes 393224 | tf_op jit(solution)/shard_map/ppermute | solution.py:47
  140.1 9.4 %collective-permute-start.23 = (bf16[64,1024]{1,0:T(8,128)(2,1)}, bf16[64,1024]{1,0:T(8,128)(2,1)}, u32[]{:S(2)}, u32[]{:S(2)}) collective-permute-start(bf16[64,1024]{1,0:T(8,128)(2,1)} %collective-permute-done.15.refs_11_.refs_29_), channel_id=1, source_target_pairs={{0,8},{8,0},{16,24},{24,16},{32,40},{40,32},{48,56},{56,48},{64,72... | collective-permute-start | bytes 393224 | tf_op jit(solution)/shard_map/ppermute | solution.py:47
  148.9 1.7 collective-permute-start.25
  148.9 1.9 collective-permute-start.26
  149.5 3.9 %collective-permute-start.21 = (bf16[256,1024]{1,0:T(8,128)(2,1)S(1)}, bf16[256,1024]{1,0:T(8,128)(2,1)S(1)}, u32[]{:S(2)}, u32[]{:S(2)}) collective-permute-start(bf16[256,1024]{1,0:T(8,128)(2,1)S(1)} %collective-permute-done.13.refs_9_.refs_27_), channel_id=1, source_target_pairs={{0,8},{8,0},{16,24},{24,16},{32,40},{40,32},{48,56},{56,48},{64,72... | collective-permute-start | bytes 1572872 | tf_op jit(solution)/shard_map/ppermute | solution.py:47
  150.5 1.7 collective-permute-start.19
  150.7 2.7 %collective-permute-start.20 = (bf16[192,1024]{1,0:T(8,128)(2,1)S(1)}, bf16[192,1024]{1,0:T(8,128)(2,1)S(1)}, u32[]{:S(2)}, u32[]{:S(2)}) collective-permute-start(bf16[192,1024]{1,0:T(8,128)(2,1)S(1)} %collective-permute-done.12.refs_8_.refs_26_), channel_id=1, source_target_pairs={{0,8},{8,0},{16,24},{24,16},{32,40},{40,32},{48,56},{56,48},{64,72... | collective-permute-start | bytes 1179656 | tf_op jit(solution)/shard_map/ppermute | solution.py:47
  151.1 2.5 collective-permute-start.24
  164.0 15.9 %collective-permute-start.28 = (bf16[1024,256]{1,0:T(8,128)(2,1)}, bf16[1024,256]{1,0:T(8,128)(2,1)S(1)}, u32[]{:S(2)}, u32[]{:S(2)}) collective-permute-start(bf16[1024,256]{1,0:T(8,128)(2,1)} %attend.2.refs_1_), channel_id=1, source_target_pairs={{0,2},{1,3},{2,4},{3,5},{4,6},{5,7},{6,0},{7,1},{8,10},{9,11},{10,... | collective-permute-start | bytes 1572872 | tf_op jit(solution)/shard_map/ppermute | solution.py:39
  173.2 16.6 %collective-permute-start.27 = (bf16[1024,256]{1,0:T(8,128)(2,1)}, bf16[1024,256]{1,0:T(8,128)(2,1)S(1)}, u32[]{:S(2)}, u32[]{:S(2)}) collective-permute-start(bf16[1024,256]{1,0:T(8,128)(2,1)} %attend.3), channel_id=1, source_target_pairs={{0,1},{1,0},{2,3},{3,2},{4,5},{5,4},{6,7},{7,6},{8,9},{9,8},{10,11... | collective-permute-start | bytes 1572872 | tf_op jit(solution)/shard_map/ppermute | solution.py:43
  175.3 14.4 %collective-permute-start.29 = (bf16[1024,256]{1,0:T(8,128)(2,1)S(1)}, bf16[1024,256]{1,0:T(8,128)(2,1)S(1)}, u32[]{:S(2)}, u32[]{:S(2)}) collective-permute-start(bf16[1024,256]{1,0:T(8,128)(2,1)S(1)} %copy-done.20), channel_id=1, source_target_pairs={{0,6},{1,7},{2,0},{3,1},{4,2},{5,3},{6,4},{7,5},{8,14},{9,15},{10,... | collective-permute-start | bytes 1572872 | tf_op jit(solution)/shard_map/ppermute | solution.py:39
  178.3 21.8 %collective-permute-start.34 = (bf16[1024,256]{1,0:T(8,128)(2,1)S(1)}, bf16[1024,256]{1,0:T(8,128)(2,1)S(1)}, u32[]{:S(2)}, u32[]{:S(2)}) collective-permute-start(bf16[1024,256]{1,0:T(8,128)(2,1)S(1)} %copy-done.20), channel_id=1, source_target_pairs={{0,1},{1,0},{2,3},{3,2},{4,5},{5,4},{6,7},{7,6},{8,9},{9,8},{10,11... | collective-permute-start | bytes 1572872 | tf_op jit(solution)/shard_map/ppermute | solution.py:43
  179.8 21.3 %copy-start.4 = (bf16[1024,256]{1,0:T(8,128)(2,1)}, bf16[1024,256]{1,0:T(8,128)(2,1)S(1)}, u32[]{:S(2)}) copy-start(bf16[1024,256]{1,0:T(8,128)(2,1)S(1)} %collective-permute-done.28.refs_2_) | copy-start | bytes 1572868
  179.8 20.4 %collective-permute-start.35 = (bf16[1024,256]{1,0:T(8,128)(2,1)S(1)}, bf16[1024,256]{1,0:T(8,128)(2,1)S(1)}, u32[]{:S(2)}, u32[]{:S(2)}) collective-permute-start(bf16[1024,256]{1,0:T(8,128)(2,1)S(1)} %collective-permute-done.28.refs_2_), channel_id=1, source_target_pairs={{0,2},{1,3},{2,4},{3,5},{4,6},{5,7},{6,0},{7,1},{8,10},{9,11},{10,... | collective-permute-start | bytes 1572872 | tf_op jit(solution)/shard_map/ppermute | solution.py:39
  201.2 37.3 %collective-permute-start.36 = (bf16[3,1024,256]{2,1,0:T(8,128)(2,1)S(1)}, bf16[3,1024,256]{2,1,0:T(8,128)(2,1)}, u32[]{:S(2)}, u32[]{:S(2)}) collective-permute-start(bf16[3,1024,256]{2,1,0:T(8,128)(2,1)S(1)} %pad_maximum_fusion.1), channel_id=1, source_target_pairs={{0,1},{1,0},{2,3},{3,2},{4,5},{5,4},{6,7},{7,6},{8,9},{9,8},{10,11... | collective-permute-start | bytes 4718600 | tf_op jit(solution)/shard_map/ppermute | solution.py:43
  203.5 43.0 %copy-start.3 = (bf16[2,1024,256]{2,1,0:T(8,128)(2,1)}, bf16[2,1024,256]{2,1,0:T(8,128)(2,1)S(1)}, u32[]{:S(2)}) copy-start(bf16[2,1024,256]{2,1,0:T(8,128)(2,1)S(1)} %pad_maximum_fusion.2.refs_1_) | copy-start | bytes 3145732
  203.5 25.5 %collective-permute-start.30 = (bf16[2,1024,256]{2,1,0:T(8,128)(2,1)S(1)}, bf16[2,1024,256]{2,1,0:T(8,128)(2,1)}, u32[]{:S(2)}, u32[]{:S(2)}) collective-permute-start(bf16[2,1024,256]{2,1,0:T(8,128)(2,1)S(1)} %pad_maximum_fusion.2.refs_1_), channel_id=1, source_target_pairs={{0,2},{1,3},{2,4},{3,5},{4,6},{5,7},{6,0},{7,1},{8,10},{9,11},{10,... | collective-permute-start | bytes 3145736 | tf_op jit(solution)/shard_map/ppermute | solution.py:39
  203.6 26.6 %collective-permute-start.31 = (bf16[2,1024,256]{2,1,0:T(8,128)(2,1)S(1)}, bf16[2,1024,256]{2,1,0:T(8,128)(2,1)}, u32[]{:S(2)}, u32[]{:S(2)}) collective-permute-start(bf16[2,1024,256]{2,1,0:T(8,128)(2,1)S(1)} %pad_maximum_fusion.2.refs_1_), channel_id=1, source_target_pairs={{0,6},{1,7},{2,0},{3,1},{4,2},{5,3},{6,4},{7,5},{8,14},{9,15},{10,... | collective-permute-start | bytes 3145736 | tf_op jit(solution)/shard_map/ppermute | solution.py:39
  230.1 16.4 %collective-permute-start.32 = (bf16[1024,256]{1,0:T(8,128)(2,1)S(1)}, bf16[1024,256]{1,0:T(8,128)(2,1)}, u32[]{:S(2)}, u32[]{:S(2)}) collective-permute-start(bf16[1024,256]{1,0:T(8,128)(2,1)S(1)} %slice_bitcast_fusion.3), channel_id=1, source_target_pairs={{0,2},{1,3},{2,4},{3,5},{4,6},{5,7},{6,0},{7,1},{8,10},{9,11},{10,... | collective-permute-start | bytes 1572872 | tf_op jit(solution)/shard_map/ppermute | solution.py:39
  232.0 14.4 %collective-permute-start.33 = (bf16[1024,256]{1,0:T(8,128)(2,1)}, bf16[1024,256]{1,0:T(8,128)(2,1)}, u32[]{:S(2)}, u32[]{:S(2)}) collective-permute-start(bf16[1024,256]{1,0:T(8,128)(2,1)} %slice_bitcast_fusion.2), channel_id=1, source_target_pairs={{0,6},{1,7},{2,0},{3,1},{4,2},{5,3},{6,4},{7,5},{8,14},{9,15},{10,... | collective-permute-start | bytes 1572872 | tf_op jit(solution)/shard_map/ppermute | solution.py:39
  (19 other events, 92.4 us)
Sparse Core Ops, SparseCore 0:
  57.2 31.5 all-gather.2

commit v3 on v2

--- a/solution.py
+++ b/solution.py
@@ -15,7 +15,7 @@
 FAR = 1 << 20
 VMEM_LIMIT = 56 * 1024 * 1024
 FLOPS_PER_US = 1000000000
-F1 = 0
+F1 = 1
 F3 = 1
 F4 = 1
 F7 = 1
@@ -335,11 +335,11 @@
 def second_exchange(own, core_own, by_x, by_y, by_x2, by_y2, by_y3, ready):
     unit = by_y2.shape[0]
     by_x, by_y, by_x2 = after(by_x, ready, by_y), after(by_y, ready), after(by_x2, ready)
-    by_y2, by_y3 = after(by_y2, ready), after(by_y3, ready)
     by_yx = seq_swap(by_x, 4)
     x_fourth = by_x[2 * unit :]
     by_y2x = seq_swap(x_fourth, 8)
     by_y3x = seq_swap(x_fourth, 12)
+    by_y2, by_y3 = after(by_y2, by_yx), after(by_y3, by_yx)
     others = [by_x, by_y, by_x2, by_y2, by_y3, by_yx, by_y2x, by_y3x]
     return own, core_own, *others, *[seq_swap(value, 1) for value in others]
 
@@ -567,22 +567,22 @@
     low = rows // 4
     weights = (w_key, w_value, w_query)
 
-    mine = column_shares(w_out)
-    t0, t1 = tokens[:low], after(tokens[low:], mine)
+    t0, t1 = tokens[:low], tokens[low:]
     below0, above0 = z_shift(t0, 1), z_shift(t0, -1)
     other0, other1 = x_swap(t0), x_swap(t1)
     far0 = z_shift(below0, 1)
-    pair1 = jnp.stack([t1, after(other1, below0, above0)])
+    pair1 = jnp.stack([t1, after(other1, below0, above0, far0)])
     below1, above1 = z_shift(pair1, 1), z_shift(pair1, -1)
     others0 = x_swap(jnp.stack([below0, above0, far0]))
     first = z_first_pieces(t0, below0, above0, far0, other0, others0)
     old = project(first, 0, rows, [], [], True, norm_gain, weights, offsets, C0)
-    w_columns = gather_shares(after(mine, far0))
     if F1:
         below1 = after(below1, old[1])
     far1 = z_shift(below1[0], 1), z_shift(above1[1], -1)
-    second = x_first_pieces(pair1, below1, above1, *far1)
+    mine = column_shares(after(w_out, far0))
+    second = x_first_pieces(pair1, after(below1, mine), above1, *far1)
     sums = project(second[:6], low, rows, [], [], False, norm_gain, weights, offsets, C1)
+    w_columns = gather_shares(after(mine, sums[1]))
     old = project(second[6:], low, rows, sums, old, True, norm_gain, weights, offsets, C2)
     k, v, q = old[:3]
     exchanged = first_exchange(*old[3:])

time: 262 us -> 258 us (0.985)
  waiting for transfers between devices: 102 us -> 89.8 us
  starting transfers between devices: 48.3 us -> 53.5 us
  local copies, waits for them, and re-layouts: 13.3 us -> 16.4 us
    ppermute x6, waiting for transfers between devices: 43.1 us -> 32.6 us  [x_swap(): return lax.ppermute(value, 'tp', [(t, t ^ 1) for t in range(8)])]
    all_to_all x1, waiting for transfers between devices: 9.45 us -> 0.01 us  [column_shares(): return lax.all_to_all(cut, 'tp', 0, 0, tiled=True)]
    ppermute x14, waiting for transfers between devices: 32.2 us -> 40.3 us  [z_shift(): return lax.ppermute(value, 'tp', pairs)]
    ppermute x14, starting transfers between devices: 17.8 us -> 21.2 us  [z_shift(): return lax.ppermute(value, 'tp', pairs)]
    ppermute x17, starting transfers between devices: 10.4 us -> 13.2 us  [seq_swap(): return lax.ppermute(value, 'seq', [(s, s ^ mask) for s in range(16)])]
  transfers between devices with their start and end apart: 39 -> 39, of which waited for: 17 -> 18; matrix products, arithmetic and copies ran while one was open for 4% -> 6% of each run, Pallas kernels for 28% -> 28%
where the time goes in v3:
time: 258 us; the launch traced here: 257 us
  waiting for transfers between devices  89.8 us (35%)
  Pallas kernels  80.4 us (31%)
  starting transfers between devices  53.5 us (21%)
  local copies, waits for them, and re-layouts  16.4 us (6%)
  between operations  13.9 us (5%)
  other arithmetic  2.89 us (1%)
    ppermute x14, waiting for transfers between devices, z_shift(): return lax.ppermute(value, 'tp', pairs)  40.3 us
    pallas_call x3, Pallas kernels, project(): pl.pallas_call(functools.partial(project_kernel, where, len(operands), fi...  37.5 us
    ppermute x6, waiting for transfers between devices, x_swap(): return lax.ppermute(value, 'tp', [(t, t ^ 1) for t in range(8)])  32.6 us
    ppermute x14, starting transfers between devices, z_shift(): return lax.ppermute(value, 'tp', pairs)  21.2 us
    pallas_call x2, Pallas kernels, attend(): pl.pallas_call(functools.partial(attend_kernel, levels, head_base), grid_...  17.8 us
    ppermute x17, waiting for transfers between devices, seq_swap(): return lax.ppermute(value, 'seq', [(s, s ^ mask) for s in range(16)])  16.9 us
    pallas_call x2, Pallas kernels, output(): pl.pallas_call(functools.partial(output_kernel, where, len(operands), sha...  15.9 us
    ppermute x17, starting transfers between devices, seq_swap(): return lax.ppermute(value, 'seq', [(s, s ^ mask) for s in range(16)])  13.2 us
  transfers between devices with their start and end apart: 39, of which 18 were waited for; matrix products, arithmetic and copies ran while one was open for 6% of the time, Pallas kernels for 28%

profile of v3, /device:TPU:0, one launch (start us, length us, event | category | flops | bytes accessed | tf_op | source)
XLA Modules:
  0.0 256.9 jit_solution(10219829261857587750)
XLA Ops:
  7.5 2.1 collective-permute-start.1
  9.6 1.2 slice_bitcast_fusion.4
  10.8 3.1 %collective-permute-start = (bf16[768,512]{1,0:T(8,128)(2,1)S(1)}, bf16[768,512]{1,0:T(8,128)(2,1)}, u32[]{:S(2)}, u32[]{:S(2)}) collective-permute-start(bf16[768,512]{1,0:T(8,128)(2,1)S(1)} %get-tuple-element.70), channel_id=1, source_target_pairs={{0,1},{1,0},{2,3},{3,2},{4,5},{5,4},{6,7},{7,6},{8,9},{9,8},{10,11... | collective-permute-start | bytes 2359304 | tf_op jit(solution)/shard_map/ppermute | solution.py:43
  14.0 2.2 collective-permute-start.2
  16.1 1.9 collective-permute-done.1.refs_3_
  18.0 3.6 %collective-permute-done.2.refs_4_ = bf16[256,512]{1,0:T(8,128)(2,1)S(1)} collective-permute-done((bf16[256,512]{1,0:T(8,128)(2,1)S(1)}, bf16[256,512]{1,0:T(8,128)(2,1)S(1)}, u32[]{:S(2)}, u32[]{:S(2)}) %collective-permute-start.2) | collective-permute-done | bytes 262176 | tf_op jit(solution)/shard_map/ppermute | solution.py:39
  21.6 5.2 %collective-permute-done.3.refs_5_ = bf16[256,512]{1,0:T(8,128)(2,1)S(1)} collective-permute-done((bf16[256,512]{1,0:T(8,128)(2,1)S(1)}, bf16[256,512]{1,0:T(8,128)(2,1)S(1)}, u32[]{:S(2)}, u32[]{:S(2)}) %collective-permute-start.3) | collective-permute-done | bytes 262176 | tf_op jit(solution)/shard_map/ppermute | solution.py:39
  26.9 3.0 %collective-permute-start.6 = (bf16[3,256,512]{2,1,0:T(8,128)(2,1)S(1)}, bf16[3,256,512]{2,1,0:T(8,128)(2,1)}, u32[]{:S(2)}, u32[]{:S(2)}) collective-permute-start(bf16[3,256,512]{2,1,0:T(8,128)(2,1)S(1)} %pad_maximum_fusion.3), channel_id=1, source_target_pairs={{0,1},{1,0},{2,3},{3,2},{4,5},{5,4},{6,7},{7,6},{8,9},{9,8},{10,11... | collective-permute-start | bytes 2359304 | tf_op jit(solution)/shard_map/ppermute | solution.py:43
  33.1 1.3 pad_maximum_fusion.refs_2_
  34.4 1.9 collective-permute-start.4
  36.3 1.4 collective-permute-start.8
  37.7 1.1 constant_dynamic-slice_fusion
  39.9 6.0 %all-to-all-start = ((bf16[8,64,512]{2,1,0:T(8,128)(2,1)}), bf16[8,64,512]{2,1,0:T(8,128)(2,1)S(1)}, u32[]{:S(2)}, u32[]{:S(2)}) async-start(bf16[8,64,512]{2,1,0:T(8,128)(2,1)} %copy.33), calls=%async_computation | async-start | bytes 1048576 | tf_op jit(solution)/shard_map/all_to_all | solution.py:552
  46.0 9.5 %collective-permute-done.5.refs_6_ = bf16[256,512]{1,0:T(8,128)(2,1)} collective-permute-done((bf16[256,512]{1,0:T(8,128)(2,1)S(1)}, bf16[256,512]{1,0:T(8,128)(2,1)}, u32[]{:S(2)}, u32[]{:S(2)}) %collective-permute-start.5) | collective-permute-done | bytes 262176 | tf_op jit(solution)/shard_map/ppermute | solution.py:43
  55.5 11.1 %project.3 = (bf16[1024,512]{1,0:T(8,128)(2,1)}, bf16[1024,512]{1,0:T(8,128)(2,1)}, bf16[1024,512]{1,0:T(8,128)(2,1)}, bf16[960,1024]{1,0:T(8,128)(2,1)}, bf16[2...) custom-call(s32[8]{0:T(128)} %stack.131.refs_0_, s32[5,4]{1,0:T(8,128)} %copy.37.refs_1_.refs_0_, ...), custom_call_target="tpu_custom_call" | custom-call | flops 12000000000 | bytes 1024 | tf_op jit(solution)/shard_map/project/pallas_call | solution.py:290
  66.6 7.7 %collective-permute-done.4.refs_3_ = bf16[2,768,512]{2,1,0:T(8,128)(2,1)} collective-permute-done((bf16[2,768,512]{2,1,0:T(8,128)(2,1)S(1)}, bf16[2,768,512]{2,1,0:T(8,128)(2,1)}, u32[]{:S(2)}, u32[]{:S(2)}) %collective-permute-start.4) | collective-permute-done | bytes 1572896 | tf_op jit(solution)/shard_map/ppermute | solution.py:39
  74.3 1.2 slice_bitcast_fusion.1
  75.6 1.2 slice_bitcast_fusion
  76.8 3.3 %collective-permute-start.9 = (bf16[768,512]{1,0:T(8,128)(2,1)S(1)}, bf16[768,512]{1,0:T(8,128)(2,1)S(1)}, u32[]{:S(2)}, u32[]{:S(2)}) collective-permute-start(bf16[768,512]{1,0:T(8,128)(2,1)S(1)} %slice_bitcast_fusion), channel_id=1, source_target_pairs={{0,6},{1,7},{2,0},{3,1},{4,2},{5,3},{6,4},{7,5},{8,14},{9,15},{10,... | collective-permute-start | bytes 2359304 | tf_op jit(solution)/shard_map/ppermute | solution.py:39
  80.0 16.2 %project.4 = (f32[3,768,512]{2,1,0:T(8,128)}, f32[768,128]{1,0:T(8,128)}) custom-call(s32[6]{0:T(128)} %stack.136.refs_0_, s32[5,4]{1,0:T(8,128)} %copy.37.refs_1_.refs_0_, bf16[2,768,512]{2,1,0:T(8,128)(2,1)} %copy-done.1, bf16[2,768,512]{2,1,0:T(8,128)(2,1)} %collective-permute-done.4.refs_3_, bf16[2,768,512]{2,1,0:T(8,128)(2,1)} %collective-permute-done.8.refs_4_, ...), custom_call_target="tpu_custom_call" | custom-call | flops 20000000000 | bytes 1024 | tf_op jit(solution)/shard_map/project/pallas_call | solution.py:290
  97.8 10.2 %project.5 = (bf16[1024,512]{1,0:T(8,128)(2,1)}, bf16[1024,512]{1,0:T(8,128)(2,1)}, bf16[1024,512]{1,0:T(8,128)(2,1)}, bf16[960,1024]{1,0:T(8,128)(2,1)}, bf16[2...) custom-call(s32[2]{0:T(128)} %pad_add_fusion.2.refs_0_, ...), custom_call_target="tpu_custom_call", output_to_operand_aliasing={{0}: (10, {}), {1}: (11, {}), {2}: (12, {}), {3}: (13, {}),... | custom-call | flops 8000000000 | bytes 1024 | tf_op jit(solution)/shard_map/project/pallas_call | solution.py:290
  108.0 1.4 collective-permute-start.11
  109.4 1.6 collective-permute-start.12
  111.8 2.9 %collective-permute-start.14 = (bf16[64,1024]{1,0:T(8,128)(2,1)}, bf16[64,1024]{1,0:T(8,128)(2,1)S(1)}, u32[]{:S(2)}, u32[]{:S(2)}) collective-permute-start(bf16[64,1024]{1,0:T(8,128)(2,1)} %get-tuple-element.62), channel_id=1, source_target_pairs={{0,64},{8,72},{16,80},{24,88},{32,96},{40,104},{48,112},{56,120},{... | collective-permute-start | bytes 393224 | tf_op jit(solution)/shard_map/ppermute | solution.py:47
  114.7 9.3 %attend_local.1 = (f32[1024,512]{1,0:T(8,128)}, f32[1024,512]{1,0:T(8,128)}, f32[1024,512]{1,0:T(8,128)}) custom-call(bf16[1024,512]{1,0:T(8,128)(2,1)} %get-tuple-element.65.q_ref.refs_1_, bf16[1024,512]{1,0:T(8,128)(2,1)} %get-tuple-element.51.k_ref, bf16[1024,512]{1,0:T(8,128)(2,1)} %get-tuple-element.52.v_ref), custom_call_target="tpu_custom_call" | custom-call | flops 8999999488 | bytes 1024 | tf_op jit(solution)/shard_map/attend_local/pallas_call | solution.py:408
  124.3 4.5 %collective-permute-done.12.refs_8_.refs_26_ = bf16[192,1024]{1,0:T(8,128)(2,1)} collective-permute-done((bf16[192,1024]{1,0:T(8,128)(2,1)}, bf16[192,1024]{1,0:T(8,128)(2,1)}, u32[]{:S(2)}, u32[]{:S(2)}) %collective-permute-start.12) | collective-permute-done | bytes 393248 | tf_op jit(solution)/shard_map/ppermute | solution.py:47
  128.9 3.4 %collective-permute-start.17 = (bf16[64,1024]{1,0:T(8,128)(2,1)S(1)}, bf16[64,1024]{1,0:T(8,128)(2,1)S(1)}, u32[]{:S(2)}, u32[]{:S(2)}) collective-permute-start(bf16[64,1024]{1,0:T(8,128)(2,1)S(1)} %slice.25), channel_id=1, source_target_pairs={{0,64},{8,72},{16,80},{24,88},{32,96},{40,104},{48,112},{56,120},{... | collective-permute-start | bytes 393224 | tf_op jit(solution)/shard_map/ppermute | solution.py:47
  132.3 4.6 %collective-permute-done.14.refs_10_.refs_28_ = bf16[64,1024]{1,0:T(8,128)(2,1)S(1)} collective-permute-done((bf16[64,1024]{1,0:T(8,128)(2,1)}, bf16[64,1024]{1,0:T(8,128)(2,1)S(1)}, u32[]{:S(2)}, u32[]{:S(2)}) %collective-permute-start.14) | collective-permute-done | bytes 131104 | tf_op jit(solution)/shard_map/ppermute | solution.py:47
  137.8 3.3 %collective-permute-done.17.refs_13_.refs_31_ = bf16[64,1024]{1,0:T(8,128)(2,1)S(1)} collective-permute-done((bf16[64,1024]{1,0:T(8,128)(2,1)S(1)}, bf16[64,1024]{1,0:T(8,128)(2,1)S(1)}, u32[]{:S(2)}, u32[]{:S(2)}) %collective-permute-start.17) | collective-permute-done | bytes 131104 | tf_op jit(solution)/shard_map/ppermute | solution.py:47
  141.1 1.9 collective-permute-done.18.refs_14_.refs_32_
  144.5 1.7 collective-permute-done.15.refs_12_.refs_30_
  148.8 1.2 copy-done.14
  150.0 8.9 %attend.2.refs_1_ = bf16[1024,256]{1,0:T(8,128)(2,1)} custom-call(s32[5,4]{1,0:T(8,128)} %copy.37.refs_1_.refs_0_, bf16[1024,512]{1,0:T(8,128)(2,1)} %get-tuple-element.65.q_ref.refs_1_, f32[1024,512]{1,0:T(8,128)} %get-tuple-element.53.refs_2_, f32[1024,512]{1,0:T(8,128)} %get-tuple-element.54.refs_3_, f32[1024,512]{1,0:T(8,128)} %get-tuple-element.55.refs_4_, ...), custom_call_target="tpu_custom_call" | custom-call | flops 8999999488 | bytes 1024 | tf_op jit(solution)/shard_map/attend/pallas_call | solution.py:472
  159.9 8.9 %attend.3 = bf16[1024,256]{1,0:T(8,128)(2,1)} custom-call(s32[5,4]{1,0:T(8,128)} %copy.37.refs_1_.refs_0_, bf16[1024,512]{1,0:T(8,128)(2,1)} %get-tuple-element.65.q_ref.refs_1_, f32[1024,512]{1,0:T(8,128)} %get-tuple-element.53.refs_2_, f32[1024,512]{1,0:T(8,128)} %get-tuple-element.54.refs_3_, f32[1024,512]{1,0:T(8,128)} %get-tuple-element.55.refs_4_, ...), custom_call_target="tpu_custom_call" | custom-call | flops 8999999488 | bytes 1024 | tf_op jit(solution)/shard_map/attend/pallas_call | solution.py:472
  168.8 3.0 %collective-permute-start.27 = (bf16[1024,256]{1,0:T(8,128)(2,1)}, bf16[1024,256]{1,0:T(8,128)(2,1)S(1)}, u32[]{:S(2)}, u32[]{:S(2)}) collective-permute-start(bf16[1024,256]{1,0:T(8,128)(2,1)} %attend.3), channel_id=1, source_target_pairs={{0,1},{1,0},{2,3},{3,2},{4,5},{5,4},{6,7},{7,6},{8,9},{9,8},{10,11... | collective-permute-start | bytes 1572872 | tf_op jit(solution)/shard_map/ppermute | solution.py:43
  171.8 2.7 %collective-permute-start.29 = (bf16[1024,256]{1,0:T(8,128)(2,1)S(1)}, bf16[1024,256]{1,0:T(8,128)(2,1)S(1)}, u32[]{:S(2)}, u32[]{:S(2)}) collective-permute-start(bf16[1024,256]{1,0:T(8,128)(2,1)S(1)} %copy-done.17), channel_id=1, source_target_pairs={{0,6},{1,7},{2,0},{3,1},{4,2},{5,3},{6,4},{7,5},{8,14},{9,15},{10,... | collective-permute-start | bytes 1572872 | tf_op jit(solution)/shard_map/ppermute | solution.py:39
  174.8 10.6 %collective-permute-done.27 = bf16[1024,256]{1,0:T(8,128)(2,1)S(1)} collective-permute-done((bf16[1024,256]{1,0:T(8,128)(2,1)}, bf16[1024,256]{1,0:T(8,128)(2,1)S(1)}, u32[]{:S(2)}, u32[]{:S(2)}) %collective-permute-start.27) | collective-permute-done | bytes 524320 | tf_op jit(solution)/shard_map/ppermute | solution.py:43
  185.7 10.1 %collective-permute-done.34.refs_5_ = bf16[1024,256]{1,0:T(8,128)(2,1)S(1)} collective-permute-done((bf16[1024,256]{1,0:T(8,128)(2,1)S(1)}, bf16[1024,256]{1,0:T(8,128)(2,1)S(1)}, u32[]{:S(2)}, u32[]{:S(2)}) %collective-permute-start.34) | collective-permute-done | bytes 524320 | tf_op jit(solution)/shard_map/ppermute | solution.py:43
  196.8 3.0 %collective-permute-start.36 = (bf16[3,1024,256]{2,1,0:T(8,128)(2,1)S(1)}, bf16[3,1024,256]{2,1,0:T(8,128)(2,1)}, u32[]{:S(2)}, u32[]{:S(2)}) collective-permute-start(bf16[3,1024,256]{2,1,0:T(8,128)(2,1)S(1)} %pad_maximum_fusion.1), channel_id=1, source_target_pairs={{0,1},{1,0},{2,3},{3,2},{4,5},{5,4},{6,7},{7,6},{8,9},{9,8},{10,11... | collective-permute-start | bytes 4718600 | tf_op jit(solution)/shard_map/ppermute | solution.py:43
  199.9 1.4 collective-permute-start.30
  201.4 1.9 collective-permute-start.31
  203.9 21.5 %collective-permute-done.30.refs_2_ = bf16[2,1024,256]{2,1,0:T(8,128)(2,1)} collective-permute-done((bf16[2,1024,256]{2,1,0:T(8,128)(2,1)S(1)}, bf16[2,1024,256]{2,1,0:T(8,128)(2,1)}, u32[]{:S(2)}, u32[]{:S(2)}) %collective-permute-start.30) | collective-permute-done | bytes 1048608 | tf_op jit(solution)/shard_map/ppermute | solution.py:39
  225.4 1.1 slice_bitcast_fusion.3
  226.7 1.9 slice_bitcast_fusion.2
  228.6 3.1 %collective-permute-start.33 = (bf16[1024,256]{1,0:T(8,128)(2,1)}, bf16[1024,256]{1,0:T(8,128)(2,1)}, u32[]{:S(2)}, u32[]{:S(2)}) collective-permute-start(bf16[1024,256]{1,0:T(8,128)(2,1)} %slice_bitcast_fusion.2), channel_id=1, source_target_pairs={{0,6},{1,7},{2,0},{3,1},{4,2},{5,3},{6,4},{7,5},{8,14},{9,15},{10,... | collective-permute-start | bytes 1572872 | tf_op jit(solution)/shard_map/ppermute | solution.py:39
  231.7 2.4 collective-permute-done.36.refs_6_
  234.1 7.9 %output.2.refs_6_ = f32[1024,512]{1,0:T(8,128)} custom-call(s32[8]{0:T(128)} %stack.131.refs_0_, bf16[1024,256]{1,0:T(8,128)(2,1)} %attend.2.refs_1_, bf16[1024,256]{1,0:T(8,128)(2,1)} %copy-done.3, bf16[1024,256]{1,0:T(8,128)(2,1)} %copy-done.4, bf16[1024,256]{1,0:T(8,128)(2,1)} %copy-done.5, bf16[1024,256]{1,0:T(8,128)(2,1)} %copy-done.18, ...), custom_call_target="tpu_custom_call" | custom-call | flops 8000000000 | bytes 1024 | tf_op jit(solution)/shard_map/output/pallas_call | solution.py:526
  242.1 8.0 %output.3 = bf16[1024,512]{1,0:T(8,128)(2,1)} custom-call(s32[8]{0:T(128)} %stack.126.refs_0_, bf16[2,1024,256]{2,1,0:T(8,128)(2,1)} %copy-done.2, bf16[2,1024,256]{2,1,0:T(8,128)(2,1)} %collective-permute-done.30.refs_2_, bf16[2,1024,256]{2,1,0:T(8,128)(2,1)} %collective-permute-done.31.refs_3_, bf16[1024,256]{1,0:T(8,128)(2,1)} %collective-permute-done.32.refs_4_, ...), custom_call_target="tpu_custom_call" | custom-call | flops 30000001024 | bytes 1024 | tf_op jit(solution)/shard_map/output/pallas_call | solution.py:526
  (133 shorter events, 16.5 us)
Async XLA Ops:
  7.5 22.4 %copy-start.7 = (bf16[256,512]{1,0:T(8,128)(2,1)}, bf16[256,512]{1,0:T(8,128)(2,1)S(1)}, u32[]{:S(2)}) copy-start(bf16[256,512]{1,0:T(8,128)(2,1)S(1)} %slice.22.refs_2_) | copy-start | bytes 786436
  7.5 23.0 %copy-start.13 = (s32[5,4]{0,1:T(4,128)S(1)}, s32[5,4]{0,1:T(4,128)}, u32[]{:S(2)}) copy-start(s32[5,4]{0,1:T(4,128)} %param.13) | copy-start | bytes 244
  7.5 23.7 %copy-start.12 = (f32[4096]{0:T(1024)S(1)}, f32[4096]{0:T(1024)}, u32[]{:S(2)}) copy-start(f32[4096]{0:T(1024)} %param.8) | copy-start | bytes 49156
  7.5 10.5 %collective-permute-start.1 = (bf16[256,512]{1,0:T(8,128)(2,1)S(1)}, bf16[256,512]{1,0:T(8,128)(2,1)S(1)}, u32[]{:S(2)}, u32[]{:S(2)}) collective-permute-start(bf16[256,512]{1,0:T(8,128)(2,1)S(1)} %slice.22.refs_2_), channel_id=1, source_target_pairs={{0,2},{1,3},{2,4},{3,5},{4,6},{5,7},{6,0},{7,1},{8,10},{9,11},{10,... | collective-permute-start | bytes 786440 | tf_op jit(solution)/shard_map/ppermute | solution.py:39
  10.8 22.2 %collective-permute-start = (bf16[768,512]{1,0:T(8,128)(2,1)S(1)}, bf16[768,512]{1,0:T(8,128)(2,1)}, u32[]{:S(2)}, u32[]{:S(2)}) collective-permute-start(bf16[768,512]{1,0:T(8,128)(2,1)S(1)} %get-tuple-element.70), channel_id=1, source_target_pairs={{0,1},{1,0},{2,3},{3,2},{4,5},{5,4},{6,7},{7,6},{8,9},{9,8},{10,11... | collective-permute-start | bytes 2359304 | tf_op jit(solution)/shard_map/ppermute | solution.py:43
  14.0 7.7 %collective-permute-start.2 = (bf16[256,512]{1,0:T(8,128)(2,1)S(1)}, bf16[256,512]{1,0:T(8,128)(2,1)S(1)}, u32[]{:S(2)}, u32[]{:S(2)}) collective-permute-start(bf16[256,512]{1,0:T(8,128)(2,1)S(1)} %slice.22.refs_2_), channel_id=1, source_target_pairs={{0,6},{1,7},{2,0},{3,1},{4,2},{5,3},{6,4},{7,5},{8,14},{9,15},{10,... | collective-permute-start | bytes 786440 | tf_op jit(solution)/shard_map/ppermute | solution.py:39
  18.0 15.0 %copy-start.8 = (bf16[256,512]{1,0:T(8,128)(2,1)}, bf16[256,512]{1,0:T(8,128)(2,1)S(1)}, u32[]{:S(2)}) copy-start(bf16[256,512]{1,0:T(8,128)(2,1)S(1)} %collective-permute-done.1.refs_3_) | copy-start | bytes 786436
  18.0 8.8 %collective-permute-start.3 = (bf16[256,512]{1,0:T(8,128)(2,1)S(1)}, bf16[256,512]{1,0:T(8,128)(2,1)S(1)}, u32[]{:S(2)}, u32[]{:S(2)}) collective-permute-start(bf16[256,512]{1,0:T(8,128)(2,1)S(1)} %collective-permute-done.1.refs_3_), channel_id=1, source_target_pairs={{0,2},{1,3},{2,4},{3,5},{4,6},{5,7},{6,0},{7,1},{8,10},{9,11},{10,... | collective-permute-start | bytes 786440 | tf_op jit(solution)/shard_map/ppermute | solution.py:39
  26.9 28.5 %collective-permute-start.6 = (bf16[3,256,512]{2,1,0:T(8,128)(2,1)S(1)}, bf16[3,256,512]{2,1,0:T(8,128)(2,1)}, u32[]{:S(2)}, u32[]{:S(2)}) collective-permute-start(bf16[3,256,512]{2,1,0:T(8,128)(2,1)S(1)} %pad_maximum_fusion.3), channel_id=1, source_target_pairs={{0,1},{1,0},{2,3},{3,2},{4,5},{5,4},{6,7},{7,6},{8,9},{9,8},{10,11... | collective-permute-start | bytes 2359304 | tf_op jit(solution)/shard_map/ppermute | solution.py:43
  29.9 25.5 %collective-permute-start.5 = (bf16[256,512]{1,0:T(8,128)(2,1)S(1)}, bf16[256,512]{1,0:T(8,128)(2,1)}, u32[]{:S(2)}, u32[]{:S(2)}) collective-permute-start(bf16[256,512]{1,0:T(8,128)(2,1)S(1)} %slice.22.refs_2_), channel_id=1, source_target_pairs={{0,1},{1,0},{2,3},{3,2},{4,5},{5,4},{6,7},{7,6},{8,9},{9,8},{10,11... | collective-permute-start | bytes 786440 | tf_op jit(solution)/shard_map/ppermute | solution.py:43
  34.4 39.9 %collective-permute-start.4 = (bf16[2,768,512]{2,1,0:T(8,128)(2,1)S(1)}, bf16[2,768,512]{2,1,0:T(8,128)(2,1)}, u32[]{:S(2)}, u32[]{:S(2)}) collective-permute-start(bf16[2,768,512]{2,1,0:T(8,128)(2,1)S(1)} %pad_maximum_fusion.refs_2_), channel_id=1, source_target_pairs={{0,2},{1,3},{2,4},{3,5},{4,6},{5,7},{6,0},{7,1},{8,10},{9,11},{10,... | collective-permute-start | bytes 4718600 | tf_op jit(solution)/shard_map/ppermute | solution.py:39
  36.3 39.3 %collective-permute-start.8 = (bf16[2,768,512]{2,1,0:T(8,128)(2,1)S(1)}, bf16[2,768,512]{2,1,0:T(8,128)(2,1)}, u32[]{:S(2)}, u32[]{:S(2)}) collective-permute-start(bf16[2,768,512]{2,1,0:T(8,128)(2,1)S(1)} %pad_maximum_fusion.refs_2_), channel_id=1, source_target_pairs={{0,6},{1,7},{2,0},{3,1},{4,2},{5,3},{6,4},{7,5},{8,14},{9,15},{10,... | collective-permute-start | bytes 4718600 | tf_op jit(solution)/shard_map/ppermute | solution.py:39
  39.9 40.1 %all-to-all-start = ((bf16[8,64,512]{2,1,0:T(8,128)(2,1)}), bf16[8,64,512]{2,1,0:T(8,128)(2,1)S(1)}, u32[]{:S(2)}, u32[]{:S(2)}) async-start(bf16[8,64,512]{2,1,0:T(8,128)(2,1)} %copy.33), calls=%async_computation | async-start | bytes 1048576 | tf_op jit(solution)/shard_map/all_to_all | solution.py:552
  46.0 188.2 %all-gather.3.cloned.1.call-start = ((), (), s32[]{:S(2)}) async-start(), calls=%async_computation.1 | async-start | bytes 4718592 | tf_op jit(solution)/shard_map/all_gather | solution.py:557
  75.5 21.4 %collective-permute-start.7 = (bf16[768,512]{1,0:T(8,128)(2,1)S(1)}, bf16[768,512]{1,0:T(8,128)(2,1)}, u32[]{:S(2)}, u32[]{:S(2)}) collective-permute-start(bf16[768,512]{1,0:T(8,128)(2,1)S(1)} %slice_bitcast_fusion.1), channel_id=1, source_target_pairs={{0,2},{1,3},{2,4},{3,5},{4,6},{5,7},{6,0},{7,1},{8,10},{9,11},{10,... | collective-permute-start | bytes 2359304 | tf_op jit(solution)/shard_map/ppermute | solution.py:39
  76.8 20.1 %collective-permute-start.9 = (bf16[768,512]{1,0:T(8,128)(2,1)S(1)}, bf16[768,512]{1,0:T(8,128)(2,1)S(1)}, u32[]{:S(2)}, u32[]{:S(2)}) collective-permute-start(bf16[768,512]{1,0:T(8,128)(2,1)S(1)} %slice_bitcast_fusion), channel_id=1, source_target_pairs={{0,6},{1,7},{2,0},{3,1},{4,2},{5,3},{6,4},{7,5},{8,14},{9,15},{10,... | collective-permute-start | bytes 2359304 | tf_op jit(solution)/shard_map/ppermute | solution.py:39
  80.0 16.2 %copy-start = (bf16[8,64,512]{2,1,0:T(8,128)(2,1)}, bf16[8,64,512]{2,1,0:T(8,128)(2,1)S(1)}, u32[]{:S(2)}) copy-start(bf16[8,64,512]{2,1,0:T(8,128)(2,1)S(1)} %all-to-all-done) | copy-start | bytes 1572868
  108.0 16.1 %collective-permute-start.11 = (bf16[192,1024]{1,0:T(8,128)(2,1)}, bf16[192,1024]{1,0:T(8,128)(2,1)S(1)}, u32[]{:S(2)}, u32[]{:S(2)}) collective-permute-start(bf16[192,1024]{1,0:T(8,128)(2,1)} %get-tuple-element.57), channel_id=1, source_target_pairs={{0,16},{8,24},{16,0},{24,8},{32,48},{40,56},{48,32},{56,40},{64,80... | collective-permute-start | bytes 1179656 | tf_op jit(solution)/shard_map/ppermute | solution.py:47
  109.4 19.5 %collective-permute-start.12 = (bf16[192,1024]{1,0:T(8,128)(2,1)}, bf16[192,1024]{1,0:T(8,128)(2,1)}, u32[]{:S(2)}, u32[]{:S(2)}) collective-permute-start(bf16[192,1024]{1,0:T(8,128)(2,1)} %get-tuple-element.57), channel_id=1, source_target_pairs={{0,32},{8,40},{16,48},{24,56},{32,0},{40,8},{48,16},{56,24},{64,96... | collective-permute-start | bytes 1179656 | tf_op jit(solution)/shard_map/ppermute | solution.py:47
  111.0 37.7 %collective-permute-start.10 = (bf16[960,1024]{1,0:T(8,128)(2,1)}, bf16[960,1024]{1,0:T(8,128)(2,1)S(1)}, u32[]{:S(2)}, u32[]{:S(2)}) collective-permute-start(bf16[960,1024]{1,0:T(8,128)(2,1)} %get-tuple-element.56.refs_5_.refs_23_), channel_id=1, source_target_pairs={{0,8},{8,0},{16,24},{24,16},{32,40},{40,32},{48,56},{56,48},{64,72... | collective-permute-start | bytes 5898248 | tf_op jit(solution)/shard_map/ppermute | solution.py:47
  111.0 32.1 %collective-permute-start.13 = (bf16[256,1024]{1,0:T(8,128)(2,1)}, bf16[256,1024]{1,0:T(8,128)(2,1)S(1)}, u32[]{:S(2)}, u32[]{:S(2)}) collective-permute-start(bf16[256,1024]{1,0:T(8,128)(2,1)} %get-tuple-element.60), channel_id=1, source_target_pairs={{0,16},{8,24},{16,0},{24,8},{32,48},{40,56},{48,32},{56,40},{64,80... | collective-permute-start | bytes 1572872 | tf_op jit(solution)/shard_map/ppermute | solution.py:47
  111.8 25.0 %collective-permute-start.14 = (bf16[64,1024]{1,0:T(8,128)(2,1)}, bf16[64,1024]{1,0:T(8,128)(2,1)S(1)}, u32[]{:S(2)}, u32[]{:S(2)}) collective-permute-start(bf16[64,1024]{1,0:T(8,128)(2,1)} %get-tuple-element.62), channel_id=1, source_target_pairs={{0,64},{8,72},{16,80},{24,88},{32,96},{40,104},{48,112},{56,120},{... | collective-permute-start | bytes 393224 | tf_op jit(solution)/shard_map/ppermute | solution.py:47
  124.0 24.7 %copy-start.11 = (bf16[192,1024]{1,0:T(8,128)(2,1)}, bf16[192,1024]{1,0:T(8,128)(2,1)S(1)}, u32[]{:S(2)}) copy-start(bf16[192,1024]{1,0:T(8,128)(2,1)S(1)} %collective-permute-done.11.refs_7_.refs_25_) | copy-start | bytes 1179652
  124.0 12.9 %collective-permute-start.16 = (bf16[64,1024]{1,0:T(8,128)(2,1)}, bf16[64,1024]{1,0:T(8,128)(2,1)S(1)}, u32[]{:S(2)}, u32[]{:S(2)}) collective-permute-start(bf16[64,1024]{1,0:T(8,128)(2,1)} %get-tuple-element.62), channel_id=1, source_target_pairs={{0,96},{8,104},{16,112},{24,120},{32,64},{40,72},{48,80},{56,88},{... | collective-permute-start | bytes 393224 | tf_op jit(solution)/shard_map/ppermute | solution.py:47
  128.9 12.2 %collective-permute-start.17 = (bf16[64,1024]{1,0:T(8,128)(2,1)S(1)}, bf16[64,1024]{1,0:T(8,128)(2,1)S(1)}, u32[]{:S(2)}, u32[]{:S(2)}) collective-permute-start(bf16[64,1024]{1,0:T(8,128)(2,1)S(1)} %slice.25), channel_id=1, source_target_pairs={{0,64},{8,72},{16,80},{24,88},{32,96},{40,104},{48,112},{56,120},{... | collective-permute-start | bytes 393224 | tf_op jit(solution)/shard_map/ppermute | solution.py:47
  136.8 6.2 %collective-permute-start.18 = (bf16[64,1024]{1,0:T(8,128)(2,1)S(1)}, bf16[64,1024]{1,0:T(8,128)(2,1)S(1)}, u32[]{:S(2)}, u32[]{:S(2)}) collective-permute-start(bf16[64,1024]{1,0:T(8,128)(2,1)S(1)} %slice.25), channel_id=1, source_target_pairs={{0,96},{8,104},{16,112},{24,120},{32,64},{40,72},{48,80},{56,88},{... | collective-permute-start | bytes 393224 | tf_op jit(solution)/shard_map/ppermute | solution.py:47
  137.0 9.3 %collective-permute-start.15 = (bf16[192,1024]{1,0:T(8,128)(2,1)S(1)}, bf16[192,1024]{1,0:T(8,128)(2,1)}, u32[]{:S(2)}, u32[]{:S(2)}) collective-permute-start(bf16[192,1024]{1,0:T(8,128)(2,1)S(1)} %collective-permute-done.11.refs_7_.refs_25_), channel_id=1, source_target_pairs={{0,32},{8,40},{16,48},{24,56},{32,0},{40,8},{48,16},{56,24},{64,96... | collective-permute-start | bytes 1179656 | tf_op jit(solution)/shard_map/ppermute | solution.py:47
  141.1 2.6 collective-permute-start.25
  143.0 1.3 collective-permute-start.26
  143.1 3.2 %collective-permute-start.19 = (bf16[192,1024]{1,0:T(8,128)(2,1)S(1)}, bf16[192,1024]{1,0:T(8,128)(2,1)S(1)}, u32[]{:S(2)}, u32[]{:S(2)}) collective-permute-start(bf16[192,1024]{1,0:T(8,128)(2,1)S(1)} %collective-permute-done.11.refs_7_.refs_25_), channel_id=1, source_target_pairs={{0,8},{8,0},{16,24},{24,16},{32,40},{40,32},{48,56},{56,48},{64,72... | collective-permute-start | bytes 1179656 | tf_op jit(solution)/shard_map/ppermute | solution.py:47
  143.6 3.3 %collective-permute-start.20 = (bf16[192,1024]{1,0:T(8,128)(2,1)}, bf16[192,1024]{1,0:T(8,128)(2,1)S(1)}, u32[]{:S(2)}, u32[]{:S(2)}) collective-permute-start(bf16[192,1024]{1,0:T(8,128)(2,1)} %collective-permute-done.12.refs_8_.refs_26_), channel_id=1, source_target_pairs={{0,8},{8,0},{16,24},{24,16},{32,40},{40,32},{48,56},{56,48},{64,72... | collective-permute-start | bytes 1179656 | tf_op jit(solution)/shard_map/ppermute | solution.py:47
  144.4 4.3 %collective-permute-start.21 = (bf16[256,1024]{1,0:T(8,128)(2,1)S(1)}, bf16[256,1024]{1,0:T(8,128)(2,1)}, u32[]{:S(2)}, u32[]{:S(2)}) collective-permute-start(bf16[256,1024]{1,0:T(8,128)(2,1)S(1)} %collective-permute-done.13.refs_9_.refs_27_), channel_id=1, source_target_pairs={{0,8},{8,0},{16,24},{24,16},{32,40},{40,32},{48,56},{56,48},{64,72... | collective-permute-start | bytes 1572872 | tf_op jit(solution)/shard_map/ppermute | solution.py:47
  146.2 2.4 collective-permute-start.24
  146.3 2.3 collective-permute-start.22
  147.1 1.6 collective-permute-start.23
  158.9 13.0 %copy-start.17 = (bf16[1024,256]{1,0:T(8,128)(2,1)S(1)}, bf16[1024,256]{1,0:T(8,128)(2,1)}, u32[]{:S(2)}) copy-start(bf16[1024,256]{1,0:T(8,128)(2,1)} %attend.2.refs_1_) | copy-start | bytes 1572868
  158.9 15.9 %collective-permute-start.28 = (bf16[1024,256]{1,0:T(8,128)(2,1)}, bf16[1024,256]{1,0:T(8,128)(2,1)S(1)}, u32[]{:S(2)}, u32[]{:S(2)}) collective-permute-start(bf16[1024,256]{1,0:T(8,128)(2,1)} %attend.2.refs_1_), channel_id=1, source_target_pairs={{0,2},{1,3},{2,4},{3,5},{4,6},{5,7},{6,0},{7,1},{8,10},{9,11},{10,... | collective-permute-start | bytes 1572872 | tf_op jit(solution)/shard_map/ppermute | solution.py:39
  168.8 16.6 %collective-permute-start.27 = (bf16[1024,256]{1,0:T(8,128)(2,1)}, bf16[1024,256]{1,0:T(8,128)(2,1)S(1)}, u32[]{:S(2)}, u32[]{:S(2)}) collective-permute-start(bf16[1024,256]{1,0:T(8,128)(2,1)} %attend.3), channel_id=1, source_target_pairs={{0,1},{1,0},{2,3},{3,2},{4,5},{5,4},{6,7},{7,6},{8,9},{9,8},{10,11... | collective-permute-start | bytes 1572872 | tf_op jit(solution)/shard_map/ppermute | solution.py:43
  171.8 13.9 %collective-permute-start.29 = (bf16[1024,256]{1,0:T(8,128)(2,1)S(1)}, bf16[1024,256]{1,0:T(8,128)(2,1)S(1)}, u32[]{:S(2)}, u32[]{:S(2)}) collective-permute-start(bf16[1024,256]{1,0:T(8,128)(2,1)S(1)} %copy-done.17), channel_id=1, source_target_pairs={{0,6},{1,7},{2,0},{3,1},{4,2},{5,3},{6,4},{7,5},{8,14},{9,15},{10,... | collective-permute-start | bytes 1572872 | tf_op jit(solution)/shard_map/ppermute | solution.py:39
  174.5 21.3 %collective-permute-start.34 = (bf16[1024,256]{1,0:T(8,128)(2,1)S(1)}, bf16[1024,256]{1,0:T(8,128)(2,1)S(1)}, u32[]{:S(2)}, u32[]{:S(2)}) collective-permute-start(bf16[1024,256]{1,0:T(8,128)(2,1)S(1)} %copy-done.17), channel_id=1, source_target_pairs={{0,1},{1,0},{2,3},{3,2},{4,5},{5,4},{6,7},{7,6},{8,9},{9,8},{10,11... | collective-permute-start | bytes 1572872 | tf_op jit(solution)/shard_map/ppermute | solution.py:43
  174.8 22.0 %copy-start.3 = (bf16[1024,256]{1,0:T(8,128)(2,1)}, bf16[1024,256]{1,0:T(8,128)(2,1)S(1)}, u32[]{:S(2)}) copy-start(bf16[1024,256]{1,0:T(8,128)(2,1)S(1)} %collective-permute-done.28.refs_2_) | copy-start | bytes 1572868
  174.8 21.0 %collective-permute-start.35 = (bf16[1024,256]{1,0:T(8,128)(2,1)S(1)}, bf16[1024,256]{1,0:T(8,128)(2,1)S(1)}, u32[]{:S(2)}, u32[]{:S(2)}) collective-permute-start(bf16[1024,256]{1,0:T(8,128)(2,1)S(1)} %collective-permute-done.28.refs_2_), channel_id=1, source_target_pairs={{0,2},{1,3},{2,4},{3,5},{4,6},{5,7},{6,0},{7,1},{8,10},{9,11},{10,... | collective-permute-start | bytes 1572872 | tf_op jit(solution)/shard_map/ppermute | solution.py:39
  196.8 37.3 %collective-permute-start.36 = (bf16[3,1024,256]{2,1,0:T(8,128)(2,1)S(1)}, bf16[3,1024,256]{2,1,0:T(8,128)(2,1)}, u32[]{:S(2)}, u32[]{:S(2)}) collective-permute-start(bf16[3,1024,256]{2,1,0:T(8,128)(2,1)S(1)} %pad_maximum_fusion.1), channel_id=1, source_target_pairs={{0,1},{1,0},{2,3},{3,2},{4,5},{5,4},{6,7},{7,6},{8,9},{9,8},{10,11... | collective-permute-start | bytes 4718600 | tf_op jit(solution)/shard_map/ppermute | solution.py:43
  199.9 42.1 %copy-start.2 = (bf16[2,1024,256]{2,1,0:T(8,128)(2,1)}, bf16[2,1024,256]{2,1,0:T(8,128)(2,1)S(1)}, u32[]{:S(2)}) copy-start(bf16[2,1024,256]{2,1,0:T(8,128)(2,1)S(1)} %pad_maximum_fusion.2.refs_1_) | copy-start | bytes 3145732
  199.9 25.5 %collective-permute-start.30 = (bf16[2,1024,256]{2,1,0:T(8,128)(2,1)S(1)}, bf16[2,1024,256]{2,1,0:T(8,128)(2,1)}, u32[]{:S(2)}, u32[]{:S(2)}) collective-permute-start(bf16[2,1024,256]{2,1,0:T(8,128)(2,1)S(1)} %pad_maximum_fusion.2.refs_1_), channel_id=1, source_target_pairs={{0,2},{1,3},{2,4},{3,5},{4,6},{5,7},{6,0},{7,1},{8,10},{9,11},{10,... | collective-permute-start | bytes 3145736 | tf_op jit(solution)/shard_map/ppermute | solution.py:39
  201.4 25.4 %collective-permute-start.31 = (bf16[2,1024,256]{2,1,0:T(8,128)(2,1)S(1)}, bf16[2,1024,256]{2,1,0:T(8,128)(2,1)}, u32[]{:S(2)}, u32[]{:S(2)}) collective-permute-start(bf16[2,1024,256]{2,1,0:T(8,128)(2,1)S(1)} %pad_maximum_fusion.2.refs_1_), channel_id=1, source_target_pairs={{0,6},{1,7},{2,0},{3,1},{4,2},{5,3},{6,4},{7,5},{8,14},{9,15},{10,... | collective-permute-start | bytes 3145736 | tf_op jit(solution)/shard_map/ppermute | solution.py:39
  226.5 15.6 %collective-permute-start.32 = (bf16[1024,256]{1,0:T(8,128)(2,1)S(1)}, bf16[1024,256]{1,0:T(8,128)(2,1)}, u32[]{:S(2)}, u32[]{:S(2)}) collective-permute-start(bf16[1024,256]{1,0:T(8,128)(2,1)S(1)} %slice_bitcast_fusion.3), channel_id=1, source_target_pairs={{0,2},{1,3},{2,4},{3,5},{4,6},{5,7},{6,0},{7,1},{8,10},{9,11},{10,... | collective-permute-start | bytes 1572872 | tf_op jit(solution)/shard_map/ppermute | solution.py:39
  228.6 13.5 %collective-permute-start.33 = (bf16[1024,256]{1,0:T(8,128)(2,1)}, bf16[1024,256]{1,0:T(8,128)(2,1)}, u32[]{:S(2)}, u32[]{:S(2)}) collective-permute-start(bf16[1024,256]{1,0:T(8,128)(2,1)} %slice_bitcast_fusion.2), channel_id=1, source_target_pairs={{0,6},{1,7},{2,0},{3,1},{4,2},{5,3},{6,4},{7,5},{8,14},{9,15},{10,... | collective-permute-start | bytes 1572872 | tf_op jit(solution)/shard_map/ppermute | solution.py:39
  (17 other events, 87.6 us)
Sparse Core Ops, SparseCore 0:
  96.4 43.1 all-gather.2

commit v4 on v3

--- a/solution.py
+++ b/solution.py
@@ -22,12 +22,12 @@
 F8 = 0
 F9 = 0
 CO = 30
+CX = 0.01
 CA = 9
 C0 = 12
 C1 = 20
 C2 = 8
 F5 = 1
-F6 = 0
 
 
 def cost(us):
@@ -98,13 +98,12 @@
     return pl.BlockSpec(array.shape, lambda *_: zeros)
 
 
-def copy_pieces(where, owner_ref, arrays, x_s, sems, owned):
+def copy_pieces(where, arrays, x_s, sems):
     copies = []
     for number, (array, index) in enumerate(where):
         source = arrays[array] if index is None else arrays[array].at[index]
         depth = source.shape[1]
-        place = owner_ref[number] if owned else number
-        low = pl.multiple_of(place * depth, depth) if owned else number * depth
+        low = number * depth
         copies.append(
             pltpu.make_async_copy(source, x_s.at[:, pl.ds(low, depth)], sems.at[number])
         )
@@ -145,7 +144,7 @@
     rows = x_s.shape[0]
     depth = x_s.shape[1] // len(where)
 
-    copies = copy_pieces(where, owner_ref, arrays, x_s, piece_sems, False)
+    copies = copy_pieces(where, arrays, x_s, piece_sems)
     w_copies = []
     for i, w_ref in enumerate(w_refs):
         for number in range(len(where)):
@@ -429,29 +428,30 @@
     m_s[...] = m_ref[...]
     l_s[...] = l_ref[...]
     a_s[...] = a_ref[...]
-    v_s[:, 128:] = jnp.ones((tokens, 128), BF16)
+    for level in range(1, levels):
+        row = 0
+        for source, low, count, _ in level_blocks(level, unit):
+            k_s[level - 1, row : row + count, :] = k_group[source][low : low + count, :]
+            v_s[level - 1, row : row + count, :128] = v_group[source][low : low + count, :]
+            row += count
+        v_s[level - 1, :, 128:] = jnp.ones((tokens, 128), BF16)
 
     for level in range(1, levels):
         dilation = 2**level
         picked = tokens // dilation
         start = offset_ref[level, head]
-        row = 0
-        for source, low, count, _ in level_blocks(level, unit):
-            k_s[row : row + count, :] = k_group[source][low : low + count, :]
-            v_s[row : row + count, :128] = v_group[source][low : low + count, :]
-            row += count
         order = table_ref[level - 1 : level, :]
         size = min(TILE, picked)
         for number in range(picked // size):
             rows = pl.ds(start + number * size * dilation, size, stride=dilation)
             query = q_f[rows, :].astype(BF16)
-            scores = lax.dot_general(query, k_s[...], NT, preferred_element_type=F32)
+            scores = lax.dot_general(query, k_s[level - 1], NT, preferred_element_type=F32)
             at = lax.broadcasted_iota(jnp.int32, (size, tokens), 0) + number * size
             scores = jnp.where(order <= at, scores, LOW)
             m_old = m_s[rows, :]
             top = jnp.maximum(m_old[:, :1], jnp.max(scores, 1, keepdims=True))
             probs = jnp.exp2(scores - top).astype(BF16)
-            both = jnp.dot(probs, v_s[...], preferred_element_type=F32)
+            both = jnp.dot(probs, v_s[level - 1], preferred_element_type=F32)
             factor = jnp.exp2(m_old - top)
             m_s[rows, :] = jnp.broadcast_to(top, (size, 128))
             a_s[rows, :] = factor * a_s[rows, :] + both[:, :128]
@@ -481,8 +481,8 @@
             out_specs=pl.BlockSpec((tokens, 128), lambda h, offset: (0, h)),
             scratch_shapes=[
                 pltpu.VMEM((tokens, 128), F32),
-                pltpu.VMEM((tokens, 128), BF16),
-                pltpu.VMEM((tokens, 256), BF16),
+                pltpu.VMEM((levels - 1, tokens, 128), BF16),
+                pltpu.VMEM((levels - 1, tokens, 256), BF16),
                 pltpu.VMEM((tokens, 128), F32),
                 pltpu.VMEM((tokens, 128), F32),
                 pltpu.VMEM((tokens, 128), F32),
@@ -495,13 +495,14 @@
     )(offsets, q, *state, *exchanged, *exchanged, table)
 
 
-def output_kernel(where, n_arrays, share, *refs):
+def output_kernel(where, n_arrays, shares, *refs):
     owner_ref, refs = refs[0], refs[1:]
     arrays, refs = refs[:n_arrays], refs[n_arrays:]
     base_ref, w_ref, out_ref, x_s, w_s, piece_sems, w_sems = refs
-    copies = copy_pieces(where, owner_ref, arrays, x_s, piece_sems, True)
-    for i in range(w_s.shape[1]):
-        copies.append(pltpu.make_async_copy(w_ref.at[share + i], w_s.at[:, i], w_sems.at[i]))
+    copies = copy_pieces(where, arrays, x_s, piece_sems)
+    for number, share in enumerate(shares):
+        source = w_ref.at[share : share + w_s.shape[1], owner_ref[number]]
+        copies.append(pltpu.make_async_copy(source, w_s.at[number], w_sems.at[number]))
         copies[-1].start()
     for copy in copies:
         copy.wait()
@@ -516,24 +517,25 @@
         out_ref[at, :] = (base_ref[at, :].astype(F32) + total).astype(out_ref.dtype)
 
 
-def output(pieces, base, w_columns, share, dtype, us):
+def output(parts, base, w_columns, dtype, us):
+    pieces = [piece for part, _ in parts for piece in part]
+    shares = [share for part, share in parts for _ in part]
     operands, where = split_pieces(pieces)
     rows, width = base.shape
-    shares = w_columns.shape[0] // 2
-    depth = w_columns.size // width // 2
+    depth = w_columns.size // width // 16
     anywhere = pl.BlockSpec(memory_space=pl.ANY)
     vector = pl.BlockSpec(memory_space=pltpu.VMEM)
     return pl.pallas_call(
-        functools.partial(output_kernel, where, len(operands), share),
+        functools.partial(output_kernel, where, len(operands), shares),
         in_specs=[pl.BlockSpec(memory_space=pltpu.SMEM)]
         + [anywhere] * len(operands)
         + [vector, anywhere],
         out_specs=vector,
         scratch_shapes=[
-            pltpu.VMEM((rows, depth), BF16),
-            pltpu.VMEM((w_columns.shape[1], shares) + w_columns.shape[2:], BF16),
-            pltpu.SemaphoreType.DMA((8,)),
-            pltpu.SemaphoreType.DMA((shares,)),
+            pltpu.VMEM((rows, len(where) * depth), BF16),
+            pltpu.VMEM((len(where), w_columns.shape[0] // 2) + w_columns.shape[2:], BF16),
+            pltpu.SemaphoreType.DMA((len(where),)),
+            pltpu.SemaphoreType.DMA((len(where),)),
         ],
         out_shape=jax.ShapeDtypeStruct((rows, width), dtype),
         compiler_params=pltpu.CompilerParams(vmem_limit_bytes=VMEM_LIMIT),
@@ -594,8 +596,6 @@
     below_a, above_a, other_a = z_shift(att_a, 1), z_shift(att_a, -1), x_swap(att_a)
     if F5:
         q = after(q, att_a)
-    if F6:
-        q = after(q, below_a)
     att_b = attend(q, state, exchanged, table, offsets, heads // 2)
     far_a = z_shift(below_a, 1)
     other_b = x_swap(att_b)
@@ -617,11 +617,10 @@
         z_first_pieces(att_a, below_a, above_a, far_a, other_a, others_a, other_far_a),
         x_first_pieces(pair_b, below_b, above_b, *far_b),
     ]
-    if F7:
-        total = output(gathered[0], tokens, w_columns, 0, F32, 8)
-        return output(gathered[1], total, w_columns, 4, BF16, CO)
-    total = output(gathered[1], tokens, w_columns, 4, F32, 8)
-    return output(gathered[0], total, w_columns, 0, BF16, CO)
+    heads_a, heads_b = gathered
+    total = output([(heads_a[:4], 0)], tokens, w_columns, F32, CX)
+    total = output([(heads_b[:6], 4)], total, w_columns, F32, CX)
+    return output([(heads_b[6:], 4), (heads_a[4:], 0)], total, w_columns, BF16, CO)
 
 
 def solution(mesh):

time: 258 us -> 250 us (0.969)
  waiting for transfers between devices: 89.8 us -> 76.4 us
  Pallas kernels: 80.4 us -> 84.6 us
  other arithmetic: 2.89 us -> 6 us
  local copies, waits for them, and re-layouts: 16.4 us -> 13.7 us
    ppermute x14, waiting for transfers between devices: 40.3 us -> 31.8 us  [z_shift(): return lax.ppermute(value, 'tp', pairs)]
    ppermute x6, waiting for transfers between devices: 32.6 us -> 27.7 us  [x_swap(): return lax.ppermute(value, 'tp', [(t, t ^ 1) for t in range(8)])]
    pallas_call x2 -> x3, Pallas kernels: 15.9 us -> 20.1 us  [output(): pl.pallas_call(functools.partial(output_kernel, where, len(operands), sha...]
  transfers between devices with their start and end apart: 39 -> 39, of which waited for: 18 -> 18; matrix products, arithmetic and copies ran while one was open for 6% -> 6% of each run, Pallas kernels for 28% -> 31%
where the time goes in v4:
time: 250 us; the launch traced here: 248 us
  Pallas kernels  84.6 us (34%)
  waiting for transfers between devices  76.4 us (31%)
  starting transfers between devices  53.9 us (22%)
  between operations  13.9 us (6%)
  local copies, waits for them, and re-layouts  13.7 us (5%)
  other arithmetic  6 us (2%)
    pallas_call x3, Pallas kernels, project(): pl.pallas_call(functools.partial(project_kernel, where, len(operands), fi...  37.5 us
    ppermute x14, waiting for transfers between devices, z_shift(): return lax.ppermute(value, 'tp', pairs)  31.8 us
    ppermute x6, waiting for transfers between devices, x_swap(): return lax.ppermute(value, 'tp', [(t, t ^ 1) for t in range(8)])  27.7 us
    ppermute x14, starting transfers between devices, z_shift(): return lax.ppermute(value, 'tp', pairs)  21.9 us
    pallas_call x3, Pallas kernels, output(): pl.pallas_call(functools.partial(output_kernel, where, len(operands), sha...  20.1 us
    pallas_call x2, Pallas kernels, attend(): pl.pallas_call(functools.partial(attend_kernel, levels, head_base), grid_...  17.8 us
    ppermute x17, waiting for transfers between devices, seq_swap(): return lax.ppermute(value, 'seq', [(s, s ^ mask) for s in range(16)])  16.9 us
    ppermute x17, starting transfers between devices, seq_swap(): return lax.ppermute(value, 'seq', [(s, s ^ mask) for s in range(16)])  13.2 us
  transfers between devices with their start and end apart: 39, of which 18 were waited for; matrix products, arithmetic and copies ran while one was open for 6% of the time, Pallas kernels for 31%

profile of v4, /device:TPU:0, one launch (start us, length us, event | category | flops | bytes accessed | tf_op | source)
XLA Modules:
  0.0 248.4 jit_solution(879663506403224928)
XLA Ops:
  7.5 2.1 collective-permute-start.1
  9.6 1.2 slice_bitcast_fusion.4
  10.8 3.1 %collective-permute-start = (bf16[768,512]{1,0:T(8,128)(2,1)S(1)}, bf16[768,512]{1,0:T(8,128)(2,1)}, u32[]{:S(2)}, u32[]{:S(2)}) collective-permute-start(bf16[768,512]{1,0:T(8,128)(2,1)S(1)} %get-tuple-element.70), channel_id=1, source_target_pairs={{0,1},{1,0},{2,3},{3,2},{4,5},{5,4},{6,7},{7,6},{8,9},{9,8},{10,11... | collective-permute-start | bytes 2359304 | tf_op jit(solution)/shard_map/ppermute | solution.py:43
  14.0 2.2 collective-permute-start.2
  16.1 1.9 collective-permute-done.1.refs_3_
  18.0 3.6 %collective-permute-done.2.refs_4_ = bf16[256,512]{1,0:T(8,128)(2,1)S(1)} collective-permute-done((bf16[256,512]{1,0:T(8,128)(2,1)S(1)}, bf16[256,512]{1,0:T(8,128)(2,1)S(1)}, u32[]{:S(2)}, u32[]{:S(2)}) %collective-permute-start.2) | collective-permute-done | bytes 262176 | tf_op jit(solution)/shard_map/ppermute | solution.py:39
  21.6 5.2 %collective-permute-done.3.refs_5_ = bf16[256,512]{1,0:T(8,128)(2,1)S(1)} collective-permute-done((bf16[256,512]{1,0:T(8,128)(2,1)S(1)}, bf16[256,512]{1,0:T(8,128)(2,1)S(1)}, u32[]{:S(2)}, u32[]{:S(2)}) %collective-permute-start.3) | collective-permute-done | bytes 262176 | tf_op jit(solution)/shard_map/ppermute | solution.py:39
  26.9 3.0 %collective-permute-start.6 = (bf16[3,256,512]{2,1,0:T(8,128)(2,1)S(1)}, bf16[3,256,512]{2,1,0:T(8,128)(2,1)}, u32[]{:S(2)}, u32[]{:S(2)}) collective-permute-start(bf16[3,256,512]{2,1,0:T(8,128)(2,1)S(1)} %pad_maximum_fusion.3), channel_id=1, source_target_pairs={{0,1},{1,0},{2,3},{3,2},{4,5},{5,4},{6,7},{7,6},{8,9},{9,8},{10,11... | collective-permute-start | bytes 2359304 | tf_op jit(solution)/shard_map/ppermute | solution.py:43
  33.1 1.3 pad_maximum_fusion.refs_2_
  34.4 1.9 collective-permute-start.4
  36.3 1.4 collective-permute-start.8
  39.9 6.0 %all-to-all-start = ((bf16[8,64,512]{2,1,0:T(8,128)(2,1)}), bf16[8,64,512]{2,1,0:T(8,128)(2,1)S(1)}, u32[]{:S(2)}, u32[]{:S(2)}) async-start(bf16[8,64,512]{2,1,0:T(8,128)(2,1)} %copy.33), calls=%async_computation | async-start | bytes 1048576 | tf_op jit(solution)/shard_map/all_to_all | solution.py:554
  46.0 9.5 %collective-permute-done.5.refs_6_ = bf16[256,512]{1,0:T(8,128)(2,1)} collective-permute-done((bf16[256,512]{1,0:T(8,128)(2,1)S(1)}, bf16[256,512]{1,0:T(8,128)(2,1)}, u32[]{:S(2)}, u32[]{:S(2)}) %collective-permute-start.5) | collective-permute-done | bytes 262176 | tf_op jit(solution)/shard_map/ppermute | solution.py:43
  55.5 11.1 %project.3 = (bf16[1024,512]{1,0:T(8,128)(2,1)}, bf16[1024,512]{1,0:T(8,128)(2,1)}, bf16[1024,512]{1,0:T(8,128)(2,1)}, bf16[960,1024]{1,0:T(8,128)(2,1)}, bf16[2...) custom-call(s32[8]{0:T(128)} %stack.134.refs_0_, s32[5,4]{1,0:T(8,128)} %copy.37.refs_1_.refs_0_, ...), custom_call_target="tpu_custom_call" | custom-call | flops 12000000000 | bytes 1024 | tf_op jit(solution)/shard_map/project/pallas_call | solution.py:289
  66.6 7.7 %collective-permute-done.4.refs_3_ = bf16[2,768,512]{2,1,0:T(8,128)(2,1)} collective-permute-done((bf16[2,768,512]{2,1,0:T(8,128)(2,1)S(1)}, bf16[2,768,512]{2,1,0:T(8,128)(2,1)}, u32[]{:S(2)}, u32[]{:S(2)}) %collective-permute-start.4) | collective-permute-done | bytes 1572896 | tf_op jit(solution)/shard_map/ppermute | solution.py:39
  74.3 1.2 slice_bitcast_fusion.1
  75.6 1.2 slice_bitcast_fusion
  76.8 3.3 %collective-permute-start.9 = (bf16[768,512]{1,0:T(8,128)(2,1)S(1)}, bf16[768,512]{1,0:T(8,128)(2,1)S(1)}, u32[]{:S(2)}, u32[]{:S(2)}) collective-permute-start(bf16[768,512]{1,0:T(8,128)(2,1)S(1)} %slice_bitcast_fusion), channel_id=1, source_target_pairs={{0,6},{1,7},{2,0},{3,1},{4,2},{5,3},{6,4},{7,5},{8,14},{9,15},{10,... | collective-permute-start | bytes 2359304 | tf_op jit(solution)/shard_map/ppermute | solution.py:39
  80.0 16.2 %project.4 = (f32[3,768,512]{2,1,0:T(8,128)}, f32[768,128]{1,0:T(8,128)}) custom-call(s32[6]{0:T(128)} %stack.139.refs_0_, s32[5,4]{1,0:T(8,128)} %copy.37.refs_1_.refs_0_, bf16[2,768,512]{2,1,0:T(8,128)(2,1)} %copy-done.7, bf16[2,768,512]{2,1,0:T(8,128)(2,1)} %collective-permute-done.4.refs_3_, bf16[2,768,512]{2,1,0:T(8,128)(2,1)} %collective-permute-done.8.refs_4_, ...), custom_call_target="tpu_custom_call" | custom-call | flops 20000000000 | bytes 1024 | tf_op jit(solution)/shard_map/project/pallas_call | solution.py:289
  97.8 10.2 %project.5 = (bf16[1024,512]{1,0:T(8,128)(2,1)}, bf16[1024,512]{1,0:T(8,128)(2,1)}, bf16[1024,512]{1,0:T(8,128)(2,1)}, bf16[960,1024]{1,0:T(8,128)(2,1)}, bf16[2...) custom-call(s32[2]{0:T(128)} %pad_add_fusion.2.refs_0_, ...), custom_call_target="tpu_custom_call", output_to_operand_aliasing={{0}: (10, {}), {1}: (11, {}), {2}: (12, {}), {3}: (13, {}),... | custom-call | flops 8000000000 | bytes 1024 | tf_op jit(solution)/shard_map/project/pallas_call | solution.py:289
  108.0 1.4 collective-permute-start.11
  109.4 1.6 collective-permute-start.12
  111.8 2.9 %collective-permute-start.14 = (bf16[64,1024]{1,0:T(8,128)(2,1)}, bf16[64,1024]{1,0:T(8,128)(2,1)S(1)}, u32[]{:S(2)}, u32[]{:S(2)}) collective-permute-start(bf16[64,1024]{1,0:T(8,128)(2,1)} %get-tuple-element.62), channel_id=1, source_target_pairs={{0,64},{8,72},{16,80},{24,88},{32,96},{40,104},{48,112},{56,120},{... | collective-permute-start | bytes 393224 | tf_op jit(solution)/shard_map/ppermute | solution.py:47
  114.7 9.3 %attend_local.1 = (f32[1024,512]{1,0:T(8,128)}, f32[1024,512]{1,0:T(8,128)}, f32[1024,512]{1,0:T(8,128)}) custom-call(bf16[1024,512]{1,0:T(8,128)(2,1)} %get-tuple-element.65.q_ref.refs_1_, bf16[1024,512]{1,0:T(8,128)(2,1)} %get-tuple-element.51.k_ref, bf16[1024,512]{1,0:T(8,128)(2,1)} %get-tuple-element.52.v_ref), custom_call_target="tpu_custom_call" | custom-call | flops 8999999488 | bytes 1024 | tf_op jit(solution)/shard_map/attend_local/pallas_call | solution.py:407
  124.3 4.5 %collective-permute-done.12.refs_8_.refs_26_ = bf16[192,1024]{1,0:T(8,128)(2,1)} collective-permute-done((bf16[192,1024]{1,0:T(8,128)(2,1)}, bf16[192,1024]{1,0:T(8,128)(2,1)}, u32[]{:S(2)}, u32[]{:S(2)}) %collective-permute-start.12) | collective-permute-done | bytes 393248 | tf_op jit(solution)/shard_map/ppermute | solution.py:47
  128.8 3.4 %collective-permute-start.17 = (bf16[64,1024]{1,0:T(8,128)(2,1)S(1)}, bf16[64,1024]{1,0:T(8,128)(2,1)S(1)}, u32[]{:S(2)}, u32[]{:S(2)}) collective-permute-start(bf16[64,1024]{1,0:T(8,128)(2,1)S(1)} %slice.25), channel_id=1, source_target_pairs={{0,64},{8,72},{16,80},{24,88},{32,96},{40,104},{48,112},{56,120},{... | collective-permute-start | bytes 393224 | tf_op jit(solution)/shard_map/ppermute | solution.py:47
  132.3 4.6 %collective-permute-done.14.refs_10_.refs_28_ = bf16[64,1024]{1,0:T(8,128)(2,1)S(1)} collective-permute-done((bf16[64,1024]{1,0:T(8,128)(2,1)}, bf16[64,1024]{1,0:T(8,128)(2,1)S(1)}, u32[]{:S(2)}, u32[]{:S(2)}) %collective-permute-start.14) | collective-permute-done | bytes 131104 | tf_op jit(solution)/shard_map/ppermute | solution.py:47
  137.7 3.3 %collective-permute-done.17.refs_13_.refs_31_ = bf16[64,1024]{1,0:T(8,128)(2,1)S(1)} collective-permute-done((bf16[64,1024]{1,0:T(8,128)(2,1)S(1)}, bf16[64,1024]{1,0:T(8,128)(2,1)S(1)}, u32[]{:S(2)}, u32[]{:S(2)}) %collective-permute-start.17) | collective-permute-done | bytes 131104 | tf_op jit(solution)/shard_map/ppermute | solution.py:47
  141.1 1.9 collective-permute-done.18.refs_14_.refs_32_
  144.5 1.7 collective-permute-done.15.refs_12_.refs_30_
  148.7 1.2 copy-done.16
  150.0 8.9 %attend.2.refs_1_ = bf16[1024,256]{1,0:T(8,128)(2,1)} custom-call(s32[5,4]{1,0:T(8,128)} %copy.37.refs_1_.refs_0_, bf16[1024,512]{1,0:T(8,128)(2,1)} %get-tuple-element.65.q_ref.refs_1_, f32[1024,512]{1,0:T(8,128)} %get-tuple-element.53.refs_2_, f32[1024,512]{1,0:T(8,128)} %get-tuple-element.54.refs_3_, f32[1024,512]{1,0:T(8,128)} %get-tuple-element.55.refs_4_, ...), custom_call_target="tpu_custom_call" | custom-call | flops 8999999488 | bytes 1024 | tf_op jit(solution)/shard_map/attend/pallas_call | solution.py:472
  159.8 8.9 %attend.3 = bf16[1024,256]{1,0:T(8,128)(2,1)} custom-call(s32[5,4]{1,0:T(8,128)} %copy.37.refs_1_.refs_0_, bf16[1024,512]{1,0:T(8,128)(2,1)} %get-tuple-element.65.q_ref.refs_1_, f32[1024,512]{1,0:T(8,128)} %get-tuple-element.53.refs_2_, f32[1024,512]{1,0:T(8,128)} %get-tuple-element.54.refs_3_, f32[1024,512]{1,0:T(8,128)} %get-tuple-element.55.refs_4_, ...), custom_call_target="tpu_custom_call" | custom-call | flops 8999999488 | bytes 1024 | tf_op jit(solution)/shard_map/attend/pallas_call | solution.py:472
  168.7 2.9 %collective-permute-start.27 = (bf16[1024,256]{1,0:T(8,128)(2,1)}, bf16[1024,256]{1,0:T(8,128)(2,1)S(1)}, u32[]{:S(2)}, u32[]{:S(2)}) collective-permute-start(bf16[1024,256]{1,0:T(8,128)(2,1)} %attend.3), channel_id=1, source_target_pairs={{0,1},{1,0},{2,3},{3,2},{4,5},{5,4},{6,7},{7,6},{8,9},{9,8},{10,11... | collective-permute-start | bytes 1572872 | tf_op jit(solution)/shard_map/ppermute | solution.py:43
  171.5 2.9 %collective-permute-start.29 = (bf16[1024,256]{1,0:T(8,128)(2,1)S(1)}, bf16[1024,256]{1,0:T(8,128)(2,1)S(1)}, u32[]{:S(2)}, u32[]{:S(2)}) collective-permute-start(bf16[1024,256]{1,0:T(8,128)(2,1)S(1)} %copy-done.8), channel_id=1, source_target_pairs={{0,6},{1,7},{2,0},{3,1},{4,2},{5,3},{6,4},{7,5},{8,14},{9,15},{10,... | collective-permute-start | bytes 1572872 | tf_op jit(solution)/shard_map/ppermute | solution.py:39
  174.7 10.5 %collective-permute-done.27 = bf16[1024,256]{1,0:T(8,128)(2,1)S(1)} collective-permute-done((bf16[1024,256]{1,0:T(8,128)(2,1)}, bf16[1024,256]{1,0:T(8,128)(2,1)S(1)}, u32[]{:S(2)}, u32[]{:S(2)}) %collective-permute-start.27) | collective-permute-done | bytes 524320 | tf_op jit(solution)/shard_map/ppermute | solution.py:43
  185.6 1.3 pad_maximum_fusion.2.refs_1_
  187.0 1.8 collective-permute-start.30
  188.8 2.1 collective-permute-start.32
  190.8 4.9 %collective-permute-done.34.refs_3_ = bf16[1024,256]{1,0:T(8,128)(2,1)S(1)} collective-permute-done((bf16[1024,256]{1,0:T(8,128)(2,1)S(1)}, bf16[1024,256]{1,0:T(8,128)(2,1)S(1)}, u32[]{:S(2)}, u32[]{:S(2)}) %collective-permute-start.34) | collective-permute-done | bytes 524320 | tf_op jit(solution)/shard_map/ppermute | solution.py:43
  195.7 1.5 pad_maximum_fusion.1
  197.2 2.9 %collective-permute-start.36 = (bf16[3,1024,256]{2,1,0:T(8,128)(2,1)}, bf16[3,1024,256]{2,1,0:T(8,128)(2,1)}, u32[]{:S(2)}, u32[]{:S(2)}) collective-permute-start(bf16[3,1024,256]{2,1,0:T(8,128)(2,1)} %pad_maximum_fusion.1), channel_id=1, source_target_pairs={{0,1},{1,0},{2,3},{3,2},{4,5},{5,4},{6,7},{7,6},{8,9},{9,8},{10,11... | collective-permute-start | bytes 4718600 | tf_op jit(solution)/shard_map/ppermute | solution.py:43
  200.1 12.9 %collective-permute-done.30.refs_2_ = bf16[2,1024,256]{2,1,0:T(8,128)(2,1)S(1)} collective-permute-done((bf16[2,1024,256]{2,1,0:T(8,128)(2,1)S(1)}, bf16[2,1024,256]{2,1,0:T(8,128)(2,1)S(1)}, u32[]{:S(2)}, u32[]{:S(2)}) %collective-permute-start.30) | collective-permute-done | bytes 1048608 | tf_op jit(solution)/shard_map/ppermute | solution.py:39
  214.1 3.3 %collective-permute-start.33 = (bf16[1024,256]{1,0:T(8,128)(2,1)S(1)}, bf16[1024,256]{1,0:T(8,128)(2,1)S(1)}, u32[]{:S(2)}, u32[]{:S(2)}) collective-permute-start(bf16[1024,256]{1,0:T(8,128)(2,1)S(1)} %slice_bitcast_fusion.2), channel_id=1, source_target_pairs={{0,6},{1,7},{2,0},{3,1},{4,2},{5,3},{6,4},{7,5},{8,14},{9,15},{10,... | collective-permute-start | bytes 1572872 | tf_op jit(solution)/shard_map/ppermute | solution.py:39
  218.6 5.9 %output.3.refs_4_ = f32[1024,512]{1,0:T(8,128)} custom-call(s32[4]{0:T(128)} %pad_add_fusion.3.refs_0_, bf16[1024,256]{1,0:T(8,128)(2,1)} %attend.2.refs_1_, bf16[1024,256]{1,0:T(8,128)(2,1)} %copy-done.4, bf16[1024,256]{1,0:T(8,128)(2,1)} %copy-done.5, bf16[1024,256]{1,0:T(8,128)(2,1)} %copy-done.6, bf16[1024,512]{1,0:T(8,128)(2,1)} %refs_5_.3, ...), custom_call_target="tpu_custom_call" | custom-call | flops 10000000 | bytes 1024 | tf_op jit(solution)/shard_map/output/pallas_call | solution.py:528
  224.5 7.3 %output.4.refs_5_ = f32[1024,512]{1,0:T(8,128)} custom-call(s32[6]{0:T(128)} %stack.139.refs_0_, bf16[2,1024,256]{2,1,0:T(8,128)(2,1)} %copy-done, bf16[2,1024,256]{2,1,0:T(8,128)(2,1)} %copy-done.1, bf16[2,1024,256]{2,1,0:T(8,128)(2,1)} %copy-done.2, f32[1024,512]{1,0:T(8,128)} %output.3.refs_4_, bf16[8,8,64,512]{3,2,1,0:T(8,128)(2,1)} %bitcast.37), custom_call_target="tpu_custom_call" | custom-call | flops 10000000 | bytes 1024 | tf_op jit(solution)/shard_map/output/pallas_call | solution.py:528
  231.9 2.8 %collective-permute-done.36.refs_4_ = bf16[3,1024,256]{2,1,0:T(8,128)(2,1)} collective-permute-done((bf16[3,1024,256]{2,1,0:T(8,128)(2,1)}, bf16[3,1024,256]{2,1,0:T(8,128)(2,1)}, u32[]{:S(2)}, u32[]{:S(2)}) %collective-permute-start.36) | collective-permute-done | bytes 1572896 | tf_op jit(solution)/shard_map/ppermute | solution.py:43
  234.6 6.9 %output.5 = bf16[1024,512]{1,0:T(8,128)(2,1)} custom-call(s32[6]{0:T(128)} %stack.126.refs_0_, bf16[1024,256]{1,0:T(8,128)(2,1)} %collective-permute-done.31.refs_1_, bf16[1024,256]{1,0:T(8,128)(2,1)} %copy-done.20, bf16[1024,256]{1,0:T(8,128)(2,1)} %copy-done.19, bf16[3,1024,256]{2,1,0:T(8,128)(2,1)} %collective-permute-done.36.refs_4_, ...), custom_call_target="tpu_custom_call" | custom-call | flops 30000001024 | bytes 1024 | tf_op jit(solution)/shard_map/output/pallas_call | solution.py:528
  (139 shorter events, 17.9 us)
Async XLA Ops:
  7.5 22.4 %copy-start.9 = (bf16[256,512]{1,0:T(8,128)(2,1)}, bf16[256,512]{1,0:T(8,128)(2,1)S(1)}, u32[]{:S(2)}) copy-start(bf16[256,512]{1,0:T(8,128)(2,1)S(1)} %slice.22.refs_2_) | copy-start | bytes 786436
  7.5 23.0 %copy-start.15 = (s32[5,4]{0,1:T(4,128)S(1)}, s32[5,4]{0,1:T(4,128)}, u32[]{:S(2)}) copy-start(s32[5,4]{0,1:T(4,128)} %param.13) | copy-start | bytes 244
  7.5 23.7 %copy-start.14 = (f32[4096]{0:T(1024)S(1)}, f32[4096]{0:T(1024)}, u32[]{:S(2)}) copy-start(f32[4096]{0:T(1024)} %param.8) | copy-start | bytes 49156
  7.5 10.5 %collective-permute-start.1 = (bf16[256,512]{1,0:T(8,128)(2,1)S(1)}, bf16[256,512]{1,0:T(8,128)(2,1)S(1)}, u32[]{:S(2)}, u32[]{:S(2)}) collective-permute-start(bf16[256,512]{1,0:T(8,128)(2,1)S(1)} %slice.22.refs_2_), channel_id=1, source_target_pairs={{0,2},{1,3},{2,4},{3,5},{4,6},{5,7},{6,0},{7,1},{8,10},{9,11},{10,... | collective-permute-start | bytes 786440 | tf_op jit(solution)/shard_map/ppermute | solution.py:39
  10.8 22.2 %collective-permute-start = (bf16[768,512]{1,0:T(8,128)(2,1)S(1)}, bf16[768,512]{1,0:T(8,128)(2,1)}, u32[]{:S(2)}, u32[]{:S(2)}) collective-permute-start(bf16[768,512]{1,0:T(8,128)(2,1)S(1)} %get-tuple-element.70), channel_id=1, source_target_pairs={{0,1},{1,0},{2,3},{3,2},{4,5},{5,4},{6,7},{7,6},{8,9},{9,8},{10,11... | collective-permute-start | bytes 2359304 | tf_op jit(solution)/shard_map/ppermute | solution.py:43
  14.0 7.7 %collective-permute-start.2 = (bf16[256,512]{1,0:T(8,128)(2,1)S(1)}, bf16[256,512]{1,0:T(8,128)(2,1)S(1)}, u32[]{:S(2)}, u32[]{:S(2)}) collective-permute-start(bf16[256,512]{1,0:T(8,128)(2,1)S(1)} %slice.22.refs_2_), channel_id=1, source_target_pairs={{0,6},{1,7},{2,0},{3,1},{4,2},{5,3},{6,4},{7,5},{8,14},{9,15},{10,... | collective-permute-start | bytes 786440 | tf_op jit(solution)/shard_map/ppermute | solution.py:39
  18.0 8.8 %collective-permute-start.3 = (bf16[256,512]{1,0:T(8,128)(2,1)S(1)}, bf16[256,512]{1,0:T(8,128)(2,1)S(1)}, u32[]{:S(2)}, u32[]{:S(2)}) collective-permute-start(bf16[256,512]{1,0:T(8,128)(2,1)S(1)} %collective-permute-done.1.refs_3_), channel_id=1, source_target_pairs={{0,2},{1,3},{2,4},{3,5},{4,6},{5,7},{6,0},{7,1},{8,10},{9,11},{10,... | collective-permute-start | bytes 786440 | tf_op jit(solution)/shard_map/ppermute | solution.py:39
  26.9 28.5 %collective-permute-start.6 = (bf16[3,256,512]{2,1,0:T(8,128)(2,1)S(1)}, bf16[3,256,512]{2,1,0:T(8,128)(2,1)}, u32[]{:S(2)}, u32[]{:S(2)}) collective-permute-start(bf16[3,256,512]{2,1,0:T(8,128)(2,1)S(1)} %pad_maximum_fusion.3), channel_id=1, source_target_pairs={{0,1},{1,0},{2,3},{3,2},{4,5},{5,4},{6,7},{7,6},{8,9},{9,8},{10,11... | collective-permute-start | bytes 2359304 | tf_op jit(solution)/shard_map/ppermute | solution.py:43
  29.9 25.5 %collective-permute-start.5 = (bf16[256,512]{1,0:T(8,128)(2,1)S(1)}, bf16[256,512]{1,0:T(8,128)(2,1)}, u32[]{:S(2)}, u32[]{:S(2)}) collective-permute-start(bf16[256,512]{1,0:T(8,128)(2,1)S(1)} %slice.22.refs_2_), channel_id=1, source_target_pairs={{0,1},{1,0},{2,3},{3,2},{4,5},{5,4},{6,7},{7,6},{8,9},{9,8},{10,11... | collective-permute-start | bytes 786440 | tf_op jit(solution)/shard_map/ppermute | solution.py:43
  34.4 39.9 %collective-permute-start.4 = (bf16[2,768,512]{2,1,0:T(8,128)(2,1)S(1)}, bf16[2,768,512]{2,1,0:T(8,128)(2,1)}, u32[]{:S(2)}, u32[]{:S(2)}) collective-permute-start(bf16[2,768,512]{2,1,0:T(8,128)(2,1)S(1)} %pad_maximum_fusion.refs_2_), channel_id=1, source_target_pairs={{0,2},{1,3},{2,4},{3,5},{4,6},{5,7},{6,0},{7,1},{8,10},{9,11},{10,... | collective-permute-start | bytes 4718600 | tf_op jit(solution)/shard_map/ppermute | solution.py:39
  36.3 39.3 %collective-permute-start.8 = (bf16[2,768,512]{2,1,0:T(8,128)(2,1)S(1)}, bf16[2,768,512]{2,1,0:T(8,128)(2,1)}, u32[]{:S(2)}, u32[]{:S(2)}) collective-permute-start(bf16[2,768,512]{2,1,0:T(8,128)(2,1)S(1)} %pad_maximum_fusion.refs_2_), channel_id=1, source_target_pairs={{0,6},{1,7},{2,0},{3,1},{4,2},{5,3},{6,4},{7,5},{8,14},{9,15},{10,... | collective-permute-start | bytes 4718600 | tf_op jit(solution)/shard_map/ppermute | solution.py:39
  39.9 40.1 %all-to-all-start = ((bf16[8,64,512]{2,1,0:T(8,128)(2,1)}), bf16[8,64,512]{2,1,0:T(8,128)(2,1)S(1)}, u32[]{:S(2)}, u32[]{:S(2)}) async-start(bf16[8,64,512]{2,1,0:T(8,128)(2,1)} %copy.33), calls=%async_computation | async-start | bytes 1048576 | tf_op jit(solution)/shard_map/all_to_all | solution.py:554
  45.9 172.7 %all-gather.3.cloned.1.call-start = ((), (), s32[]{:S(2)}) async-start(), calls=%async_computation.1 | async-start | bytes 4718592 | tf_op jit(solution)/shard_map/all_gather | solution.py:559
  75.5 21.4 %collective-permute-start.7 = (bf16[768,512]{1,0:T(8,128)(2,1)S(1)}, bf16[768,512]{1,0:T(8,128)(2,1)}, u32[]{:S(2)}, u32[]{:S(2)}) collective-permute-start(bf16[768,512]{1,0:T(8,128)(2,1)S(1)} %slice_bitcast_fusion.1), channel_id=1, source_target_pairs={{0,2},{1,3},{2,4},{3,5},{4,6},{5,7},{6,0},{7,1},{8,10},{9,11},{10,... | collective-permute-start | bytes 2359304 | tf_op jit(solution)/shard_map/ppermute | solution.py:39
  76.8 20.1 %collective-permute-start.9 = (bf16[768,512]{1,0:T(8,128)(2,1)S(1)}, bf16[768,512]{1,0:T(8,128)(2,1)S(1)}, u32[]{:S(2)}, u32[]{:S(2)}) collective-permute-start(bf16[768,512]{1,0:T(8,128)(2,1)S(1)} %slice_bitcast_fusion), channel_id=1, source_target_pairs={{0,6},{1,7},{2,0},{3,1},{4,2},{5,3},{6,4},{7,5},{8,14},{9,15},{10,... | collective-permute-start | bytes 2359304 | tf_op jit(solution)/shard_map/ppermute | solution.py:39
  80.0 16.2 %copy-start.3 = (bf16[8,64,512]{2,1,0:T(8,128)(2,1)}, bf16[8,64,512]{2,1,0:T(8,128)(2,1)S(1)}, u32[]{:S(2)}) copy-start(bf16[8,64,512]{2,1,0:T(8,128)(2,1)S(1)} %all-to-all-done) | copy-start | bytes 1572868
  108.0 16.0 %collective-permute-start.11 = (bf16[192,1024]{1,0:T(8,128)(2,1)}, bf16[192,1024]{1,0:T(8,128)(2,1)S(1)}, u32[]{:S(2)}, u32[]{:S(2)}) collective-permute-start(bf16[192,1024]{1,0:T(8,128)(2,1)} %get-tuple-element.57), channel_id=1, source_target_pairs={{0,16},{8,24},{16,0},{24,8},{32,48},{40,56},{48,32},{56,40},{64,80... | collective-permute-start | bytes 1179656 | tf_op jit(solution)/shard_map/ppermute | solution.py:47
  109.4 19.4 %collective-permute-start.12 = (bf16[192,1024]{1,0:T(8,128)(2,1)}, bf16[192,1024]{1,0:T(8,128)(2,1)}, u32[]{:S(2)}, u32[]{:S(2)}) collective-permute-start(bf16[192,1024]{1,0:T(8,128)(2,1)} %get-tuple-element.57), channel_id=1, source_target_pairs={{0,32},{8,40},{16,48},{24,56},{32,0},{40,8},{48,16},{56,24},{64,96... | collective-permute-start | bytes 1179656 | tf_op jit(solution)/shard_map/ppermute | solution.py:47
  111.0 37.7 %collective-permute-start.10 = (bf16[960,1024]{1,0:T(8,128)(2,1)}, bf16[960,1024]{1,0:T(8,128)(2,1)S(1)}, u32[]{:S(2)}, u32[]{:S(2)}) collective-permute-start(bf16[960,1024]{1,0:T(8,128)(2,1)} %get-tuple-element.56.refs_5_.refs_23_), channel_id=1, source_target_pairs={{0,8},{8,0},{16,24},{24,16},{32,40},{40,32},{48,56},{56,48},{64,72... | collective-permute-start | bytes 5898248 | tf_op jit(solution)/shard_map/ppermute | solution.py:47
  111.0 32.1 %collective-permute-start.13 = (bf16[256,1024]{1,0:T(8,128)(2,1)}, bf16[256,1024]{1,0:T(8,128)(2,1)S(1)}, u32[]{:S(2)}, u32[]{:S(2)}) collective-permute-start(bf16[256,1024]{1,0:T(8,128)(2,1)} %get-tuple-element.60), channel_id=1, source_target_pairs={{0,16},{8,24},{16,0},{24,8},{32,48},{40,56},{48,32},{56,40},{64,80... | collective-permute-start | bytes 1572872 | tf_op jit(solution)/shard_map/ppermute | solution.py:47
  111.8 25.0 %collective-permute-start.14 = (bf16[64,1024]{1,0:T(8,128)(2,1)}, bf16[64,1024]{1,0:T(8,128)(2,1)S(1)}, u32[]{:S(2)}, u32[]{:S(2)}) collective-permute-start(bf16[64,1024]{1,0:T(8,128)(2,1)} %get-tuple-element.62), channel_id=1, source_target_pairs={{0,64},{8,72},{16,80},{24,88},{32,96},{40,104},{48,112},{56,120},{... | collective-permute-start | bytes 393224 | tf_op jit(solution)/shard_map/ppermute | solution.py:47
  124.0 24.7 %copy-start.13 = (bf16[192,1024]{1,0:T(8,128)(2,1)}, bf16[192,1024]{1,0:T(8,128)(2,1)S(1)}, u32[]{:S(2)}) copy-start(bf16[192,1024]{1,0:T(8,128)(2,1)S(1)} %collective-permute-done.11.refs_7_.refs_25_) | copy-start | bytes 1179652
  124.0 12.9 %collective-permute-start.16 = (bf16[64,1024]{1,0:T(8,128)(2,1)}, bf16[64,1024]{1,0:T(8,128)(2,1)S(1)}, u32[]{:S(2)}, u32[]{:S(2)}) collective-permute-start(bf16[64,1024]{1,0:T(8,128)(2,1)} %get-tuple-element.62), channel_id=1, source_target_pairs={{0,96},{8,104},{16,112},{24,120},{32,64},{40,72},{48,80},{56,88},{... | collective-permute-start | bytes 393224 | tf_op jit(solution)/shard_map/ppermute | solution.py:47
  128.8 12.2 %collective-permute-start.17 = (bf16[64,1024]{1,0:T(8,128)(2,1)S(1)}, bf16[64,1024]{1,0:T(8,128)(2,1)S(1)}, u32[]{:S(2)}, u32[]{:S(2)}) collective-permute-start(bf16[64,1024]{1,0:T(8,128)(2,1)S(1)} %slice.25), channel_id=1, source_target_pairs={{0,64},{8,72},{16,80},{24,88},{32,96},{40,104},{48,112},{56,120},{... | collective-permute-start | bytes 393224 | tf_op jit(solution)/shard_map/ppermute | solution.py:47
  136.8 6.2 %collective-permute-start.18 = (bf16[64,1024]{1,0:T(8,128)(2,1)S(1)}, bf16[64,1024]{1,0:T(8,128)(2,1)S(1)}, u32[]{:S(2)}, u32[]{:S(2)}) collective-permute-start(bf16[64,1024]{1,0:T(8,128)(2,1)S(1)} %slice.25), channel_id=1, source_target_pairs={{0,96},{8,104},{16,112},{24,120},{32,64},{40,72},{48,80},{56,88},{... | collective-permute-start | bytes 393224 | tf_op jit(solution)/shard_map/ppermute | solution.py:47
  136.9 9.3 %collective-permute-start.15 = (bf16[192,1024]{1,0:T(8,128)(2,1)S(1)}, bf16[192,1024]{1,0:T(8,128)(2,1)}, u32[]{:S(2)}, u32[]{:S(2)}) collective-permute-start(bf16[192,1024]{1,0:T(8,128)(2,1)S(1)} %collective-permute-done.11.refs_7_.refs_25_), channel_id=1, source_target_pairs={{0,32},{8,40},{16,48},{24,56},{32,0},{40,8},{48,16},{56,24},{64,96... | collective-permute-start | bytes 1179656 | tf_op jit(solution)/shard_map/ppermute | solution.py:47
  141.1 2.6 %collective-permute-start.25 = (bf16[64,1024]{1,0:T(8,128)(2,1)S(1)}, bf16[64,1024]{1,0:T(8,128)(2,1)}, u32[]{:S(2)}, u32[]{:S(2)}) collective-permute-start(bf16[64,1024]{1,0:T(8,128)(2,1)S(1)} %collective-permute-done.17.refs_13_.refs_31_), channel_id=1, source_target_pairs={{0,8},{8,0},{16,24},{24,16},{32,40},{40,32},{48,56},{56,48},{64,72... | collective-permute-start | bytes 393224 | tf_op jit(solution)/shard_map/ppermute | solution.py:47
  143.0 1.3 collective-permute-start.26
  143.1 3.2 %collective-permute-start.19 = (bf16[192,1024]{1,0:T(8,128)(2,1)S(1)}, bf16[192,1024]{1,0:T(8,128)(2,1)S(1)}, u32[]{:S(2)}, u32[]{:S(2)}) collective-permute-start(bf16[192,1024]{1,0:T(8,128)(2,1)S(1)} %collective-permute-done.11.refs_7_.refs_25_), channel_id=1, source_target_pairs={{0,8},{8,0},{16,24},{24,16},{32,40},{40,32},{48,56},{56,48},{64,72... | collective-permute-start | bytes 1179656 | tf_op jit(solution)/shard_map/ppermute | solution.py:47
  143.6 3.3 %collective-permute-start.20 = (bf16[192,1024]{1,0:T(8,128)(2,1)}, bf16[192,1024]{1,0:T(8,128)(2,1)S(1)}, u32[]{:S(2)}, u32[]{:S(2)}) collective-permute-start(bf16[192,1024]{1,0:T(8,128)(2,1)} %collective-permute-done.12.refs_8_.refs_26_), channel_id=1, source_target_pairs={{0,8},{8,0},{16,24},{24,16},{32,40},{40,32},{48,56},{56,48},{64,72... | collective-permute-start | bytes 1179656 | tf_op jit(solution)/shard_map/ppermute | solution.py:47
  144.4 4.3 %collective-permute-start.21 = (bf16[256,1024]{1,0:T(8,128)(2,1)S(1)}, bf16[256,1024]{1,0:T(8,128)(2,1)}, u32[]{:S(2)}, u32[]{:S(2)}) collective-permute-start(bf16[256,1024]{1,0:T(8,128)(2,1)S(1)} %collective-permute-done.13.refs_9_.refs_27_), channel_id=1, source_target_pairs={{0,8},{8,0},{16,24},{24,16},{32,40},{40,32},{48,56},{56,48},{64,72... | collective-permute-start | bytes 1572872 | tf_op jit(solution)/shard_map/ppermute | solution.py:47
  146.2 2.4 collective-permute-start.24
  146.3 2.2 collective-permute-start.22
  147.0 1.6 collective-permute-start.23
  158.9 15.9 %collective-permute-start.28 = (bf16[1024,256]{1,0:T(8,128)(2,1)}, bf16[1024,256]{1,0:T(8,128)(2,1)S(1)}, u32[]{:S(2)}, u32[]{:S(2)}) collective-permute-start(bf16[1024,256]{1,0:T(8,128)(2,1)} %attend.2.refs_1_), channel_id=1, source_target_pairs={{0,2},{1,3},{2,4},{3,5},{4,6},{5,7},{6,0},{7,1},{8,10},{9,11},{10,... | collective-permute-start | bytes 1572872 | tf_op jit(solution)/shard_map/ppermute | solution.py:39
  168.7 16.6 %collective-permute-start.27 = (bf16[1024,256]{1,0:T(8,128)(2,1)}, bf16[1024,256]{1,0:T(8,128)(2,1)S(1)}, u32[]{:S(2)}, u32[]{:S(2)}) collective-permute-start(bf16[1024,256]{1,0:T(8,128)(2,1)} %attend.3), channel_id=1, source_target_pairs={{0,1},{1,0},{2,3},{3,2},{4,5},{5,4},{6,7},{7,6},{8,9},{9,8},{10,11... | collective-permute-start | bytes 1572872 | tf_op jit(solution)/shard_map/ppermute | solution.py:43
  171.5 14.1 %collective-permute-start.29 = (bf16[1024,256]{1,0:T(8,128)(2,1)S(1)}, bf16[1024,256]{1,0:T(8,128)(2,1)S(1)}, u32[]{:S(2)}, u32[]{:S(2)}) collective-permute-start(bf16[1024,256]{1,0:T(8,128)(2,1)S(1)} %copy-done.8), channel_id=1, source_target_pairs={{0,6},{1,7},{2,0},{3,1},{4,2},{5,3},{6,4},{7,5},{8,14},{9,15},{10,... | collective-permute-start | bytes 1572872 | tf_op jit(solution)/shard_map/ppermute | solution.py:39
  174.4 21.3 %collective-permute-start.34 = (bf16[1024,256]{1,0:T(8,128)(2,1)S(1)}, bf16[1024,256]{1,0:T(8,128)(2,1)S(1)}, u32[]{:S(2)}, u32[]{:S(2)}) collective-permute-start(bf16[1024,256]{1,0:T(8,128)(2,1)S(1)} %copy-done.8), channel_id=1, source_target_pairs={{0,1},{1,0},{2,3},{3,2},{4,5},{5,4},{6,7},{7,6},{8,9},{9,8},{10,11... | collective-permute-start | bytes 1572872 | tf_op jit(solution)/shard_map/ppermute | solution.py:43
  174.7 22.5 %copy-start.4 = (bf16[1024,256]{1,0:T(8,128)(2,1)}, bf16[1024,256]{1,0:T(8,128)(2,1)S(1)}, u32[]{:S(2)}) copy-start(bf16[1024,256]{1,0:T(8,128)(2,1)S(1)} %collective-permute-done.28.refs_2_) | copy-start | bytes 1572868
  174.7 21.0 %collective-permute-start.35 = (bf16[1024,256]{1,0:T(8,128)(2,1)S(1)}, bf16[1024,256]{1,0:T(8,128)(2,1)S(1)}, u32[]{:S(2)}, u32[]{:S(2)}) collective-permute-start(bf16[1024,256]{1,0:T(8,128)(2,1)S(1)} %collective-permute-done.28.refs_2_), channel_id=1, source_target_pairs={{0,2},{1,3},{2,4},{3,5},{4,6},{5,7},{6,0},{7,1},{8,10},{9,11},{10,... | collective-permute-start | bytes 1572872 | tf_op jit(solution)/shard_map/ppermute | solution.py:39
  187.0 27.0 %copy-start = (bf16[2,1024,256]{2,1,0:T(8,128)(2,1)}, bf16[2,1024,256]{2,1,0:T(8,128)(2,1)S(1)}, u32[]{:S(2)}) copy-start(bf16[2,1024,256]{2,1,0:T(8,128)(2,1)S(1)} %pad_maximum_fusion.2.refs_1_) | copy-start | bytes 3145732
  187.0 26.1 %collective-permute-start.30 = (bf16[2,1024,256]{2,1,0:T(8,128)(2,1)S(1)}, bf16[2,1024,256]{2,1,0:T(8,128)(2,1)S(1)}, u32[]{:S(2)}, u32[]{:S(2)}) collective-permute-start(bf16[2,1024,256]{2,1,0:T(8,128)(2,1)S(1)} %pad_maximum_fusion.2.refs_1_), channel_id=1, source_target_pairs={{0,2},{1,3},{2,4},{3,5},{4,6},{5,7},{6,0},{7,1},{8,10},{9,11},{10,... | collective-permute-start | bytes 3145736 | tf_op jit(solution)/shard_map/ppermute | solution.py:39
  188.8 25.3 %collective-permute-start.32 = (bf16[2,1024,256]{2,1,0:T(8,128)(2,1)S(1)}, bf16[2,1024,256]{2,1,0:T(8,128)(2,1)S(1)}, u32[]{:S(2)}, u32[]{:S(2)}) collective-permute-start(bf16[2,1024,256]{2,1,0:T(8,128)(2,1)S(1)} %pad_maximum_fusion.2.refs_1_), channel_id=1, source_target_pairs={{0,6},{1,7},{2,0},{3,1},{4,2},{5,3},{6,4},{7,5},{8,14},{9,15},{10,... | collective-permute-start | bytes 3145736 | tf_op jit(solution)/shard_map/ppermute | solution.py:39
  195.7 18.3 %copy-start.19 = (bf16[1024,256]{1,0:T(8,128)(2,1)}, bf16[1024,256]{1,0:T(8,128)(2,1)S(1)}, u32[]{:S(2)}) copy-start(bf16[1024,256]{1,0:T(8,128)(2,1)S(1)} %collective-permute-done.34.refs_3_) | copy-start | bytes 1572868
  195.7 18.3 %copy-start.6 = (bf16[1024,256]{1,0:T(8,128)(2,1)}, bf16[1024,256]{1,0:T(8,128)(2,1)S(1)}, u32[]{:S(2)}) copy-start(bf16[1024,256]{1,0:T(8,128)(2,1)S(1)} %collective-permute-done.35.refs_4_) | copy-start | bytes 1572868
  197.2 37.4 %collective-permute-start.36 = (bf16[3,1024,256]{2,1,0:T(8,128)(2,1)}, bf16[3,1024,256]{2,1,0:T(8,128)(2,1)}, u32[]{:S(2)}, u32[]{:S(2)}) collective-permute-start(bf16[3,1024,256]{2,1,0:T(8,128)(2,1)} %pad_maximum_fusion.1), channel_id=1, source_target_pairs={{0,1},{1,0},{2,3},{3,2},{4,5},{5,4},{6,7},{7,6},{8,9},{9,8},{10,11... | collective-permute-start | bytes 4718600 | tf_op jit(solution)/shard_map/ppermute | solution.py:43
  214.0 17.9 %collective-permute-start.31 = (bf16[1024,256]{1,0:T(8,128)(2,1)}, bf16[1024,256]{1,0:T(8,128)(2,1)}, u32[]{:S(2)}, u32[]{:S(2)}) collective-permute-start(bf16[1024,256]{1,0:T(8,128)(2,1)} %slice_bitcast_fusion.3), channel_id=1, source_target_pairs={{0,2},{1,3},{2,4},{3,5},{4,6},{5,7},{6,0},{7,1},{8,10},{9,11},{10,... | collective-permute-start | bytes 1572872 | tf_op jit(solution)/shard_map/ppermute | solution.py:39
  214.1 17.7 %collective-permute-start.33 = (bf16[1024,256]{1,0:T(8,128)(2,1)S(1)}, bf16[1024,256]{1,0:T(8,128)(2,1)S(1)}, u32[]{:S(2)}, u32[]{:S(2)}) collective-permute-start(bf16[1024,256]{1,0:T(8,128)(2,1)S(1)} %slice_bitcast_fusion.2), channel_id=1, source_target_pairs={{0,6},{1,7},{2,0},{3,1},{4,2},{5,3},{6,4},{7,5},{8,14},{9,15},{10,... | collective-permute-start | bytes 1572872 | tf_op jit(solution)/shard_map/ppermute | solution.py:39
  (19 other events, 135.5 us)
Sparse Core Ops, SparseCore 0:
  96.4 43.0 all-gather.2

commit v5 on v4

--- a/solution.py
+++ b/solution.py
@@ -584,7 +584,6 @@
     mine = column_shares(after(w_out, far0))
     second = x_first_pieces(pair1, after(below1, mine), above1, *far1)
     sums = project(second[:6], low, rows, [], [], False, norm_gain, weights, offsets, C1)
-    w_columns = gather_shares(after(mine, sums[1]))
     old = project(second[6:], low, rows, sums, old, True, norm_gain, weights, offsets, C2)
     k, v, q = old[:3]
     exchanged = first_exchange(*old[3:])
@@ -593,6 +592,7 @@
     table = key_table(rows // 16, levels)
     gathered = []
     att_a = attend(q, state, exchanged, table, offsets, 0)
+    w_columns = gather_shares(after(mine, att_a))
     below_a, above_a, other_a = z_shift(att_a, 1), z_shift(att_a, -1), x_swap(att_a)
     if F5:
         q = after(q, att_a)

time: 250 us -> 248 us (level)
  transfers between devices with their start and end apart: 39 -> 39, of which waited for: 18 -> 15; matrix products, arithmetic and copies ran while one was open for 6% -> 6% of each run, Pallas kernels for 31% -> 24%
where the time goes in v5:
time: 248 us; the launch traced here: 247 us
  Pallas kernels  84.9 us (34%)
  waiting for transfers between devices  76.9 us (31%)
  starting transfers between devices  52.1 us (21%)
  between operations  13.9 us (6%)
  local copies, waits for them, and re-layouts  13.6 us (5%)
  other arithmetic  6.03 us (2%)
    pallas_call x3, Pallas kernels, project(): pl.pallas_call(functools.partial(project_kernel, where, len(operands), fi...  37.5 us
    ppermute x14, waiting for transfers between devices, z_shift(): return lax.ppermute(value, 'tp', pairs)  33.3 us
    ppermute x6, waiting for transfers between devices, x_swap(): return lax.ppermute(value, 'tp', [(t, t ^ 1) for t in range(8)])  27 us
    ppermute x14, starting transfers between devices, z_shift(): return lax.ppermute(value, 'tp', pairs)  21.2 us
    pallas_call x3, Pallas kernels, output(): pl.pallas_call(functools.partial(output_kernel, where, len(operands), sha...  20.1 us
    pallas_call x2, Pallas kernels, attend(): pl.pallas_call(functools.partial(attend_kernel, levels, head_base), grid_...  17.9 us
    ppermute x17, waiting for transfers between devices, seq_swap(): return lax.ppermute(value, 'seq', [(s, s ^ mask) for s in range(16)])  16.6 us
    ppermute x6, starting transfers between devices, x_swap(): return lax.ppermute(value, 'tp', [(t, t ^ 1) for t in range(8)])  13.3 us
  transfers between devices with their start and end apart: 39, of which 15 were waited for; matrix products, arithmetic and copies ran while one was open for 6% of the time, Pallas kernels for 24%

profile of v5, /device:TPU:0, one launch (start us, length us, event | category | flops | bytes accessed | tf_op | source)
XLA Modules:
  0.0 247.5 jit_solution(17423003403690671166)
XLA Ops:
  6.5 1.0 slice.22.refs_2_
  7.5 2.1 collective-permute-start.1
  9.6 1.2 slice_bitcast_fusion.4
  10.8 3.1 %collective-permute-start = (bf16[768,512]{1,0:T(8,128)(2,1)S(1)}, bf16[768,512]{1,0:T(8,128)(2,1)S(1)}, u32[]{:S(2)}, u32[]{:S(2)}) collective-permute-start(bf16[768,512]{1,0:T(8,128)(2,1)S(1)} %get-tuple-element.70), channel_id=1, source_target_pairs={{0,1},{1,0},{2,3},{3,2},{4,5},{5,4},{6,7},{7,6},{8,9},{9,8},{10,11... | collective-permute-start | bytes 2359304 | tf_op jit(solution)/shard_map/ppermute | solution.py:43
  14.0 2.2 collective-permute-start.2
  16.1 1.9 collective-permute-done.1.refs_3_
  18.0 3.6 %collective-permute-done.2.refs_4_ = bf16[256,512]{1,0:T(8,128)(2,1)S(1)} collective-permute-done((bf16[256,512]{1,0:T(8,128)(2,1)S(1)}, bf16[256,512]{1,0:T(8,128)(2,1)S(1)}, u32[]{:S(2)}, u32[]{:S(2)}) %collective-permute-start.2) | collective-permute-done | bytes 262176 | tf_op jit(solution)/shard_map/ppermute | solution.py:39
  21.6 5.1 %collective-permute-done.3.refs_5_ = bf16[256,512]{1,0:T(8,128)(2,1)S(1)} collective-permute-done((bf16[256,512]{1,0:T(8,128)(2,1)S(1)}, bf16[256,512]{1,0:T(8,128)(2,1)S(1)}, u32[]{:S(2)}, u32[]{:S(2)}) %collective-permute-start.3) | collective-permute-done | bytes 262176 | tf_op jit(solution)/shard_map/ppermute | solution.py:39
  26.8 3.1 %collective-permute-start.6 = (bf16[3,256,512]{2,1,0:T(8,128)(2,1)S(1)}, bf16[3,256,512]{2,1,0:T(8,128)(2,1)}, u32[]{:S(2)}, u32[]{:S(2)}) collective-permute-start(bf16[3,256,512]{2,1,0:T(8,128)(2,1)S(1)} %pad_maximum_fusion.3), channel_id=1, source_target_pairs={{0,1},{1,0},{2,3},{3,2},{4,5},{5,4},{6,7},{7,6},{8,9},{9,8},{10,11... | collective-permute-start | bytes 2359304 | tf_op jit(solution)/shard_map/ppermute | solution.py:43
  34.5 1.3 pad_maximum_fusion.refs_2_
  35.8 1.3 collective-permute-start.4
  37.1 2.0 collective-permute-start.8
  39.1 1.1 constant_dynamic-slice_fusion
  41.3 5.4 %all-to-all-start = ((bf16[8,64,512]{2,1,0:T(8,128)(2,1)}), bf16[8,64,512]{2,1,0:T(8,128)(2,1)S(1)}, u32[]{:S(2)}, u32[]{:S(2)}) async-start(bf16[8,64,512]{2,1,0:T(8,128)(2,1)} %copy.33), calls=%async_computation | async-start | bytes 1048576 | tf_op jit(solution)/shard_map/all_to_all | solution.py:554
  46.7 8.7 %collective-permute-done.5.refs_6_ = bf16[256,512]{1,0:T(8,128)(2,1)} collective-permute-done((bf16[256,512]{1,0:T(8,128)(2,1)S(1)}, bf16[256,512]{1,0:T(8,128)(2,1)}, u32[]{:S(2)}, u32[]{:S(2)}) %collective-permute-start.5) | collective-permute-done | bytes 262176 | tf_op jit(solution)/shard_map/ppermute | solution.py:43
  55.5 11.1 %project.3 = (bf16[1024,512]{1,0:T(8,128)(2,1)}, bf16[1024,512]{1,0:T(8,128)(2,1)}, bf16[1024,512]{1,0:T(8,128)(2,1)}, bf16[960,1024]{1,0:T(8,128)(2,1)}, bf16[2...) custom-call(s32[8]{0:T(128)} %stack.134.refs_0_, s32[5,4]{1,0:T(8,128)} %copy.37.refs_1_.refs_0_, ...), custom_call_target="tpu_custom_call" | custom-call | flops 12000000000 | bytes 1024 | tf_op jit(solution)/shard_map/project/pallas_call | solution.py:289
  66.6 8.9 %collective-permute-done.4.refs_3_ = bf16[2,768,512]{2,1,0:T(8,128)(2,1)} collective-permute-done((bf16[2,768,512]{2,1,0:T(8,128)(2,1)S(1)}, bf16[2,768,512]{2,1,0:T(8,128)(2,1)}, u32[]{:S(2)}, u32[]{:S(2)}) %collective-permute-start.4) | collective-permute-done | bytes 1572896 | tf_op jit(solution)/shard_map/ppermute | solution.py:39
  75.5 1.2 slice_bitcast_fusion.1
  76.8 1.2 slice_bitcast_fusion
  78.0 3.3 %collective-permute-start.9 = (bf16[768,512]{1,0:T(8,128)(2,1)S(1)}, bf16[768,512]{1,0:T(8,128)(2,1)S(1)}, u32[]{:S(2)}, u32[]{:S(2)}) collective-permute-start(bf16[768,512]{1,0:T(8,128)(2,1)S(1)} %slice_bitcast_fusion), channel_id=1, source_target_pairs={{0,6},{1,7},{2,0},{3,1},{4,2},{5,3},{6,4},{7,5},{8,14},{9,15},{10,... | collective-permute-start | bytes 2359304 | tf_op jit(solution)/shard_map/ppermute | solution.py:39
  81.3 16.2 %project.4 = (f32[3,768,512]{2,1,0:T(8,128)}, f32[768,128]{1,0:T(8,128)}) custom-call(s32[6]{0:T(128)} %stack.139.refs_0_, s32[5,4]{1,0:T(8,128)} %copy.37.refs_1_.refs_0_, bf16[2,768,512]{2,1,0:T(8,128)(2,1)} %copy-done.7, bf16[2,768,512]{2,1,0:T(8,128)(2,1)} %collective-permute-done.4.refs_3_, bf16[2,768,512]{2,1,0:T(8,128)(2,1)} %collective-permute-done.8.refs_4_, ...), custom_call_target="tpu_custom_call" | custom-call | flops 20000000000 | bytes 1024 | tf_op jit(solution)/shard_map/project/pallas_call | solution.py:289
  98.4 10.2 %project.5 = (bf16[1024,512]{1,0:T(8,128)(2,1)}, bf16[1024,512]{1,0:T(8,128)(2,1)}, bf16[1024,512]{1,0:T(8,128)(2,1)}, bf16[960,1024]{1,0:T(8,128)(2,1)}, bf16[2...) custom-call(s32[2]{0:T(128)} %pad_add_fusion.2.refs_0_, ...), custom_call_target="tpu_custom_call", output_to_operand_aliasing={{0}: (10, {}), {1}: (11, {}), {2}: (12, {}), {3}: (13, {}),... | custom-call | flops 8000000000 | bytes 1024 | tf_op jit(solution)/shard_map/project/pallas_call | solution.py:289
  108.6 1.7 collective-permute-start.11
  110.3 1.6 collective-permute-start.12
  112.5 2.9 %collective-permute-start.14 = (bf16[64,1024]{1,0:T(8,128)(2,1)}, bf16[64,1024]{1,0:T(8,128)(2,1)}, u32[]{:S(2)}, u32[]{:S(2)}) collective-permute-start(bf16[64,1024]{1,0:T(8,128)(2,1)} %get-tuple-element.62), channel_id=1, source_target_pairs={{0,64},{8,72},{16,80},{24,88},{32,96},{40,104},{48,112},{56,120},{... | collective-permute-start | bytes 393224 | tf_op jit(solution)/shard_map/ppermute | solution.py:47
  115.4 9.3 %attend_local.1 = (f32[1024,512]{1,0:T(8,128)}, f32[1024,512]{1,0:T(8,128)}, f32[1024,512]{1,0:T(8,128)}) custom-call(bf16[1024,512]{1,0:T(8,128)(2,1)} %get-tuple-element.65.q_ref.refs_1_, bf16[1024,512]{1,0:T(8,128)(2,1)} %get-tuple-element.51.k_ref, bf16[1024,512]{1,0:T(8,128)(2,1)} %get-tuple-element.52.v_ref), custom_call_target="tpu_custom_call" | custom-call | flops 8999999488 | bytes 1024 | tf_op jit(solution)/shard_map/attend_local/pallas_call | solution.py:407
  125.0 2.1 collective-permute-start.17
  127.1 1.1 collective-permute-start.18
  128.2 6.5 %collective-permute-done.16.refs_11_.refs_29_ = bf16[64,1024]{1,0:T(8,128)(2,1)} collective-permute-done((bf16[64,1024]{1,0:T(8,128)(2,1)}, bf16[64,1024]{1,0:T(8,128)(2,1)}, u32[]{:S(2)}, u32[]{:S(2)}) %collective-permute-start.16) | collective-permute-done | bytes 131104 | tf_op jit(solution)/shard_map/ppermute | solution.py:47
  134.8 2.5 collective-permute-done.18.refs_14_.refs_32_
  139.0 6.4 %collective-permute-done.15.refs_12_.refs_30_ = bf16[192,1024]{1,0:T(8,128)(2,1)} collective-permute-done((bf16[192,1024]{1,0:T(8,128)(2,1)S(1)}, bf16[192,1024]{1,0:T(8,128)(2,1)}, u32[]{:S(2)}, u32[]{:S(2)}) %collective-permute-start.15) | collective-permute-done | bytes 393248 | tf_op jit(solution)/shard_map/ppermute | solution.py:47
  148.1 1.2 copy-done.17
  149.3 8.9 %attend.2.refs_1_ = bf16[1024,256]{1,0:T(8,128)(2,1)} custom-call(s32[5,4]{1,0:T(8,128)} %copy.37.refs_1_.refs_0_, bf16[1024,512]{1,0:T(8,128)(2,1)} %get-tuple-element.65.q_ref.refs_1_, f32[1024,512]{1,0:T(8,128)} %get-tuple-element.53.refs_2_, f32[1024,512]{1,0:T(8,128)} %get-tuple-element.54.refs_3_, f32[1024,512]{1,0:T(8,128)} %get-tuple-element.55.refs_4_, ...), custom_call_target="tpu_custom_call" | custom-call | flops 8999999488 | bytes 1024 | tf_op jit(solution)/shard_map/attend/pallas_call | solution.py:472
  158.3 9.0 %attend.3 = bf16[1024,256]{1,0:T(8,128)(2,1)} custom-call(s32[5,4]{1,0:T(8,128)} %copy.37.refs_1_.refs_0_, bf16[1024,512]{1,0:T(8,128)(2,1)} %get-tuple-element.65.q_ref.refs_1_, f32[1024,512]{1,0:T(8,128)} %get-tuple-element.53.refs_2_, f32[1024,512]{1,0:T(8,128)} %get-tuple-element.54.refs_3_, f32[1024,512]{1,0:T(8,128)} %get-tuple-element.55.refs_4_, ...), custom_call_target="tpu_custom_call" | custom-call | flops 8999999488 | bytes 1024 | tf_op jit(solution)/shard_map/attend/pallas_call | solution.py:472
  167.3 3.1 %collective-permute-start.27 = (bf16[1024,256]{1,0:T(8,128)(2,1)}, bf16[1024,256]{1,0:T(8,128)(2,1)S(1)}, u32[]{:S(2)}, u32[]{:S(2)}) collective-permute-start(bf16[1024,256]{1,0:T(8,128)(2,1)} %attend.3), channel_id=1, source_target_pairs={{0,1},{1,0},{2,3},{3,2},{4,5},{5,4},{6,7},{7,6},{8,9},{9,8},{10,11... | collective-permute-start | bytes 1572872 | tf_op jit(solution)/shard_map/ppermute | solution.py:43
  170.4 3.0 %collective-permute-start.29 = (bf16[1024,256]{1,0:T(8,128)(2,1)S(1)}, bf16[1024,256]{1,0:T(8,128)(2,1)S(1)}, u32[]{:S(2)}, u32[]{:S(2)}) collective-permute-start(bf16[1024,256]{1,0:T(8,128)(2,1)S(1)} %copy-done.9), channel_id=1, source_target_pairs={{0,6},{1,7},{2,0},{3,1},{4,2},{5,3},{6,4},{7,5},{8,14},{9,15},{10,... | collective-permute-start | bytes 1572872 | tf_op jit(solution)/shard_map/ppermute | solution.py:39
  174.0 9.9 %collective-permute-done.27 = bf16[1024,256]{1,0:T(8,128)(2,1)S(1)} collective-permute-done((bf16[1024,256]{1,0:T(8,128)(2,1)}, bf16[1024,256]{1,0:T(8,128)(2,1)S(1)}, u32[]{:S(2)}, u32[]{:S(2)}) %collective-permute-start.27) | collective-permute-done | bytes 524320 | tf_op jit(solution)/shard_map/ppermute | solution.py:43
  184.6 1.3 pad_maximum_fusion.2.refs_1_
  186.4 3.3 %collective-permute-start.32 = (bf16[2,1024,256]{2,1,0:T(8,128)(2,1)S(1)}, bf16[2,1024,256]{2,1,0:T(8,128)(2,1)S(1)}, u32[]{:S(2)}, u32[]{:S(2)}) collective-permute-start(bf16[2,1024,256]{2,1,0:T(8,128)(2,1)S(1)} %pad_maximum_fusion.2.refs_1_), channel_id=1, source_target_pairs={{0,6},{1,7},{2,0},{3,1},{4,2},{5,3},{6,4},{7,5},{8,14},{9,15},{10,... | collective-permute-start | bytes 3145736 | tf_op jit(solution)/shard_map/ppermute | solution.py:39
  189.8 4.8 %collective-permute-done.34.refs_3_ = bf16[1024,256]{1,0:T(8,128)(2,1)S(1)} collective-permute-done((bf16[1024,256]{1,0:T(8,128)(2,1)S(1)}, bf16[1024,256]{1,0:T(8,128)(2,1)S(1)}, u32[]{:S(2)}, u32[]{:S(2)}) %collective-permute-start.34) | collective-permute-done | bytes 524320 | tf_op jit(solution)/shard_map/ppermute | solution.py:43
  194.6 1.5 pad_maximum_fusion.1
  196.0 3.0 %collective-permute-start.36 = (bf16[3,1024,256]{2,1,0:T(8,128)(2,1)}, bf16[3,1024,256]{2,1,0:T(8,128)(2,1)}, u32[]{:S(2)}, u32[]{:S(2)}) collective-permute-start(bf16[3,1024,256]{2,1,0:T(8,128)(2,1)} %pad_maximum_fusion.1), channel_id=1, source_target_pairs={{0,1},{1,0},{2,3},{3,2},{4,5},{5,4},{6,7},{7,6},{8,9},{9,8},{10,11... | collective-permute-start | bytes 4718600 | tf_op jit(solution)/shard_map/ppermute | solution.py:43
  199.0 13.1 %collective-permute-done.30.refs_2_ = bf16[2,1024,256]{2,1,0:T(8,128)(2,1)S(1)} collective-permute-done((bf16[2,1024,256]{2,1,0:T(8,128)(2,1)S(1)}, bf16[2,1024,256]{2,1,0:T(8,128)(2,1)S(1)}, u32[]{:S(2)}, u32[]{:S(2)}) %collective-permute-start.30) | collective-permute-done | bytes 1048608 | tf_op jit(solution)/shard_map/ppermute | solution.py:39
  212.3 3.3 %collective-permute-start.33 = (bf16[1024,256]{1,0:T(8,128)(2,1)S(1)}, bf16[1024,256]{1,0:T(8,128)(2,1)}, u32[]{:S(2)}, u32[]{:S(2)}) collective-permute-start(bf16[1024,256]{1,0:T(8,128)(2,1)S(1)} %slice_bitcast_fusion.2), channel_id=1, source_target_pairs={{0,6},{1,7},{2,0},{3,1},{4,2},{5,3},{6,4},{7,5},{8,14},{9,15},{10,... | collective-permute-start | bytes 1572872 | tf_op jit(solution)/shard_map/ppermute | solution.py:39
  216.8 5.9 %output.3.refs_4_ = f32[1024,512]{1,0:T(8,128)} custom-call(s32[4]{0:T(128)} %pad_add_fusion.3.refs_0_, bf16[1024,256]{1,0:T(8,128)(2,1)} %attend.2.refs_1_, bf16[1024,256]{1,0:T(8,128)(2,1)} %copy-done.4, bf16[1024,256]{1,0:T(8,128)(2,1)} %copy-done.5, bf16[1024,256]{1,0:T(8,128)(2,1)} %copy-done.6, bf16[1024,512]{1,0:T(8,128)(2,1)} %refs_5_.3, ...), custom_call_target="tpu_custom_call" | custom-call | flops 10000000 | bytes 1024 | tf_op jit(solution)/shard_map/output/pallas_call | solution.py:528
  222.8 7.3 %output.4.refs_5_ = f32[1024,512]{1,0:T(8,128)} custom-call(s32[6]{0:T(128)} %stack.139.refs_0_, bf16[2,1024,256]{2,1,0:T(8,128)(2,1)} %copy-done, bf16[2,1024,256]{2,1,0:T(8,128)(2,1)} %copy-done.1, bf16[2,1024,256]{2,1,0:T(8,128)(2,1)} %copy-done.2, f32[1024,512]{1,0:T(8,128)} %output.3.refs_4_, bf16[8,8,64,512]{3,2,1,0:T(8,128)(2,1)} %bitcast.37), custom_call_target="tpu_custom_call" | custom-call | flops 10000000 | bytes 1024 | tf_op jit(solution)/shard_map/output/pallas_call | solution.py:528
  230.1 3.6 %collective-permute-done.36.refs_4_ = bf16[3,1024,256]{2,1,0:T(8,128)(2,1)} collective-permute-done((bf16[3,1024,256]{2,1,0:T(8,128)(2,1)}, bf16[3,1024,256]{2,1,0:T(8,128)(2,1)}, u32[]{:S(2)}, u32[]{:S(2)}) %collective-permute-start.36) | collective-permute-done | bytes 1572896 | tf_op jit(solution)/shard_map/ppermute | solution.py:43
  233.7 6.9 %output.5 = bf16[1024,512]{1,0:T(8,128)(2,1)} custom-call(s32[6]{0:T(128)} %stack.126.refs_0_, bf16[1024,256]{1,0:T(8,128)(2,1)} %collective-permute-done.31.refs_1_, bf16[1024,256]{1,0:T(8,128)(2,1)} %collective-permute-done.33.refs_2_, bf16[1024,256]{1,0:T(8,128)(2,1)} %copy-done.20, bf16[3,1024,256]{2,1,0:T(8,128)(2,1)} %collective-permute-done.36.refs_4_, ...), custom_call_target="tpu_custom_call" | custom-call | flops 30000001024 | bytes 1024 | tf_op jit(solution)/shard_map/output/pallas_call | solution.py:528
  (133 shorter events, 15.3 us)
Async XLA Ops:
  7.5 22.4 %copy-start.10 = (bf16[256,512]{1,0:T(8,128)(2,1)}, bf16[256,512]{1,0:T(8,128)(2,1)S(1)}, u32[]{:S(2)}) copy-start(bf16[256,512]{1,0:T(8,128)(2,1)S(1)} %slice.22.refs_2_) | copy-start | bytes 786436
  7.5 22.9 %copy-start.16 = (s32[5,4]{0,1:T(4,128)S(1)}, s32[5,4]{0,1:T(4,128)}, u32[]{:S(2)}) copy-start(s32[5,4]{0,1:T(4,128)} %param.13) | copy-start | bytes 244
  7.5 23.6 %copy-start.15 = (f32[4096]{0:T(1024)S(1)}, f32[4096]{0:T(1024)}, u32[]{:S(2)}) copy-start(f32[4096]{0:T(1024)} %param.8) | copy-start | bytes 49156
  7.5 10.5 %collective-permute-start.1 = (bf16[256,512]{1,0:T(8,128)(2,1)S(1)}, bf16[256,512]{1,0:T(8,128)(2,1)S(1)}, u32[]{:S(2)}, u32[]{:S(2)}) collective-permute-start(bf16[256,512]{1,0:T(8,128)(2,1)S(1)} %slice.22.refs_2_), channel_id=1, source_target_pairs={{0,2},{1,3},{2,4},{3,5},{4,6},{5,7},{6,0},{7,1},{8,10},{9,11},{10,... | collective-permute-start | bytes 786440 | tf_op jit(solution)/shard_map/ppermute | solution.py:39
  10.8 22.8 %collective-permute-start = (bf16[768,512]{1,0:T(8,128)(2,1)S(1)}, bf16[768,512]{1,0:T(8,128)(2,1)S(1)}, u32[]{:S(2)}, u32[]{:S(2)}) collective-permute-start(bf16[768,512]{1,0:T(8,128)(2,1)S(1)} %get-tuple-element.70), channel_id=1, source_target_pairs={{0,1},{1,0},{2,3},{3,2},{4,5},{5,4},{6,7},{7,6},{8,9},{9,8},{10,11... | collective-permute-start | bytes 2359304 | tf_op jit(solution)/shard_map/ppermute | solution.py:43
  14.0 7.7 %collective-permute-start.2 = (bf16[256,512]{1,0:T(8,128)(2,1)S(1)}, bf16[256,512]{1,0:T(8,128)(2,1)S(1)}, u32[]{:S(2)}, u32[]{:S(2)}) collective-permute-start(bf16[256,512]{1,0:T(8,128)(2,1)S(1)} %slice.22.refs_2_), channel_id=1, source_target_pairs={{0,6},{1,7},{2,0},{3,1},{4,2},{5,3},{6,4},{7,5},{8,14},{9,15},{10,... | collective-permute-start | bytes 786440 | tf_op jit(solution)/shard_map/ppermute | solution.py:39
  18.0 8.7 %collective-permute-start.3 = (bf16[256,512]{1,0:T(8,128)(2,1)S(1)}, bf16[256,512]{1,0:T(8,128)(2,1)S(1)}, u32[]{:S(2)}, u32[]{:S(2)}) collective-permute-start(bf16[256,512]{1,0:T(8,128)(2,1)S(1)} %collective-permute-done.1.refs_3_), channel_id=1, source_target_pairs={{0,2},{1,3},{2,4},{3,5},{4,6},{5,7},{6,0},{7,1},{8,10},{9,11},{10,... | collective-permute-start | bytes 786440 | tf_op jit(solution)/shard_map/ppermute | solution.py:39
  26.8 28.6 %collective-permute-start.6 = (bf16[3,256,512]{2,1,0:T(8,128)(2,1)S(1)}, bf16[3,256,512]{2,1,0:T(8,128)(2,1)}, u32[]{:S(2)}, u32[]{:S(2)}) collective-permute-start(bf16[3,256,512]{2,1,0:T(8,128)(2,1)S(1)} %pad_maximum_fusion.3), channel_id=1, source_target_pairs={{0,1},{1,0},{2,3},{3,2},{4,5},{5,4},{6,7},{7,6},{8,9},{9,8},{10,11... | collective-permute-start | bytes 2359304 | tf_op jit(solution)/shard_map/ppermute | solution.py:43
  29.9 25.5 %collective-permute-start.5 = (bf16[256,512]{1,0:T(8,128)(2,1)S(1)}, bf16[256,512]{1,0:T(8,128)(2,1)}, u32[]{:S(2)}, u32[]{:S(2)}) collective-permute-start(bf16[256,512]{1,0:T(8,128)(2,1)S(1)} %slice.22.refs_2_), channel_id=1, source_target_pairs={{0,1},{1,0},{2,3},{3,2},{4,5},{5,4},{6,7},{7,6},{8,9},{9,8},{10,11... | collective-permute-start | bytes 786440 | tf_op jit(solution)/shard_map/ppermute | solution.py:43
  35.8 39.7 %collective-permute-start.4 = (bf16[2,768,512]{2,1,0:T(8,128)(2,1)S(1)}, bf16[2,768,512]{2,1,0:T(8,128)(2,1)}, u32[]{:S(2)}, u32[]{:S(2)}) collective-permute-start(bf16[2,768,512]{2,1,0:T(8,128)(2,1)S(1)} %pad_maximum_fusion.refs_2_), channel_id=1, source_target_pairs={{0,2},{1,3},{2,4},{3,5},{4,6},{5,7},{6,0},{7,1},{8,10},{9,11},{10,... | collective-permute-start | bytes 4718600 | tf_op jit(solution)/shard_map/ppermute | solution.py:39
  37.1 39.7 %collective-permute-start.8 = (bf16[2,768,512]{2,1,0:T(8,128)(2,1)S(1)}, bf16[2,768,512]{2,1,0:T(8,128)(2,1)}, u32[]{:S(2)}, u32[]{:S(2)}) collective-permute-start(bf16[2,768,512]{2,1,0:T(8,128)(2,1)S(1)} %pad_maximum_fusion.refs_2_), channel_id=1, source_target_pairs={{0,6},{1,7},{2,0},{3,1},{4,2},{5,3},{6,4},{7,5},{8,14},{9,15},{10,... | collective-permute-start | bytes 4718600 | tf_op jit(solution)/shard_map/ppermute | solution.py:39
  41.3 40.0 %all-to-all-start = ((bf16[8,64,512]{2,1,0:T(8,128)(2,1)}), bf16[8,64,512]{2,1,0:T(8,128)(2,1)S(1)}, u32[]{:S(2)}, u32[]{:S(2)}) async-start(bf16[8,64,512]{2,1,0:T(8,128)(2,1)} %copy.33), calls=%async_computation | async-start | bytes 1048576 | tf_op jit(solution)/shard_map/all_to_all | solution.py:554
  46.7 170.1 %all-gather.3.cloned.1.call-start = ((), (), s32[]{:S(2)}) async-start(), calls=%async_computation.1 | async-start | bytes 4718592 | tf_op jit(solution)/shard_map/all_gather | solution.py:559
  76.7 20.8 %collective-permute-start.7 = (bf16[768,512]{1,0:T(8,128)(2,1)S(1)}, bf16[768,512]{1,0:T(8,128)(2,1)}, u32[]{:S(2)}, u32[]{:S(2)}) collective-permute-start(bf16[768,512]{1,0:T(8,128)(2,1)S(1)} %slice_bitcast_fusion.1), channel_id=1, source_target_pairs={{0,2},{1,3},{2,4},{3,5},{4,6},{5,7},{6,0},{7,1},{8,10},{9,11},{10,... | collective-permute-start | bytes 2359304 | tf_op jit(solution)/shard_map/ppermute | solution.py:39
  78.0 19.5 %collective-permute-start.9 = (bf16[768,512]{1,0:T(8,128)(2,1)S(1)}, bf16[768,512]{1,0:T(8,128)(2,1)S(1)}, u32[]{:S(2)}, u32[]{:S(2)}) collective-permute-start(bf16[768,512]{1,0:T(8,128)(2,1)S(1)} %slice_bitcast_fusion), channel_id=1, source_target_pairs={{0,6},{1,7},{2,0},{3,1},{4,2},{5,3},{6,4},{7,5},{8,14},{9,15},{10,... | collective-permute-start | bytes 2359304 | tf_op jit(solution)/shard_map/ppermute | solution.py:39
  108.6 16.1 %collective-permute-start.11 = (bf16[192,1024]{1,0:T(8,128)(2,1)}, bf16[192,1024]{1,0:T(8,128)(2,1)S(1)}, u32[]{:S(2)}, u32[]{:S(2)}) collective-permute-start(bf16[192,1024]{1,0:T(8,128)(2,1)} %get-tuple-element.57), channel_id=1, source_target_pairs={{0,16},{8,24},{16,0},{24,8},{32,48},{40,56},{48,32},{56,40},{64,80... | collective-permute-start | bytes 1179656 | tf_op jit(solution)/shard_map/ppermute | solution.py:47
  110.3 14.7 %collective-permute-start.12 = (bf16[192,1024]{1,0:T(8,128)(2,1)}, bf16[192,1024]{1,0:T(8,128)(2,1)S(1)}, u32[]{:S(2)}, u32[]{:S(2)}) collective-permute-start(bf16[192,1024]{1,0:T(8,128)(2,1)} %get-tuple-element.57), channel_id=1, source_target_pairs={{0,32},{8,40},{16,48},{24,56},{32,0},{40,8},{48,16},{56,24},{64,96... | collective-permute-start | bytes 1179656 | tf_op jit(solution)/shard_map/ppermute | solution.py:47
  111.9 36.1 %collective-permute-start.10 = (bf16[960,1024]{1,0:T(8,128)(2,1)}, bf16[960,1024]{1,0:T(8,128)(2,1)S(1)}, u32[]{:S(2)}, u32[]{:S(2)}) collective-permute-start(bf16[960,1024]{1,0:T(8,128)(2,1)} %get-tuple-element.56.refs_5_.refs_23_), channel_id=1, source_target_pairs={{0,8},{8,0},{16,24},{24,16},{32,40},{40,32},{48,56},{56,48},{64,72... | collective-permute-start | bytes 5898248 | tf_op jit(solution)/shard_map/ppermute | solution.py:47
  111.9 25.4 %collective-permute-start.13 = (bf16[256,1024]{1,0:T(8,128)(2,1)}, bf16[256,1024]{1,0:T(8,128)(2,1)S(1)}, u32[]{:S(2)}, u32[]{:S(2)}) collective-permute-start(bf16[256,1024]{1,0:T(8,128)(2,1)} %get-tuple-element.60), channel_id=1, source_target_pairs={{0,16},{8,24},{16,0},{24,8},{32,48},{40,56},{48,32},{56,40},{64,80... | collective-permute-start | bytes 1572872 | tf_op jit(solution)/shard_map/ppermute | solution.py:47
  112.5 14.6 %collective-permute-start.14 = (bf16[64,1024]{1,0:T(8,128)(2,1)}, bf16[64,1024]{1,0:T(8,128)(2,1)}, u32[]{:S(2)}, u32[]{:S(2)}) collective-permute-start(bf16[64,1024]{1,0:T(8,128)(2,1)} %get-tuple-element.62), channel_id=1, source_target_pairs={{0,64},{8,72},{16,80},{24,88},{32,96},{40,104},{48,112},{56,120},{... | collective-permute-start | bytes 393224 | tf_op jit(solution)/shard_map/ppermute | solution.py:47
  124.7 23.4 %copy-start.14 = (bf16[192,1024]{1,0:T(8,128)(2,1)}, bf16[192,1024]{1,0:T(8,128)(2,1)S(1)}, u32[]{:S(2)}) copy-start(bf16[192,1024]{1,0:T(8,128)(2,1)S(1)} %collective-permute-done.11.refs_7_.refs_25_) | copy-start | bytes 1179652
  124.7 10.1 %collective-permute-start.16 = (bf16[64,1024]{1,0:T(8,128)(2,1)}, bf16[64,1024]{1,0:T(8,128)(2,1)}, u32[]{:S(2)}, u32[]{:S(2)}) collective-permute-start(bf16[64,1024]{1,0:T(8,128)(2,1)} %get-tuple-element.62), channel_id=1, source_target_pairs={{0,96},{8,104},{16,112},{24,120},{32,64},{40,72},{48,80},{56,88},{... | collective-permute-start | bytes 393224 | tf_op jit(solution)/shard_map/ppermute | solution.py:47
  125.0 23.1 %copy-start.21 = (bf16[192,1024]{1,0:T(8,128)(2,1)}, bf16[192,1024]{1,0:T(8,128)(2,1)S(1)}, u32[]{:S(2)}) copy-start(bf16[192,1024]{1,0:T(8,128)(2,1)S(1)} %collective-permute-done.12.refs_8_.refs_26_) | copy-start | bytes 1179652
  125.0 9.8 %collective-permute-start.17 = (bf16[64,1024]{1,0:T(8,128)(2,1)S(1)}, bf16[64,1024]{1,0:T(8,128)(2,1)}, u32[]{:S(2)}, u32[]{:S(2)}) collective-permute-start(bf16[64,1024]{1,0:T(8,128)(2,1)S(1)} %slice.25), channel_id=1, source_target_pairs={{0,64},{8,72},{16,80},{24,88},{32,96},{40,104},{48,112},{56,120},{... | collective-permute-start | bytes 393224 | tf_op jit(solution)/shard_map/ppermute | solution.py:47
  127.1 10.2 %collective-permute-start.18 = (bf16[64,1024]{1,0:T(8,128)(2,1)S(1)}, bf16[64,1024]{1,0:T(8,128)(2,1)}, u32[]{:S(2)}, u32[]{:S(2)}) collective-permute-start(bf16[64,1024]{1,0:T(8,128)(2,1)S(1)} %slice.25), channel_id=1, source_target_pairs={{0,96},{8,104},{16,112},{24,120},{32,64},{40,72},{48,80},{56,88},{... | collective-permute-start | bytes 393224 | tf_op jit(solution)/shard_map/ppermute | solution.py:47
  134.8 10.6 %collective-permute-start.15 = (bf16[192,1024]{1,0:T(8,128)(2,1)S(1)}, bf16[192,1024]{1,0:T(8,128)(2,1)}, u32[]{:S(2)}, u32[]{:S(2)}) collective-permute-start(bf16[192,1024]{1,0:T(8,128)(2,1)S(1)} %collective-permute-done.11.refs_7_.refs_25_), channel_id=1, source_target_pairs={{0,32},{8,40},{16,48},{24,56},{32,0},{40,8},{48,16},{56,24},{64,96... | collective-permute-start | bytes 1179656 | tf_op jit(solution)/shard_map/ppermute | solution.py:47
  134.8 3.1 %collective-permute-start.25 = (bf16[64,1024]{1,0:T(8,128)(2,1)}, bf16[64,1024]{1,0:T(8,128)(2,1)}, u32[]{:S(2)}, u32[]{:S(2)}) collective-permute-start(bf16[64,1024]{1,0:T(8,128)(2,1)} %collective-permute-done.17.refs_13_.refs_31_), channel_id=1, source_target_pairs={{0,8},{8,0},{16,24},{24,16},{32,40},{40,32},{48,56},{56,48},{64,72... | collective-permute-start | bytes 393224 | tf_op jit(solution)/shard_map/ppermute | solution.py:47
  137.2 1.6 collective-permute-start.26
  137.3 8.1 %collective-permute-start.19 = (bf16[192,1024]{1,0:T(8,128)(2,1)S(1)}, bf16[192,1024]{1,0:T(8,128)(2,1)S(1)}, u32[]{:S(2)}, u32[]{:S(2)}) collective-permute-start(bf16[192,1024]{1,0:T(8,128)(2,1)S(1)} %collective-permute-done.11.refs_7_.refs_25_), channel_id=1, source_target_pairs={{0,8},{8,0},{16,24},{24,16},{32,40},{40,32},{48,56},{56,48},{64,72... | collective-permute-start | bytes 1179656 | tf_op jit(solution)/shard_map/ppermute | solution.py:47
  137.9 8.2 %collective-permute-start.20 = (bf16[192,1024]{1,0:T(8,128)(2,1)S(1)}, bf16[192,1024]{1,0:T(8,128)(2,1)S(1)}, u32[]{:S(2)}, u32[]{:S(2)}) collective-permute-start(bf16[192,1024]{1,0:T(8,128)(2,1)S(1)} %collective-permute-done.12.refs_8_.refs_26_), channel_id=1, source_target_pairs={{0,8},{8,0},{16,24},{24,16},{32,40},{40,32},{48,56},{56,48},{64,72... | collective-permute-start | bytes 1179656 | tf_op jit(solution)/shard_map/ppermute | solution.py:47
  138.8 9.2 %collective-permute-start.21 = (bf16[256,1024]{1,0:T(8,128)(2,1)S(1)}, bf16[256,1024]{1,0:T(8,128)(2,1)}, u32[]{:S(2)}, u32[]{:S(2)}) collective-permute-start(bf16[256,1024]{1,0:T(8,128)(2,1)S(1)} %collective-permute-done.13.refs_9_.refs_27_), channel_id=1, source_target_pairs={{0,8},{8,0},{16,24},{24,16},{32,40},{40,32},{48,56},{56,48},{64,72... | collective-permute-start | bytes 1572872 | tf_op jit(solution)/shard_map/ppermute | solution.py:47
  145.4 2.6 %collective-permute-start.24 = (bf16[192,1024]{1,0:T(8,128)(2,1)}, bf16[192,1024]{1,0:T(8,128)(2,1)}, u32[]{:S(2)}, u32[]{:S(2)}) collective-permute-start(bf16[192,1024]{1,0:T(8,128)(2,1)} %collective-permute-done.15.refs_12_.refs_30_), channel_id=1, source_target_pairs={{0,8},{8,0},{16,24},{24,16},{32,40},{40,32},{48,56},{56,48},{64,72... | collective-permute-start | bytes 1179656 | tf_op jit(solution)/shard_map/ppermute | solution.py:47
  145.4 2.2 collective-permute-start.22
  146.2 1.8 collective-permute-start.23
  158.2 15.8 %collective-permute-start.28 = (bf16[1024,256]{1,0:T(8,128)(2,1)}, bf16[1024,256]{1,0:T(8,128)(2,1)S(1)}, u32[]{:S(2)}, u32[]{:S(2)}) collective-permute-start(bf16[1024,256]{1,0:T(8,128)(2,1)} %attend.2.refs_1_), channel_id=1, source_target_pairs={{0,2},{1,3},{2,4},{3,5},{4,6},{5,7},{6,0},{7,1},{8,10},{9,11},{10,... | collective-permute-start | bytes 1572872 | tf_op jit(solution)/shard_map/ppermute | solution.py:39
  167.3 16.6 %collective-permute-start.27 = (bf16[1024,256]{1,0:T(8,128)(2,1)}, bf16[1024,256]{1,0:T(8,128)(2,1)S(1)}, u32[]{:S(2)}, u32[]{:S(2)}) collective-permute-start(bf16[1024,256]{1,0:T(8,128)(2,1)} %attend.3), channel_id=1, source_target_pairs={{0,1},{1,0},{2,3},{3,2},{4,5},{5,4},{6,7},{7,6},{8,9},{9,8},{10,11... | collective-permute-start | bytes 1572872 | tf_op jit(solution)/shard_map/ppermute | solution.py:43
  170.4 14.2 %collective-permute-start.29 = (bf16[1024,256]{1,0:T(8,128)(2,1)S(1)}, bf16[1024,256]{1,0:T(8,128)(2,1)S(1)}, u32[]{:S(2)}, u32[]{:S(2)}) collective-permute-start(bf16[1024,256]{1,0:T(8,128)(2,1)S(1)} %copy-done.9), channel_id=1, source_target_pairs={{0,6},{1,7},{2,0},{3,1},{4,2},{5,3},{6,4},{7,5},{8,14},{9,15},{10,... | collective-permute-start | bytes 1572872 | tf_op jit(solution)/shard_map/ppermute | solution.py:39
  173.4 21.1 %collective-permute-start.34 = (bf16[1024,256]{1,0:T(8,128)(2,1)S(1)}, bf16[1024,256]{1,0:T(8,128)(2,1)S(1)}, u32[]{:S(2)}, u32[]{:S(2)}) collective-permute-start(bf16[1024,256]{1,0:T(8,128)(2,1)S(1)} %copy-done.9), channel_id=1, source_target_pairs={{0,1},{1,0},{2,3},{3,2},{4,5},{5,4},{6,7},{7,6},{8,9},{9,8},{10,11... | collective-permute-start | bytes 1572872 | tf_op jit(solution)/shard_map/ppermute | solution.py:43
  174.0 22.0 %copy-start.4 = (bf16[1024,256]{1,0:T(8,128)(2,1)}, bf16[1024,256]{1,0:T(8,128)(2,1)S(1)}, u32[]{:S(2)}) copy-start(bf16[1024,256]{1,0:T(8,128)(2,1)S(1)} %collective-permute-done.28.refs_2_) | copy-start | bytes 1572868
  174.0 20.6 %collective-permute-start.35 = (bf16[1024,256]{1,0:T(8,128)(2,1)S(1)}, bf16[1024,256]{1,0:T(8,128)(2,1)S(1)}, u32[]{:S(2)}, u32[]{:S(2)}) collective-permute-start(bf16[1024,256]{1,0:T(8,128)(2,1)S(1)} %collective-permute-done.28.refs_2_), channel_id=1, source_target_pairs={{0,2},{1,3},{2,4},{3,5},{4,6},{5,7},{6,0},{7,1},{8,10},{9,11},{10,... | collective-permute-start | bytes 1572872 | tf_op jit(solution)/shard_map/ppermute | solution.py:39
  185.9 26.2 %copy-start = (bf16[2,1024,256]{2,1,0:T(8,128)(2,1)}, bf16[2,1024,256]{2,1,0:T(8,128)(2,1)S(1)}, u32[]{:S(2)}) copy-start(bf16[2,1024,256]{2,1,0:T(8,128)(2,1)S(1)} %pad_maximum_fusion.2.refs_1_) | copy-start | bytes 3145732
  185.9 26.1 %collective-permute-start.30 = (bf16[2,1024,256]{2,1,0:T(8,128)(2,1)S(1)}, bf16[2,1024,256]{2,1,0:T(8,128)(2,1)S(1)}, u32[]{:S(2)}, u32[]{:S(2)}) collective-permute-start(bf16[2,1024,256]{2,1,0:T(8,128)(2,1)S(1)} %pad_maximum_fusion.2.refs_1_), channel_id=1, source_target_pairs={{0,2},{1,3},{2,4},{3,5},{4,6},{5,7},{6,0},{7,1},{8,10},{9,11},{10,... | collective-permute-start | bytes 3145736 | tf_op jit(solution)/shard_map/ppermute | solution.py:39
  186.4 25.8 %collective-permute-start.32 = (bf16[2,1024,256]{2,1,0:T(8,128)(2,1)S(1)}, bf16[2,1024,256]{2,1,0:T(8,128)(2,1)S(1)}, u32[]{:S(2)}, u32[]{:S(2)}) collective-permute-start(bf16[2,1024,256]{2,1,0:T(8,128)(2,1)S(1)} %pad_maximum_fusion.2.refs_1_), channel_id=1, source_target_pairs={{0,6},{1,7},{2,0},{3,1},{4,2},{5,3},{6,4},{7,5},{8,14},{9,15},{10,... | collective-permute-start | bytes 3145736 | tf_op jit(solution)/shard_map/ppermute | solution.py:39
  194.5 17.6 %copy-start.20 = (bf16[1024,256]{1,0:T(8,128)(2,1)}, bf16[1024,256]{1,0:T(8,128)(2,1)S(1)}, u32[]{:S(2)}) copy-start(bf16[1024,256]{1,0:T(8,128)(2,1)S(1)} %collective-permute-done.34.refs_3_) | copy-start | bytes 1572868
  194.5 17.6 %copy-start.6 = (bf16[1024,256]{1,0:T(8,128)(2,1)}, bf16[1024,256]{1,0:T(8,128)(2,1)S(1)}, u32[]{:S(2)}) copy-start(bf16[1024,256]{1,0:T(8,128)(2,1)S(1)} %collective-permute-done.35.refs_4_) | copy-start | bytes 1572868
  196.0 37.7 %collective-permute-start.36 = (bf16[3,1024,256]{2,1,0:T(8,128)(2,1)}, bf16[3,1024,256]{2,1,0:T(8,128)(2,1)}, u32[]{:S(2)}, u32[]{:S(2)}) collective-permute-start(bf16[3,1024,256]{2,1,0:T(8,128)(2,1)} %pad_maximum_fusion.1), channel_id=1, source_target_pairs={{0,1},{1,0},{2,3},{3,2},{4,5},{5,4},{6,7},{7,6},{8,9},{9,8},{10,11... | collective-permute-start | bytes 4718600 | tf_op jit(solution)/shard_map/ppermute | solution.py:43
  212.1 18.0 %collective-permute-start.31 = (bf16[1024,256]{1,0:T(8,128)(2,1)S(1)}, bf16[1024,256]{1,0:T(8,128)(2,1)}, u32[]{:S(2)}, u32[]{:S(2)}) collective-permute-start(bf16[1024,256]{1,0:T(8,128)(2,1)S(1)} %slice_bitcast_fusion.3), channel_id=1, source_target_pairs={{0,2},{1,3},{2,4},{3,5},{4,6},{5,7},{6,0},{7,1},{8,10},{9,11},{10,... | collective-permute-start | bytes 1572872 | tf_op jit(solution)/shard_map/ppermute | solution.py:39
  212.3 17.8 %collective-permute-start.33 = (bf16[1024,256]{1,0:T(8,128)(2,1)S(1)}, bf16[1024,256]{1,0:T(8,128)(2,1)}, u32[]{:S(2)}, u32[]{:S(2)}) collective-permute-start(bf16[1024,256]{1,0:T(8,128)(2,1)S(1)} %slice_bitcast_fusion.2), channel_id=1, source_target_pairs={{0,6},{1,7},{2,0},{3,1},{4,2},{5,3},{6,4},{7,5},{8,14},{9,15},{10,... | collective-permute-start | bytes 1572872 | tf_op jit(solution)/shard_map/ppermute | solution.py:39
  (16 other events, 113.4 us)
Sparse Core Ops, SparseCore 0:
  158.3 29.0 all-gather.2
